TPU v7x, 32 devices: a whole 2x2x4 slice. The times are simulated.
32 devices in a mesh: dp: 4 (over y, x), ctx: 4 (over z), tensor: 2 (over core).
Axes of the slice: x: 2, y: 2, z: 4, core: 2. Of those that a mesh axis runs over, the one named last changes fastest.
Arguments:
- tokens: bfloat16 [8, 512, 1536], P('dp', ('ctx', 'tensor')), may hold values from -6 to 6
- prefix: int32 [8], P('dp'), may hold values from 51 to 256
- w_query: float32 [1536, 1536], P(('dp', 'ctx'), 'tensor'), may hold values from -0.15625 to 0.15625
- w_key: float32 [1536, 256], P(('dp', 'ctx'), 'tensor'), may hold values from -0.15625 to 0.15625
- w_value: float32 [1536, 256], P(('dp', 'ctx'), 'tensor'), may hold values from -0.15625 to 0.15625
- w_out: float32 [1536, 1536], P(('dp', 'ctx'), 'tensor'), may hold values from -0.5 to 0.5
- w_gate: float32 [1536, 8960], P(('dp', 'ctx'), 'tensor'), may hold values from -0.15625 to 0.15625
- w_up: float32 [1536, 8960], P(('dp', 'ctx'), 'tensor'), may hold values from -0.15625 to 0.15625
- w_down: float32 [1536, 8960], P(('dp', 'ctx'), 'tensor'), may hold values from -0.0625 to 0.0625
- b_query: float32 [1536], replicated, may hold values from -0.6 to 0.6
- b_key: float32 [256], replicated, may hold values from -1.5 to 1.5
- b_value: float32 [256], replicated, may hold values from -0.6 to 0.6
- norm_attn: float32 [1536], replicated, may hold values from 0.5 to 1.5
- norm_mlp: float32 [1536], replicated, may hold values from 0.5 to 1.5
- cotangent: bfloat16 [8, 512, 1536], P('dp', ('ctx', 'tensor')), may hold values from -6 to 6
Outputs:
- output: bfloat16 [8, 512, 1536], P('dp', ('ctx', 'tensor'))
- grad_tokens: bfloat16 [8, 512, 1536], P('dp', ('ctx', 'tensor'))
- grad_w_query: float32 [1536, 1536], P(('dp', 'ctx'), 'tensor')
- grad_w_key: float32 [1536, 256], P(('dp', 'ctx'), 'tensor')
- grad_w_value: float32 [1536, 256], P(('dp', 'ctx'), 'tensor')
- grad_w_out: float32 [1536, 1536], P(('dp', 'ctx'), 'tensor')
- grad_w_gate: float32 [1536, 8960], P(('dp', 'ctx'), 'tensor')
- grad_w_up: float32 [1536, 8960], P(('dp', 'ctx'), 'tensor')
- grad_w_down: float32 [1536, 8960], P(('dp', 'ctx'), 'tensor')
- grad_b_query: float32 [1536], replicated
- grad_b_key: float32 [256], replicated
- grad_b_value: float32 [256], replicated
- grad_norm_attn: float32 [1536], replicated
- grad_norm_mlp: float32 [1536], replicated
All inputs are finite; a program needn't handle non-finite values.
Results may differ from a plain program's by a relative error of at most 0.029.
Values may be sent and summed in bfloat16 or wider, within the bound.
No kernel may reach another device: no remote copies, remote signals or barrier semaphores. Data moves between devices by JAX's collectives and lax.ppermute only.
A program may use at most 512 MiB of HBM per device.

v0:
```python
import jax
import jax.numpy as jnp
from jax import lax
from jax.sharding import PartitionSpec as P

HD = 128


epsilon = 1e-06
rope_base = 1000000.0


def inverse_root(value):
    return lax.rsqrt(jnp.mean(value * value, axis=-1, keepdims=True) + epsilon)


def rotary_tables(positions):
    half_dim = HD // 2
    frequency = rope_base ** (-2.0 * jnp.arange(half_dim, dtype=jnp.float32) / HD)
    angles = positions.astype(jnp.float32)[:, None] * frequency[None, :]
    angles = jnp.concatenate([angles, angles], axis=1)
    return (jnp.cos(angles)[:, None, :], jnp.sin(angles)[:, None, :])


def rotate(value, cosine_table, sine_table):
    half_dim = value.shape[-1] // 2
    turned = jnp.concatenate([-value[..., half_dim:], value[..., :half_dim]], axis=-1)
    return value * cosine_table + turned * sine_table


def rotate_back(grad_rows, cosine_table, sine_table):
    half_dim = grad_rows.shape[-1] // 2
    scaled = grad_rows * sine_table
    turned = jnp.concatenate([scaled[..., half_dim:], -scaled[..., :half_dim]], axis=-1)
    return grad_rows * cosine_table + turned


def scores_of(queries, key_rows, allowed, score_scale):
    raw_scores = (
        jnp.einsum("cahd,lad->ahcl", queries, key_rows, preferred_element_type=jnp.float32)
        * score_scale
    )
    return jnp.where(allowed[None, None], raw_scores, -1e30)


def attend(queries, key_rows, values, allowed, score_scale):
    scores = scores_of(queries, key_rows, allowed, score_scale)
    peak = jnp.max(scores, axis=-1, keepdims=True)
    weights = jnp.exp(scores - peak)
    denominator = jnp.sum(weights, axis=-1, keepdims=True)
    probabilities = (weights / denominator).astype(jnp.bfloat16)
    mixed_heads = jnp.einsum(
        "ahcl,lad->cahd", probabilities, values, preferred_element_type=jnp.float32
    )
    return (mixed_heads, peak + jnp.log(denominator))


def attend_back(
    queries, key_rows, values, allowed, score_scale, log_total, mixed_heads, grad_mixed
):
    scores = scores_of(queries, key_rows, allowed, score_scale)
    probabilities = jnp.exp(scores - log_total)
    grad_probs = jnp.einsum(
        "cahd,lad->ahcl", grad_mixed, values, preferred_element_type=jnp.float32
    )
    offset = jnp.einsum("cahd,cahd->ahc", grad_mixed.astype(jnp.float32), mixed_heads)[..., None]
    grad_scores = (probabilities * (grad_probs - offset)).astype(jnp.bfloat16)
    grad_query = (
        jnp.einsum("ahcl,lad->cahd", grad_scores, key_rows, preferred_element_type=jnp.float32)
        * score_scale
    )
    grad_key = (
        jnp.einsum("ahcl,cahd->lad", grad_scores, queries, preferred_element_type=jnp.float32)
        * score_scale
    )
    grad_value = jnp.einsum(
        "ahcl,cahd->lad",
        probabilities.astype(jnp.bfloat16),
        grad_mixed,
        preferred_element_type=jnp.float32,
    )
    return (grad_query, grad_key, grad_value)


def project_back(left, right):
    return jnp.einsum("rf,df->rd", left, right, preferred_element_type=jnp.float32)


def weight_term(left, right):
    return jnp.einsum("rd,rc->dc", left, right, preferred_element_type=jnp.float32)


def per_device(
    tokens,
    prefix,
    w_query,
    w_key,
    w_value,
    w_out,
    w_gate,
    w_up,
    w_down,
    b_query,
    b_key,
    b_value,
    norm_attn,
    norm_mlp,
    cotangent,
):
    seq_dev, own_rows, model_width = tokens.shape
    span_len = own_rows * lax.axis_size("tensor")
    seq_len = span_len * lax.axis_size("ctx")
    row_count = seq_dev * span_len
    q_cols = w_query.shape[1]
    kv_cols = w_key.shape[1]
    kv_heads = kv_cols // HD
    group_size = q_cols // kv_cols
    score_scale = HD ** (-0.5)
    tensor_at = lax.axis_index("tensor")
    local_pos = lax.axis_index("ctx") * span_len + jnp.arange(span_len, dtype=jnp.int32)
    key_pos = jnp.arange(seq_len, dtype=jnp.int32)
    cosine_table, sine_table = rotary_tables(local_pos)
    bias_query = lax.dynamic_slice_in_dim(b_query, tensor_at * q_cols, q_cols)
    bias_key = lax.dynamic_slice_in_dim(b_key, tensor_at * kv_cols, kv_cols)
    bias_value = lax.dynamic_slice_in_dim(b_value, tensor_at * kv_cols, kv_cols)
    cast_query = w_query.astype(jnp.bfloat16)
    cast_key = w_key.astype(jnp.bfloat16)
    cast_value = w_value.astype(jnp.bfloat16)
    cast_out = w_out.astype(jnp.bfloat16)
    cast_gate = w_gate.astype(jnp.bfloat16)
    cast_up = w_up.astype(jnp.bfloat16)
    cast_down = w_down.astype(jnp.bfloat16)
    full_query, full_key, full_value, full_out, full_gate, full_up, full_down = (
        lax.all_gather(cast_query, ("dp", "ctx"), axis=0, tiled=True),
        lax.all_gather(cast_key, ("dp", "ctx"), axis=0, tiled=True),
        lax.all_gather(cast_value, ("dp", "ctx"), axis=0, tiled=True),
        lax.all_gather(cast_out, ("dp", "ctx"), axis=0, tiled=True),
        lax.all_gather(cast_gate, ("dp", "ctx"), axis=0, tiled=True),
        lax.all_gather(cast_up, ("dp", "ctx"), axis=0, tiled=True),
        lax.all_gather(cast_down, ("dp", "ctx"), axis=0, tiled=True),
    )
    x_own = tokens.astype(jnp.float32)
    attn_root = inverse_root(x_own)
    normed1 = lax.all_gather(
        (x_own * attn_root * norm_attn).astype(jnp.bfloat16), "tensor", axis=1, tiled=True
    ).reshape(row_count, model_width)
    query_pre = jnp.dot(normed1, full_query, preferred_element_type=jnp.float32) + bias_query
    key_pre = jnp.dot(normed1, full_key, preferred_element_type=jnp.float32) + bias_key
    value_pre = jnp.dot(normed1, full_value, preferred_element_type=jnp.float32) + bias_value
    queries = rotate(
        query_pre.reshape(seq_dev, span_len, q_cols // HD, HD), cosine_table, sine_table
    ).astype(jnp.bfloat16)
    queries = queries.reshape(seq_dev, span_len, kv_heads, group_size, HD)
    keys_own = rotate(
        key_pre.reshape(seq_dev, span_len, kv_heads, HD), cosine_table, sine_table
    ).astype(jnp.bfloat16)
    values_own = value_pre.reshape(seq_dev, span_len, kv_heads, HD).astype(jnp.bfloat16)
    key_rows, value_rows = (
        lax.all_gather(keys_own, "ctx", axis=1, tiled=True),
        lax.all_gather(values_own, "ctx", axis=1, tiled=True),
    )
    masks = []
    mixed_list = []
    log_totals = []
    for seq_index in range(seq_dev):
        allowed = (key_pos[None, :] <= local_pos[:, None]) | (key_pos[None, :] < prefix[seq_index])
        mixed_heads, log_total = attend(
            queries[seq_index], key_rows[seq_index], value_rows[seq_index], allowed, score_scale
        )
        masks.append(allowed)
        mixed_list.append(mixed_heads)
        log_totals.append(log_total)
    mixed_full = jnp.stack(mixed_list)
    mixed_low = mixed_full.reshape(row_count, q_cols).astype(jnp.bfloat16)
    attn_term = project_back(mixed_low, full_out).reshape(seq_dev, span_len, model_width)
    hidden1 = x_own + lax.psum_scatter(
        attn_term.astype(jnp.bfloat16), "tensor", scatter_dimension=1, tiled=True
    ).astype(jnp.float32)
    mlp_root = inverse_root(hidden1)
    normed2 = lax.all_gather(
        (hidden1 * mlp_root * norm_mlp).astype(jnp.bfloat16), "tensor", axis=1, tiled=True
    ).reshape(row_count, model_width)
    gate_pre = jnp.dot(normed2, full_gate, preferred_element_type=jnp.float32)
    up_pre = jnp.dot(normed2, full_up, preferred_element_type=jnp.float32)
    sigmoid_gate = jax.nn.sigmoid(gate_pre)
    activation = (gate_pre * sigmoid_gate * up_pre).astype(jnp.bfloat16)
    mlp_term = project_back(activation, full_down).reshape(seq_dev, span_len, model_width)
    output = (
        hidden1
        + lax.psum_scatter(
            mlp_term.astype(jnp.bfloat16), "tensor", scatter_dimension=1, tiled=True
        ).astype(jnp.float32)
    ).astype(jnp.bfloat16)
    full_query, full_key, full_value, full_out, full_gate, full_up, full_down = (
        lax.all_gather(cast_query, ("dp", "ctx"), axis=0, tiled=True),
        lax.all_gather(cast_key, ("dp", "ctx"), axis=0, tiled=True),
        lax.all_gather(cast_value, ("dp", "ctx"), axis=0, tiled=True),
        lax.all_gather(cast_out, ("dp", "ctx"), axis=0, tiled=True),
        lax.all_gather(cast_gate, ("dp", "ctx"), axis=0, tiled=True),
        lax.all_gather(cast_up, ("dp", "ctx"), axis=0, tiled=True),
        lax.all_gather(cast_down, ("dp", "ctx"), axis=0, tiled=True),
    )
    grad_out = cotangent.astype(jnp.float32)
    grad_mlp = lax.all_gather(cotangent, "tensor", axis=1, tiled=True).reshape(
        row_count, model_width
    )
    grad_act = jnp.dot(grad_mlp, full_down, preferred_element_type=jnp.float32)
    grad_up = (grad_act * gate_pre * sigmoid_gate).astype(jnp.bfloat16)
    grad_gate = (grad_act * up_pre * sigmoid_gate * (1.0 + gate_pre * (1.0 - sigmoid_gate))).astype(
        jnp.bfloat16
    )
    mlp_back = (project_back(grad_gate, full_gate) + project_back(grad_up, full_up)).reshape(
        seq_dev, span_len, model_width
    )
    grad_normed2 = lax.psum_scatter(
        mlp_back.astype(jnp.bfloat16), "tensor", scatter_dimension=1, tiled=True
    ).astype(jnp.float32)
    scaled2 = norm_mlp * grad_normed2
    grad_hidden1 = (
        grad_out
        + mlp_root * scaled2
        - hidden1 * mlp_root**3 * jnp.mean(scaled2 * hidden1, axis=-1, keepdims=True)
    )
    gain_mlp = jnp.sum(grad_normed2 * hidden1 * mlp_root, axis=(0, 1))
    grad_attn = lax.all_gather(
        grad_hidden1.astype(jnp.bfloat16), "tensor", axis=1, tiled=True
    ).reshape(row_count, model_width)
    grad_mixed = jnp.dot(grad_attn, full_out, preferred_element_type=jnp.float32).astype(
        jnp.bfloat16
    )
    grad_mixed = grad_mixed.reshape(seq_dev, span_len, kv_heads, group_size, HD)
    query_grads = []
    key_grads = []
    value_grads = []
    for seq_index in range(seq_dev):
        grad_query, grad_key, grad_value = attend_back(
            queries[seq_index],
            key_rows[seq_index],
            value_rows[seq_index],
            masks[seq_index],
            score_scale,
            log_totals[seq_index],
            mixed_list[seq_index],
            grad_mixed[seq_index],
        )
        query_grads.append(grad_query)
        key_grads.append(grad_key)
        value_grads.append(grad_value)
    grad_keys, grad_values = (
        lax.psum_scatter(
            jnp.stack(key_grads).astype(jnp.bfloat16), "ctx", scatter_dimension=1, tiled=True
        ).astype(jnp.float32),
        lax.psum_scatter(
            jnp.stack(value_grads).astype(jnp.bfloat16), "ctx", scatter_dimension=1, tiled=True
        ).astype(jnp.float32),
    )
    grad_q = rotate_back(
        jnp.stack(query_grads).reshape(seq_dev, span_len, q_cols // HD, HD),
        cosine_table,
        sine_table,
    )
    grad_q = grad_q.reshape(row_count, q_cols).astype(jnp.bfloat16)
    grad_k = (
        rotate_back(grad_keys, cosine_table, sine_table)
        .reshape(row_count, kv_cols)
        .astype(jnp.bfloat16)
    )
    grad_v = grad_values.reshape(row_count, kv_cols).astype(jnp.bfloat16)
    attn_back = (
        project_back(grad_q, full_query)
        + project_back(grad_k, full_key)
        + project_back(grad_v, full_value)
    )
    grad_normed1 = lax.psum_scatter(
        attn_back.reshape(seq_dev, span_len, model_width).astype(jnp.bfloat16),
        "tensor",
        scatter_dimension=1,
        tiled=True,
    ).astype(jnp.float32)
    scaled1 = norm_attn * grad_normed1
    grad_tokens = (
        grad_hidden1
        + attn_root * scaled1
        - x_own * attn_root**3 * jnp.mean(scaled1 * x_own, axis=-1, keepdims=True)
    ).astype(jnp.bfloat16)
    gain_attn = jnp.sum(grad_normed1 * x_own * attn_root, axis=(0, 1))
    place_query = lax.dynamic_update_slice_in_dim(
        jnp.zeros_like(b_query), jnp.sum(grad_q, axis=0, dtype=jnp.float32), tensor_at * q_cols, 0
    )
    place_key = lax.dynamic_update_slice_in_dim(
        jnp.zeros_like(b_key), jnp.sum(grad_k, axis=0, dtype=jnp.float32), tensor_at * kv_cols, 0
    )
    place_value = lax.dynamic_update_slice_in_dim(
        jnp.zeros_like(b_value), jnp.sum(grad_v, axis=0, dtype=jnp.float32), tensor_at * kv_cols, 0
    )
    sum_attn, sum_mlp, sum_query, sum_key, sum_value = lax.psum(
        (gain_attn, gain_mlp, place_query, place_key, place_value), ("dp", "ctx", "tensor")
    )
    all_terms = jnp.concatenate(
        [
            weight_term(normed1, grad_q),
            weight_term(normed1, grad_k),
            weight_term(normed1, grad_v),
            weight_term(grad_attn, mixed_low),
            weight_term(normed2, grad_gate),
            weight_term(normed2, grad_up),
            weight_term(grad_mlp, activation),
        ],
        axis=1,
    )
    reduced = lax.psum_scatter(all_terms, ("dp", "ctx"), scatter_dimension=0, tiled=True)
    ff_cols = w_gate.shape[1]
    edges = [0, q_cols, q_cols + kv_cols, q_cols + 2 * kv_cols, 2 * q_cols + 2 * kv_cols]
    edges = edges + [edges[4] + ff_cols, edges[4] + 2 * ff_cols, edges[4] + 3 * ff_cols]
    grad_w_query = reduced[:, edges[0] : edges[1]]
    grad_w_key = reduced[:, edges[1] : edges[2]]
    grad_w_value = reduced[:, edges[2] : edges[3]]
    grad_w_out = reduced[:, edges[3] : edges[4]]
    grad_w_gate = reduced[:, edges[4] : edges[5]]
    grad_w_up = reduced[:, edges[5] : edges[6]]
    grad_w_down = reduced[:, edges[6] : edges[7]]
    return (
        output,
        grad_tokens,
        grad_w_query,
        grad_w_key,
        grad_w_value,
        grad_w_out,
        grad_w_gate,
        grad_w_up,
        grad_w_down,
        sum_query,
        sum_key,
        sum_value,
        sum_attn,
        sum_mlp,
    )


def solution(mesh):
    placed = (
        P("dp", ("ctx", "tensor"), None),
        P("dp"),
        P(("dp", "ctx"), "tensor"),
        P(("dp", "ctx"), "tensor"),
        P(("dp", "ctx"), "tensor"),
        P(("dp", "ctx"), "tensor"),
        P(("dp", "ctx"), "tensor"),
        P(("dp", "ctx"), "tensor"),
        P(("dp", "ctx"), "tensor"),
        P(),
        P(),
        P(),
        P(),
        P(),
        P("dp", ("ctx", "tensor"), None),
    )
    return jax.shard_map(
        per_device,
        mesh=mesh,
        in_specs=placed,
        out_specs=(
            P("dp", ("ctx", "tensor"), None),
            P("dp", ("ctx", "tensor"), None),
            P(("dp", "ctx"), "tensor"),
            P(("dp", "ctx"), "tensor"),
            P(("dp", "ctx"), "tensor"),
            P(("dp", "ctx"), "tensor"),
            P(("dp", "ctx"), "tensor"),
            P(("dp", "ctx"), "tensor"),
            P(("dp", "ctx"), "tensor"),
            P(),
            P(),
            P(),
            P(),
            P(),
        ),
        check_vma=False,
    )
```

profile of v0, /device:TPU:0, one launch (start us, length us, event | category | flops | bytes accessed | tf_op | source)
XLA Modules:
  0.0 2103.8 jit_solution(6809508197684230337)
XLA Ops:
  13.3 47.2 %all_gather.47 = bf16[1536,128]{1,0:T(8,128)(2,1)S(1)} all-gather(bf16[96,128]{1,0:T(8,128)(2,1)S(1)} %convert_element_type.224), channel_id=1, replica_groups=mesh['dp'=4,'ctx'=4,'tensor'=2] {'dp','ctx'}, dimensions={0}, use_global_device_ids=true | all-gather | bytes 417792 | tf_op jit(solution)/shard_map/all_gather | solution.py:136
  64.5 16.3 all_gather.48
  81.2 40.2 %all_gather.49 = bf16[1536,128]{1,0:T(8,128)(2,1)S(1)} all-gather(bf16[96,128]{1,0:T(8,128)(2,1)S(1)} %convert_element_type.227), channel_id=1, replica_groups=mesh['dp'=4,'ctx'=4,'tensor'=2] {'dp','ctx'}, dimensions={0}, use_global_device_ids=true | all-gather | bytes 417792 | tf_op jit(solution)/shard_map/all_gather | solution.py:135
  122.8 15.5 all_gather.50
  140.4 3.3 convolution_add_fusion.3
  152.3 3.3 convolution_convert_fusion.1
  160.8 2.6 convert_element_type.241
  169.5 2.5 all_gather.53
  172.1 158.0 %all-gather.12.cloned.1.call-done = bf16[1536,4480]{1,0:T(8,128)(2,1)} async-done(((bf16[96,4480]{1,0:T(8,128)(2,1)}), bf16[1536,4480]{1,0:T(8,128)(2,1)}) %all-gather.12.cloned.1.call-update) | async-done | bytes 13762576 | tf_op jit(solution)/shard_map/all_gather | solution.py:139
  330.0 10.3 fusion.93
  340.4 154.6 %all-gather.10.cloned.1.call-done = bf16[1536,4480]{1,0:T(8,128)(2,1)} async-done(((bf16[96,4480]{1,0:T(8,128)(2,1)}), bf16[1536,4480]{1,0:T(8,128)(2,1)}) %all-gather.10.cloned.1.call-update) | async-done | bytes 13762576 | tf_op jit(solution)/shard_map/all_gather | solution.py:138
  495.0 10.4 fusion.92
  505.3 154.0 %all-gather.14.cloned.1.call-done = bf16[1536,4480]{1,0:T(8,128)(2,1)} async-done(((bf16[96,4480]{1,0:T(8,128)(2,1)}), bf16[1536,4480]{1,0:T(8,128)(2,1)}) %all-gather.14.cloned.1.call-update) | async-done | bytes 13762576 | tf_op jit(solution)/shard_map/all_gather | solution.py:140
  659.3 11.3 multiply_convert_fusion
  670.6 9.9 fusion.94
  680.6 8.7 fusion
  692.9 3.0 reduce-scatter.14.cloned.1.call-done
  699.2 2.6 all_gather.58
  719.4 2.8 bitcast_reduce_fusion
  728.0 3.1 fusion.59
  731.1 7.3 reduce-scatter.16.cloned.1.call-done
  740.0 19.2 reduce-scatter.22.cloned.1.call-done
  766.1 10.7 convolution_convert_fusion
  777.3 3.1 convolution_dynamic-update-slice_fusion.3
  783.3 3.1 convolution_dynamic-update-slice_fusion.2
  786.4 11.2 convolution_dynamic-update-slice_fusion.1
  797.5 11.1 convolution_dynamic-update-slice_fusion
  808.6 11.1 bitcast_dynamic-update-slice_fusion
  822.7 42.8 %all-reduce = (f32[1536]{0:T(1024)}, f32[256]{0:T(256)}, f32[256]{0:T(256)}, f32[1536]{0:T(1024)}, f32[1536]{0:T(1024)}) all-reduce(f32[1536]{0:T(1024)S(1)} %bitcast_dynamic-update-slice_fusion.1, f32[256]{0:T(256)S(1)} %dynamic_update_slice.10, ...), channel_id=1, replica_groups=mesh['dp'=4,'ctx'=4,'tensor'=2] {'dp','ctx','tensor'}, use_global_device_ids=true, to_apply=%region_16.17 | all-reduce | flops 5120 | bytes 40960 | tf_op jit(solution)/shard_map/psum | solution.py:296
  865.5 2.7 fusion.31
  868.1 1220.0 %reduce-scatter.20.cloned.1.call-done = f32[96,15232]{1,0:T(8,128)} async-done(((f32[1536,15232]{1,0:T(8,128)}), f32[96,15232]{1,0:T(8,128)}) %reduce-scatter.20.cloned.1.call-update) | async-done | bytes 5849104 | tf_op jit(solution)/shard_map/reduce_scatter | solution.py:311
  2091.5 4.9 fusion.83
  (263 shorter events, 81.5 us)
Async XLA Ops:
  7.2 53.3 %copy-start = (bf16[2,64,1536]{2,1,0:T(8,128)(2,1)S(1)}, bf16[2,64,1536]{2,1,0:T(8,128)(2,1)}, u32[]{:S(2)}) copy-start(bf16[2,64,1536]{2,1,0:T(8,128)(2,1)} %param.15) | copy-start | bytes 1179652
  7.2 56.5 %copy-start.67 = (f32[256]{0:T(256)S(1)}, f32[256]{0:T(256)}, u32[]{:S(2)}) copy-start(f32[256]{0:T(256)} %param.26) | copy-start | bytes 3076
  7.2 133.2 %all-gather.6.cloned.1.call-start = ((), (), s32[]{:S(2)}) async-start(), calls=%async_computation.7 | async-start | bytes 2506752 | tf_op jit(solution)/shard_map/all_gather | solution.py:134
  8.9 55.2 %copy-start.68 = (f32[256]{0:T(256)S(1)}, f32[256]{0:T(256)}, u32[]{:S(2)}) copy-start(f32[256]{0:T(256)} %param.25) | copy-start | bytes 3076
  9.0 55.3 %copy-start.52 = (f32[96,128]{1,0:T(8,128)S(1)}, f32[96,128]{1,0:T(8,128)}, u32[]{:S(2)}) copy-start(f32[96,128]{1,0:T(8,128)} %param.18) | copy-start | bytes 147460
  9.0 143.3 %all-gather.8.cloned.1.call-start = ((), (), s32[]{:S(2)}) async-start(), calls=%async_computation.8 | async-start | bytes 2506752 | tf_op jit(solution)/shard_map/all_gather | solution.py:137
  10.7 53.7 %copy-start.63 = (f32[1536]{0:T(1024)S(1)}, f32[1536]{0:T(1024)}, u32[]{:S(2)}) copy-start(f32[1536]{0:T(1024)} %param.24) | copy-start | bytes 18436
  10.7 155.3 %reduce-scatter.10.cloned.1.call-start = ((), (), s32[]{:S(2)}) async-start(), calls=%async_computation.9 | async-start | bytes 1179648 | tf_op jit(solution)/shard_map/reduce_scatter | solution.py:176
  12.5 51.3 %copy-start.57 = (f32[2,64]{1,0:T(2,128)}, f32[2,64]{1,0:T(2,128)S(1)}, u32[]{:S(2)}) copy-start(f32[2,64]{1,0:T(2,128)S(1)} %get-tuple-element.53) | copy-start | bytes 1540
  60.5 62.1 %copy-start.10 = (bf16[1536,128]{1,0:T(8,128)(2,1)}, bf16[1536,128]{1,0:T(8,128)(2,1)S(1)}, u32[]{:S(2)}) copy-start(bf16[1536,128]{1,0:T(8,128)(2,1)S(1)} %all_gather.47) | copy-start | bytes 1179652
  64.1 74.1 %copy-start.64 = (s32[2]{0:T(128)S(1)}, s32[2]{0:T(128)}, u32[]{:S(2)}) copy-start(s32[2]{0:T(128)} %param.16) | copy-start | bytes 28
  81.2 64.2 %copy-start.19 = (f32[128,128]{1,0:T(8,128)}, f32[128,128]{1,0:T(8,128)S(1)}, u32[]{:S(2)}) copy-start(f32[128,128]{1,0:T(8,128)S(1)} %get-tuple-element.50) | copy-start | bytes 196612
  81.2 64.2 %copy-start.28 = (f32[128,128]{1,0:T(8,128)}, f32[128,128]{1,0:T(8,128)S(1)}, u32[]{:S(2)}) copy-start(f32[128,128]{1,0:T(8,128)S(1)} %get-tuple-element.51) | copy-start | bytes 196612
  138.3 11.7 copy-start.21
  155.7 174.3 %all-gather.12.cloned.1.call-start = ((), (), s32[]{:S(2)}) async-start(), calls=%async_computation.11 | async-start | bytes 14622720 | tf_op jit(solution)/shard_map/all_gather | solution.py:139
  158.2 336.7 %all-gather.10.cloned.1.call-start = ((), (), s32[]{:S(2)}) async-start(), calls=%async_computation.10 | async-start | bytes 14622720 | tf_op jit(solution)/shard_map/all_gather | solution.py:138
  160.8 498.6 %all-gather.14.cloned.1.call-start = ((), (), s32[]{:S(2)}) async-start(), calls=%async_computation.12 | async-start | bytes 14622720 | tf_op jit(solution)/shard_map/all_gather | solution.py:140
  163.4 532.4 %reduce-scatter.14.cloned.1.call-start = ((), (), s32[]{:S(2)}) async-start(), calls=%async_computation.14 | async-start | bytes 1179648 | tf_op jit(solution)/shard_map/reduce_scatter | solution.py:215
  172.1 322.9 %copy-start.4 = (bf16[2,128,1536]{2,1,0:T(8,128)(2,1)}, bf16[2,128,1536]{2,1,0:T(8,128)(2,1)S(1)}, u32[]{:S(2)}) copy-start(bf16[2,128,1536]{2,1,0:T(8,128)(2,1)S(1)} %all_gather.53) | copy-start | bytes 2359300
  680.6 15.3 copy-start.3
  689.3 49.1 %reduce-scatter.16.cloned.1.call-start = ((), (), s32[]{:S(2)}) async-start(), calls=%async_computation.15 | async-start | bytes 327680 | tf_op jit(solution)/shard_map/reduce_scatter | solution.py:250
  717.3 41.9 %reduce-scatter.22.cloned.1.call-start = ((), (), s32[]{:S(2)}) async-start(), calls=%async_computation.18 | async-start | bytes 327680
  727.7 93.7 %reduce-scatter.18.cloned.1.call-start = ((), (), s32[]{:S(2)}) async-start(), calls=%async_computation.16 | async-start | bytes 1179648 | tf_op jit(solution)/shard_map/reduce_scatter | solution.py:274
  728.0 35.4 %copy-start.9 = (bf16[1536,128]{1,0:T(8,128)(2,1)S(1)}, bf16[1536,128]{1,0:T(8,128)(2,1)}, u32[]{:S(2)}) copy-start(bf16[1536,128]{1,0:T(8,128)(2,1)} %copy-done.8) | copy-start | bytes 1179652
  765.3 100.2 %reduce-scatter.12.cloned.1.call-start = ((), (), s32[]{:S(2)}) async-start(), calls=%async_computation.13 | async-start | bytes 1179648 | tf_op jit(solution)/shard_map/reduce_scatter | solution.py:190
  776.8 1311.4 %reduce-scatter.20.cloned.1.call-start = ((), (), s32[]{:S(2)}) async-start(), calls=%async_computation.17 | async-start | bytes 99434496 | tf_op jit(solution)/shard_map/reduce_scatter | solution.py:311
  786.4 11.2 copy-start.25
  819.8 45.7 %copy-start.14 = (bf16[2,64,1536]{2,1,0:T(8,128)(2,1)S(1)}, bf16[2,64,1536]{2,1,0:T(8,128)(2,1)}, u32[]{:S(2)}) copy-start(bf16[2,64,1536]{2,1,0:T(8,128)(2,1)} %param.29) | copy-start | bytes 1179652
  819.8 45.7 %copy-start.15 = (bf16[2,64,1536]{2,1,0:T(8,128)(2,1)S(1)}, bf16[2,64,1536]{2,1,0:T(8,128)(2,1)}, u32[]{:S(2)}) copy-start(bf16[2,64,1536]{2,1,0:T(8,128)(2,1)} %reduce-scatter.14.cloned.1.call-done) | copy-start | bytes 1179652
  819.8 45.7 %copy-start.56 = (f32[2,64]{1,0:T(2,128)S(1)}, f32[2,64]{1,0:T(2,128)}, u32[]{:S(2)}) copy-start(f32[2,64]{1,0:T(2,128)} %copy-done.55) | copy-start | bytes 1540
  819.8 45.7 %copy-start.61 = (f32[2,64]{1,0:T(2,128)S(1)}, f32[2,64]{1,0:T(2,128)}, u32[]{:S(2)}) copy-start(f32[2,64]{1,0:T(2,128)} %get-tuple-element.54) | copy-start | bytes 1540
  819.8 45.7 %copy-start.62 = (f32[2,64]{1,0:T(2,128)S(1)}, f32[2,64]{1,0:T(2,128)}, u32[]{:S(2)}) copy-start(f32[2,64]{1,0:T(2,128)} %get-tuple-element.52) | copy-start | bytes 1540
  (49 other events, 167.3 us)
Sparse Core Ops, SparseCore 0:
  11.4 68.8 all-gather.5
  83.6 61.3 all-gather.7
  155.8 6.2 reduce-scatter.9
  165.7 164.2 all-gather.11
  333.6 161.3 all-gather.9
  498.0 161.3 all-gather.13
  689.4 6.4 reduce-scatter.13
  717.5 20.8 reduce-scatter.15
  741.3 17.9 reduce-scatter.21
  765.4 6.4 reduce-scatter.17
  776.9 7.2 reduce-scatter.11
  820.0 1268.1 reduce-scatter.19
where the time goes:
time: 2110 us; the launch traced here: 2100 us
  waiting for transfers between devices  1720 us (82%)
  blocking collectives  172 us (8%)
  matrix products  128 us (6%)
  other arithmetic  39.4 us (2%)
  local copies, waits for them, and re-layouts  32.3 us (2%)
    reduce_scatter x1, waiting for transfers between devices, per_device(): lax.psum_scatter(all_terms, ('dp', 'ctx'), scatter_dimension=0, tiled=True)  1220 us
    all_gather x1, waiting for transfers between devices, per_device(): lax.all_gather(cast_up, ('dp', 'ctx'), axis=0, tiled=True)  158 us
    all_gather x1, waiting for transfers between devices, per_device(): lax.all_gather(cast_gate, ('dp', 'ctx'), axis=0, tiled=True)  155 us
    all_gather x1, waiting for transfers between devices, per_device(): lax.all_gather(cast_down, ('dp', 'ctx'), axis=0, tiled=True)  154 us
    all_gather x1, blocking collectives, per_device(): lax.all_gather(cast_value, ('dp', 'ctx'), axis=0, tiled=True)  47.2 us
    psum x1, blocking collectives, per_device(): lax.psum((gain_attn, gain_mlp, place_query, place_key, place_value), ('dp...  42.8 us
    dot_general x7, matrix products, weight_term(): jnp.einsum('rd,rc->dc', left, right, preferred_element_type=jnp.float32)  42.4 us
  transfers between devices with their start and end apart: 12, of which 7 were waited for; matrix products, arithmetic and copies ran while one was open for 6% of the time, Pallas kernels for 0%

commit v1 on v0

v1 whole, which is shorter than its diff:
```python
import jax
import jax.numpy as jnp
from jax import lax
from jax.sharding import PartitionSpec as P

HD = 128


epsilon = 1e-06
rope_base = 1000000.0


def inverse_root(value):
    return lax.rsqrt(jnp.mean(value * value, axis=-1, keepdims=True) + epsilon)


def rotary_tables(positions):
    half_dim = HD // 2
    frequency = rope_base ** (-2.0 * jnp.arange(half_dim, dtype=jnp.float32) / HD)
    angles = positions.astype(jnp.float32)[:, None] * frequency[None, :]
    angles = jnp.concatenate([angles, angles], axis=1)
    return (jnp.cos(angles)[:, None, :], jnp.sin(angles)[:, None, :])


def rotate(value, cosine_table, sine_table):
    half_dim = value.shape[-1] // 2
    turned = jnp.concatenate([-value[..., half_dim:], value[..., :half_dim]], axis=-1)
    return value * cosine_table + turned * sine_table


def rotate_back(grad_rows, cosine_table, sine_table):
    half_dim = grad_rows.shape[-1] // 2
    scaled = grad_rows * sine_table
    turned = jnp.concatenate([scaled[..., half_dim:], -scaled[..., :half_dim]], axis=-1)
    return grad_rows * cosine_table + turned


def scores_of(queries, key_rows, allowed, score_scale):
    raw_scores = (
        jnp.einsum("cahd,lad->ahcl", queries, key_rows, preferred_element_type=jnp.float32)
        * score_scale
    )
    return jnp.where(allowed[None, None], raw_scores, -1e30)


def attend(queries, key_rows, values, allowed, score_scale):
    scores = scores_of(queries, key_rows, allowed, score_scale)
    peak = jnp.max(scores, axis=-1, keepdims=True)
    weights = jnp.exp(scores - peak)
    denominator = jnp.sum(weights, axis=-1, keepdims=True)
    probabilities = (weights / denominator).astype(jnp.bfloat16)
    mixed_heads = jnp.einsum(
        "ahcl,lad->cahd", probabilities, values, preferred_element_type=jnp.float32
    )
    return (mixed_heads, peak + jnp.log(denominator))


def attend_back(
    queries, key_rows, values, allowed, score_scale, log_total, mixed_heads, grad_mixed
):
    scores = scores_of(queries, key_rows, allowed, score_scale)
    probabilities = jnp.exp(scores - log_total)
    grad_probs = jnp.einsum(
        "cahd,lad->ahcl", grad_mixed, values, preferred_element_type=jnp.float32
    )
    offset = jnp.einsum("cahd,cahd->ahc", grad_mixed.astype(jnp.float32), mixed_heads)[..., None]
    grad_scores = (probabilities * (grad_probs - offset)).astype(jnp.bfloat16)
    grad_query = (
        jnp.einsum("ahcl,lad->cahd", grad_scores, key_rows, preferred_element_type=jnp.float32)
        * score_scale
    )
    grad_key = (
        jnp.einsum("ahcl,cahd->lad", grad_scores, queries, preferred_element_type=jnp.float32)
        * score_scale
    )
    grad_value = jnp.einsum(
        "ahcl,cahd->lad",
        probabilities.astype(jnp.bfloat16),
        grad_mixed,
        preferred_element_type=jnp.float32,
    )
    return (grad_query, grad_key, grad_value)


def project_back(left, right):
    return jnp.einsum("rf,df->rd", left, right, preferred_element_type=jnp.float32)


def weight_term(left, right):
    return jnp.einsum("rd,rc->dc", left, right, preferred_element_type=jnp.float32)


def update_at(target, block, index):
    return lax.dynamic_update_index_in_dim(target, block, index, 0)


def pick(source, index, axis=0):
    return lax.dynamic_index_in_dim(source, index, axis, keepdims=False)


def swap_tensor(value):
    return lax.ppermute(value, "tensor", [(0, 1), (1, 0)])


def shift_ctx(value, distance):
    size = lax.axis_size("ctx")
    return lax.ppermute(value, "ctx", [(i, (i + distance) % size) for i in range(size)])


def swap_dp(value, bit):
    return lax.ppermute(value, "dp", [(i, i ^ bit) for i in range(lax.axis_size("dp"))])


def ring_blocks(value):
    blocks = [value]
    for _ in range(lax.axis_size("ctx") - 1):
        blocks.append(shift_ctx(blocks[-1], 1))
    return blocks


def ring_sum(blocks):
    size = lax.axis_size("ctx")
    total = blocks[1 % size]
    for step in range(1, size):
        total = shift_ctx(total.astype(jnp.bfloat16), 1).astype(jnp.float32)
        total = total + blocks[(step + 1) % size].astype(jnp.float32)
    return total


def spread_ctx(columns):
    size = lax.axis_size("ctx")
    own = lax.axis_index("ctx")
    gathered = jnp.zeros_like(columns)
    gathered = update_at(gathered, pick(columns, own), own)
    for distance in range(1, size):
        got = shift_ctx(pick(columns, (own + distance) % size), distance)
        gathered = update_at(gathered, got, (own - distance) % size)
    return gathered


def gather_ctx(value):
    size = lax.axis_size("ctx")
    own = lax.axis_index("ctx")
    gathered = jnp.zeros((size,) + value.shape, value.dtype)
    for distance, block in enumerate(ring_blocks(value)):
        gathered = update_at(gathered, block, (own - distance) % size)
    return gathered


def gather_dp(value):
    rows, columns = value.shape
    own = lax.axis_index("dp")
    low, high = own % 2, own // 2
    half = rows // 2
    first, second = value[:half], value[half:]
    full = jnp.zeros((2, 2, 2, half, columns), value.dtype)
    pair_x = jnp.zeros((2, half, columns), value.dtype)
    pair_x = update_at(update_at(pair_x, first, low), swap_dp(first, 1), 1 - low)
    pair_y = jnp.zeros((2, half, columns), value.dtype)
    pair_y = update_at(update_at(pair_y, second, high), swap_dp(second, 2), 1 - high)
    far_x = swap_dp(pair_x, 2)
    far_y = swap_dp(pair_y, 1)
    full = lax.dynamic_update_slice(full, pair_x[None, :, None], (high, 0, 0, 0, 0))
    full = lax.dynamic_update_slice(full, far_x[None, :, None], (1 - high, 0, 0, 0, 0))
    full = lax.dynamic_update_slice(full, pair_y[:, None, None], (0, low, 1, 0, 0))
    full = lax.dynamic_update_slice(full, far_y[:, None, None], (0, 1 - low, 1, 0, 0))
    return full.reshape(4 * rows, columns)


def scatter_dp(value):
    rows, columns = value.shape[0] // 4, value.shape[1]
    own = lax.axis_index("dp")
    low, high = own % 2, own // 2
    half = rows // 2
    terms = value.reshape(2, 2, 2, half, columns)
    first, second = terms[:, :, 0], terms[:, :, 1]
    sent_x = swap_dp(pick(first, 1 - low, 1).astype(jnp.bfloat16), 1)
    sent_y = swap_dp(pick(second, 1 - high, 0).astype(jnp.bfloat16), 2)
    pair_x = pick(first, low, 1).astype(jnp.float32) + sent_x.astype(jnp.float32)
    pair_y = pick(second, high, 0).astype(jnp.float32) + sent_y.astype(jnp.float32)
    last_x = swap_dp(pick(pair_x, 1 - high).astype(jnp.bfloat16), 2)
    last_y = swap_dp(pick(pair_y, 1 - low).astype(jnp.bfloat16), 1)
    return jnp.concatenate(
        [
            pick(pair_x, high) + last_x.astype(jnp.float32),
            pick(pair_y, low) + last_y.astype(jnp.float32),
        ],
        axis=0,
    )


def hidden_weight(weight, ff_part):
    rows, columns = weight.shape
    size = lax.axis_size("ctx")
    wide = jnp.pad(weight.astype(jnp.bfloat16), ((0, 0), (0, size * ff_part - columns)))
    parts = jnp.stack([wide[:, c * ff_part : (c + 1) * ff_part] for c in range(size)])
    return gather_dp(spread_ctx(parts).reshape(size * rows, ff_part))


def hidden_grad(term, columns):
    size = lax.axis_size("ctx")
    mine = scatter_dp(term).astype(jnp.bfloat16)
    ff_part = mine.shape[1]
    parts = spread_ctx(mine.reshape(size, -1, ff_part))
    wide = jnp.concatenate([parts[c] for c in range(size)], axis=1)
    return wide[:, :columns].astype(jnp.float32)


def attn_grad(term):
    size = lax.axis_size("ctx")
    own = lax.axis_index("ctx")
    mine = scatter_dp(term)
    parts = mine.reshape(size, -1, mine.shape[1])
    return ring_sum([pick(parts, (own - j) % size) for j in range(size)])


def gather_span(value):
    mine = jnp.concatenate([b.reshape(-1, b.shape[-1]) for b in ring_blocks(value)], axis=0)
    return jnp.concatenate([mine, swap_tensor(mine)], axis=0)


def scatter_span(term, shape):
    size = lax.axis_size("ctx")
    half = term.shape[0] // 2
    mine = term[:half].astype(jnp.float32) + swap_tensor(term[half:].astype(jnp.bfloat16)).astype(
        jnp.float32
    )
    blocks = mine.reshape(size, half // size, -1)
    return ring_sum([blocks[j] for j in range(size)]).reshape(shape)


def per_device(
    tokens,
    prefix,
    w_query,
    w_key,
    w_value,
    w_out,
    w_gate,
    w_up,
    w_down,
    b_query,
    b_key,
    b_value,
    norm_attn,
    norm_mlp,
    cotangent,
):
    bf16, f32 = jnp.bfloat16, jnp.float32
    seq_dev, own_rows, model_width = tokens.shape
    ctx_size = lax.axis_size("ctx")
    span_len = own_rows * 2
    seq_len = span_len * ctx_size
    row_count = seq_dev * span_len
    q_cols = w_query.shape[1]
    kv_cols = w_key.shape[1]
    ff_cols = w_gate.shape[1]
    ff_part = -(-ff_cols // (128 * ctx_size)) * 128
    kv_heads = kv_cols // HD
    group_size = q_cols // kv_cols
    score_scale = HD ** (-0.5)
    tensor_at = lax.axis_index("tensor")
    ctx_at = lax.axis_index("ctx")
    own_pos = jnp.arange(own_rows, dtype=jnp.int32)
    in_span = jnp.concatenate([tensor_at * own_rows + own_pos, (1 - tensor_at) * own_rows + own_pos])
    local_pos = ctx_at * span_len + in_span
    key_pos = jnp.concatenate(
        [((ctx_at - j) % ctx_size) * span_len + in_span for j in range(ctx_size)]
    )
    cosine_table, sine_table = rotary_tables(local_pos)
    bias_query = lax.dynamic_slice_in_dim(b_query, tensor_at * q_cols, q_cols)
    bias_key = lax.dynamic_slice_in_dim(b_key, tensor_at * kv_cols, kv_cols)
    bias_value = lax.dynamic_slice_in_dim(b_value, tensor_at * kv_cols, kv_cols)
    bias_all = jnp.concatenate([bias_query, bias_key, bias_value])
    cast_qkv = jnp.concatenate([w.astype(bf16) for w in (w_query, w_key, w_value)], axis=1)
    full_qkv = gather_dp(gather_ctx(cast_qkv).reshape(-1, cast_qkv.shape[1]))
    full_out = gather_dp(gather_ctx(w_out.astype(bf16)).reshape(-1, q_cols))
    full_gate = hidden_weight(w_gate, ff_part)
    full_up = hidden_weight(w_up, ff_part)
    full_down = hidden_weight(w_down, ff_part)

    x_own = tokens.astype(f32)
    attn_root = inverse_root(x_own)
    normed_own = (x_own * attn_root * norm_attn).astype(bf16)
    normed1 = jnp.concatenate([normed_own, swap_tensor(normed_own)], axis=1).reshape(
        row_count, model_width
    )
    qkv_pre = jnp.dot(normed1, full_qkv, preferred_element_type=f32) + bias_all
    query_pre = qkv_pre[:, :q_cols]
    key_pre = qkv_pre[:, q_cols : q_cols + kv_cols]
    value_pre = qkv_pre[:, q_cols + kv_cols :]
    queries = rotate(
        query_pre.reshape(seq_dev, span_len, q_cols // HD, HD), cosine_table, sine_table
    ).astype(bf16)
    queries = queries.reshape(seq_dev, span_len, kv_heads, group_size, HD)
    keys_own = rotate(
        key_pre.reshape(seq_dev, span_len, kv_heads, HD), cosine_table, sine_table
    ).astype(bf16)
    values_own = value_pre.reshape(seq_dev, span_len, kv_heads, HD).astype(bf16)
    both = jnp.concatenate(ring_blocks(jnp.stack([keys_own, values_own])), axis=2)
    key_rows, value_rows = both[0], both[1]
    masks = []
    mixed_list = []
    log_totals = []
    for seq_index in range(seq_dev):
        allowed = (key_pos[None, :] <= local_pos[:, None]) | (key_pos[None, :] < prefix[seq_index])
        mixed_heads, log_total = attend(
            queries[seq_index], key_rows[seq_index], value_rows[seq_index], allowed, score_scale
        )
        masks.append(allowed)
        mixed_list.append(mixed_heads)
        log_totals.append(log_total)
    mixed_full = jnp.stack(mixed_list)
    mixed_low = mixed_full.reshape(row_count, q_cols).astype(bf16)
    attn_term = project_back(mixed_low, full_out).reshape(seq_dev, span_len, model_width)
    hidden1 = (
        x_own
        + attn_term[:, :own_rows]
        + swap_tensor(attn_term[:, own_rows:].astype(bf16)).astype(f32)
    )
    mlp_root = inverse_root(hidden1)
    normed2 = gather_span((hidden1 * mlp_root * norm_mlp).astype(bf16))
    grad_mlp = gather_span(cotangent)
    gate_pre = jnp.dot(normed2, full_gate, preferred_element_type=f32)
    up_pre = jnp.dot(normed2, full_up, preferred_element_type=f32)
    sigmoid_gate = jax.nn.sigmoid(gate_pre)
    activation = (gate_pre * sigmoid_gate * up_pre).astype(bf16)
    grad_w_down = hidden_grad(weight_term(grad_mlp, activation), ff_cols)
    grad_act = jnp.dot(grad_mlp, full_down, preferred_element_type=f32)
    grad_up = (grad_act * gate_pre * sigmoid_gate).astype(bf16)
    grad_gate = (grad_act * up_pre * sigmoid_gate * (1.0 + gate_pre * (1.0 - sigmoid_gate))).astype(
        bf16
    )
    mlp_back = project_back(grad_gate, full_gate) + project_back(grad_up, full_up)
    grad_normed2 = scatter_span(mlp_back, tokens.shape)
    grad_w_gate = hidden_grad(weight_term(normed2, grad_gate), ff_cols)
    grad_w_up = hidden_grad(weight_term(normed2, grad_up), ff_cols)
    mlp_term = project_back(activation, full_down)
    output = (hidden1 + scatter_span(mlp_term, tokens.shape)).astype(bf16)
    grad_out = cotangent.astype(f32)
    scaled2 = norm_mlp * grad_normed2
    grad_hidden1 = (
        grad_out
        + mlp_root * scaled2
        - hidden1 * mlp_root**3 * jnp.mean(scaled2 * hidden1, axis=-1, keepdims=True)
    )
    gain_mlp = jnp.sum(grad_normed2 * hidden1 * mlp_root, axis=(0, 1))
    grad_own = grad_hidden1.astype(bf16)
    grad_attn = jnp.concatenate([grad_own, swap_tensor(grad_own)], axis=1).reshape(
        row_count, model_width
    )
    grad_w_out = attn_grad(weight_term(grad_attn, mixed_low))
    grad_mixed = jnp.dot(grad_attn, full_out, preferred_element_type=f32).astype(bf16)
    grad_mixed = grad_mixed.reshape(seq_dev, span_len, kv_heads, group_size, HD)
    query_grads = []
    key_grads = []
    value_grads = []
    for seq_index in range(seq_dev):
        grad_query, grad_key, grad_value = attend_back(
            queries[seq_index],
            key_rows[seq_index],
            value_rows[seq_index],
            masks[seq_index],
            score_scale,
            log_totals[seq_index],
            mixed_list[seq_index],
            grad_mixed[seq_index],
        )
        query_grads.append(grad_query)
        key_grads.append(grad_key)
        value_grads.append(grad_value)
    kv_terms = jnp.stack([jnp.stack(key_grads), jnp.stack(value_grads)])
    kv_sum = ring_sum(
        [kv_terms[:, :, j * span_len : (j + 1) * span_len] for j in range(ctx_size)]
    )
    grad_q = rotate_back(
        jnp.stack(query_grads).reshape(seq_dev, span_len, q_cols // HD, HD),
        cosine_table,
        sine_table,
    )
    grad_q = grad_q.reshape(row_count, q_cols).astype(bf16)
    grad_k = rotate_back(kv_sum[0], cosine_table, sine_table).reshape(row_count, kv_cols)
    grad_k = grad_k.astype(bf16)
    grad_v = kv_sum[1].reshape(row_count, kv_cols).astype(bf16)
    grad_qkv = jnp.concatenate([grad_q, grad_k, grad_v], axis=1)
    attn_back = project_back(grad_qkv, full_qkv).reshape(seq_dev, span_len, model_width)
    grad_w_qkv = attn_grad(weight_term(normed1, grad_qkv))
    grad_normed1 = attn_back[:, :own_rows] + swap_tensor(
        attn_back[:, own_rows:].astype(bf16)
    ).astype(f32)
    scaled1 = norm_attn * grad_normed1
    grad_tokens = (
        grad_hidden1
        + attn_root * scaled1
        - x_own * attn_root**3 * jnp.mean(scaled1 * x_own, axis=-1, keepdims=True)
    ).astype(bf16)
    gain_attn = jnp.sum(grad_normed1 * x_own * attn_root, axis=(0, 1))
    place_query = lax.dynamic_update_slice_in_dim(
        jnp.zeros_like(b_query), jnp.sum(grad_q, axis=0, dtype=f32), tensor_at * q_cols, 0
    )
    place_key = lax.dynamic_update_slice_in_dim(
        jnp.zeros_like(b_key), jnp.sum(grad_k, axis=0, dtype=f32), tensor_at * kv_cols, 0
    )
    place_value = lax.dynamic_update_slice_in_dim(
        jnp.zeros_like(b_value), jnp.sum(grad_v, axis=0, dtype=f32), tensor_at * kv_cols, 0
    )
    sum_attn, sum_mlp, sum_query, sum_key, sum_value = lax.psum(
        (gain_attn, gain_mlp, place_query, place_key, place_value), ("dp", "ctx", "tensor")
    )
    grad_w_query = grad_w_qkv[:, :q_cols]
    grad_w_key = grad_w_qkv[:, q_cols : q_cols + kv_cols]
    grad_w_value = grad_w_qkv[:, q_cols + kv_cols :]
    return (
        output,
        grad_tokens,
        grad_w_query,
        grad_w_key,
        grad_w_value,
        grad_w_out,
        grad_w_gate,
        grad_w_up,
        grad_w_down,
        sum_query,
        sum_key,
        sum_value,
        sum_attn,
        sum_mlp,
    )


def solution(mesh):
    placed = (
        P("dp", ("ctx", "tensor"), None),
        P("dp"),
        P(("dp", "ctx"), "tensor"),
        P(("dp", "ctx"), "tensor"),
        P(("dp", "ctx"), "tensor"),
        P(("dp", "ctx"), "tensor"),
        P(("dp", "ctx"), "tensor"),
        P(("dp", "ctx"), "tensor"),
        P(("dp", "ctx"), "tensor"),
        P(),
        P(),
        P(),
        P(),
        P(),
        P("dp", ("ctx", "tensor"), None),
    )
    return jax.shard_map(
        per_device,
        mesh=mesh,
        in_specs=placed,
        out_specs=(
            P("dp", ("ctx", "tensor"), None),
            P("dp", ("ctx", "tensor"), None),
            P(("dp", "ctx"), "tensor"),
            P(("dp", "ctx"), "tensor"),
            P(("dp", "ctx"), "tensor"),
            P(("dp", "ctx"), "tensor"),
            P(("dp", "ctx"), "tensor"),
            P(("dp", "ctx"), "tensor"),
            P(("dp", "ctx"), "tensor"),
            P(),
            P(),
            P(),
            P(),
            P(),
        ),
        check_vma=False,
    )
```

time: 2110 us -> 793 us (0.38)
  waiting for transfers between devices: 1720 us -> 344 us
  starting transfers between devices: 0.75 us -> 140 us
  blocking collectives: 172 us -> 46.9 us
  local copies, waits for them, and re-layouts: 32.3 us -> 112 us
  matrix products: 128 us -> 78.6 us
    reduce_scatter x6 -> x0, waiting for transfers between devices: 1230 us -> none  [the longest x1 1220 us: per_device(): lax.psum_scatter(all_terms, ('dp', 'ctx'), scatter_dimension=0, tiled=True)]
    all_gather x5 -> x0, waiting for transfers between devices: 467 us -> none  [the longest x1 158 us: per_device(): lax.all_gather(cast_up, ('dp', 'ctx'), axis=0, tiled=True)]
    ppermute x0 -> x96, waiting for transfers between devices: none -> 344 us  [the longest x40 187 us: swap_dp(): lax.ppermute(value, 'dp', [(i, i ^ bit) for i in range(lax.axis_size('dp'...]
    ppermute x0 -> x96, starting transfers between devices: none -> 140 us  [the longest x48 91.7 us: shift_ctx(): lax.ppermute(value, 'ctx', [(i, (i + distance) % size) for i in range(siz...]
    all_gather x8 -> x0, blocking collectives: 129 us -> none  [the longest x1 47.2 us: per_device(): lax.all_gather(cast_value, ('dp', 'ctx'), axis=0, tiled=True)]
    dynamic_update_slice x0 -> x63, local copies, waits for them, and re-layouts: none -> 29 us  [the longest x43 18 us: update_at(): return lax.dynamic_update_index_in_dim(target, block, index, 0)]
    dot_general x7 -> x5, matrix products: 42.4 us -> 18.8 us  [weight_term(): jnp.einsum('rd,rc->dc', left, right, preferred_element_type=jnp.float32)]
  transfers between devices with their start and end apart: 12 -> 96, of which waited for: 7 -> 47; matrix products, arithmetic and copies ran while one was open for 6% -> 21% of each run, Pallas kernels for 0% -> 0%
where the time goes in v1:
time: 793 us; the launch traced here: 783 us
  waiting for transfers between devices  344 us (43%)
  starting transfers between devices  140 us (18%)
  local copies, waits for them, and re-layouts  112 us (14%)
  matrix products  78.6 us (10%)
  other arithmetic  58 us (7%)
  blocking collectives  46.9 us (6%)
    ppermute x40, waiting for transfers between devices, swap_dp(): lax.ppermute(value, 'dp', [(i, i ^ bit) for i in range(lax.axis_size('dp'...  187 us
    ppermute x48, waiting for transfers between devices, shift_ctx(): lax.ppermute(value, 'ctx', [(i, (i + distance) % size) for i in range(siz...  157 us
    ppermute x48, starting transfers between devices, shift_ctx(): lax.ppermute(value, 'ctx', [(i, (i + distance) % size) for i in range(siz...  91.7 us
    ppermute x40, starting transfers between devices, swap_dp(): lax.ppermute(value, 'dp', [(i, i ^ bit) for i in range(lax.axis_size('dp'...  47.5 us
    psum x1, blocking collectives, per_device(): lax.psum((gain_attn, gain_mlp, place_query, place_key, place_value), ('dp...  46.9 us
    dot_general x5, matrix products, project_back(): jnp.einsum('rf,df->rd', left, right, preferred_element_type=jnp.float32)  26.7 us
    dot_general x5, matrix products, weight_term(): jnp.einsum('rd,rc->dc', left, right, preferred_element_type=jnp.float32)  18.8 us
    dynamic_update_slice x43, local copies, waits for them, and re-layouts, update_at(): return lax.dynamic_update_index_in_dim(target, block, index, 0)  18 us
  transfers between devices with their start and end apart: 96, of which 47 were waited for; matrix products, arithmetic and copies ran while one was open for 21% of the time, Pallas kernels for 0%

profile of v1, /device:TPU:0, one launch (start us, length us, event | category | flops | bytes accessed | tf_op | source)
XLA Modules:
  0.0 783.3 jit_solution(1693122502925988908)
XLA Ops:
  33.3 6.3 collective-permute-done.1
  52.0 9.1 %collective-permute-start.37 = (bf16[96,1152]{1,0:T(8,128)(2,1)S(1)}, bf16[96,1152]{1,0:T(8,128)(2,1)S(1)}, u32[]{:S(2)}, u32[]{:S(2)}) collective-permute-start(bf16[96,1152]{1,0:T(8,128)(2,1)S(1)} %copy-done.68), channel_id=1, source_target_pairs={{0,2},{2,4},{4,6},{6,0},{1,3},{3,5},{5,7},{7,1},{8,10},{10,12},{12... | collective-permute-start | bytes 663560 | tf_op jit(solution)/shard_map/ppermute | solution.py:107
  63.3 6.0 collective-permute-start.39
  70.2 9.8 %collective-permute-start.12 = (bf16[96,768]{1,0:T(8,128)(2,1)}, bf16[96,768]{1,0:T(8,128)(2,1)S(1)}, u32[]{:S(2)}, u32[]{:S(2)}) collective-permute-start(bf16[96,768]{1,0:T(8,128)(2,1)} %collective-permute-done.11), channel_id=1, source_target_pairs={{0,2},{2,4},{4,6},{6,0},{1,3},{3,5},{5,7},{7,1},{8,10},{10,12},{12... | collective-permute-start | bytes 442376 | tf_op jit(solution)/shard_map/ppermute | solution.py:107
  112.4 6.6 collective-permute-done.3
  161.1 56.6 %collective-permute-done.15 = bf16[2,192,768]{2,1,0:T(8,128)(2,1)S(1)} collective-permute-done((bf16[2,192,768]{2,1,0:T(8,128)(2,1)S(1)}, bf16[2,192,768]{2,1,0:T(8,128)(2,1)S(1)}, u32[]{:S(2)}, u32[]{:S(2)}) %collective-permute-start.15) | collective-permute-done | bytes 589856 | tf_op jit(solution)/shard_map/ppermute | solution.py:111
  232.5 48.9 %collective-permute-done.7 = bf16[2,192,1024]{2,1,0:T(8,128)(2,1)S(1)} collective-permute-done((bf16[2,192,1024]{2,1,0:T(8,128)(2,1)S(1)}, bf16[2,192,1024]{2,1,0:T(8,128)(2,1)S(1)}, u32[]{:S(2)}, u32[]{:S(2)}) %collective-permute-start.7) | collective-permute-done | bytes 786464 | tf_op jit(solution)/shard_map/ppermute | solution.py:111
  324.8 8.1 %collective-permute-done.19 = bf16[2,64,1536]{2,1,0:T(8,128)(2,1)} collective-permute-done((bf16[2,64,1536]{2,1,0:T(8,128)(2,1)S(1)}, bf16[2,64,1536]{2,1,0:T(8,128)(2,1)}, u32[]{:S(2)}, u32[]{:S(2)}) %collective-permute-start.19) | collective-permute-done | bytes 393248 | tf_op jit(solution)/shard_map/ppermute | solution.py:107
  334.3 11.3 %collective-permute-done.20 = bf16[2,64,1536]{2,1,0:T(8,128)(2,1)S(1)} collective-permute-done((bf16[2,64,1536]{2,1,0:T(8,128)(2,1)}, bf16[2,64,1536]{2,1,0:T(8,128)(2,1)S(1)}, u32[]{:S(2)}, u32[]{:S(2)}) %collective-permute-start.20) | collective-permute-done | bytes 393248 | tf_op jit(solution)/shard_map/ppermute | solution.py:107
  348.3 8.9 %collective-permute-done.21 = bf16[2,64,1536]{2,1,0:T(8,128)(2,1)S(1)} collective-permute-done((bf16[2,64,1536]{2,1,0:T(8,128)(2,1)S(1)}, bf16[2,64,1536]{2,1,0:T(8,128)(2,1)S(1)}, u32[]{:S(2)}, u32[]{:S(2)}) %collective-permute-start.21) | collective-permute-done | bytes 393248 | tf_op jit(solution)/shard_map/ppermute | solution.py:107
  358.4 6.2 fusion.143
  368.8 6.2 fusion.141
  375.0 9.6 %multiply_convert_fusion.1 = (bf16[1024,1152]{1,0:T(8,128)(2,1)}, bf16[1024,1152]{1,0:T(8,128)(2,1)}, bf16[1024,1152]{1,0:T(8,128)(2,1)}) fusion(f32[1024,1152]{1,0:T(8,128)S(1)} %fusion.143, f32[1024,1152]{1,0:T(8,128)} %fusion.141, bf16[1024,1536]{1,0:T(8,128)(2,1)S(1)} %constant_dynamic-update-slice_fusion, bf16[1536,1152]{1,0:T(8,128)(2,1)S(1)} %bitcast.804), kind=kOutput, calls=%fused_computation.1 | convolution fusion | flops 3642753024 | bytes 23199744 | tf_op jit(solution)/shard_map/dot_general | solution.py:324
  384.7 8.1 %fusion.144 = f32[1024,1536]{1,0:T(8,128)} fusion(bf16[1024,1152]{1,0:T(8,128)(2,1)} %get-tuple-element.38, bf16[1536,1152]{1,0:T(8,128)(2,1)S(1)} %bitcast.807), kind=kOutput, calls=%fused_computation.462 | convolution fusion | flops 3623878656 | bytes 12189696 | tf_op jit(solution)/shard_map/rf,df->rd/dot_general | solution.py:86
  397.2 6.4 fusion.148
  403.6 8.5 %fusion.142 = f32[1024,1536]{1,0:T(8,128)} fusion(bf16[1024,1152]{1,0:T(8,128)(2,1)S(1)} %copy-done.100, bf16[1536,1152]{1,0:T(8,128)(2,1)} %bitcast.151), kind=kOutput, calls=%fused_computation.460 | convolution fusion | flops 3623878656 | bytes 12189696 | tf_op jit(solution)/shard_map/rf,df->rd/dot_general | solution.py:86
  412.1 6.3 fusion.146
  418.3 6.4 convolution_add_fusion
  444.6 5.9 collective-permute-done.82
  456.7 12.9 %collective-permute-done.89 = bf16[2,192,1152]{2,1,0:T(8,128)(2,1)} collective-permute-done((bf16[2,192,1152]{2,1,0:T(8,128)(2,1)}, bf16[2,192,1152]{2,1,0:T(8,128)(2,1)}, u32[]{:S(2)}, u32[]{:S(2)}) %collective-permute-start.89) | collective-permute-done | bytes 884768 | tf_op jit(solution)/shard_map/ppermute | solution.py:111
  473.4 14.6 %collective-permute-done.75 = bf16[2,192,1152]{2,1,0:T(8,128)(2,1)S(1)} collective-permute-done((bf16[2,192,1152]{2,1,0:T(8,128)(2,1)S(1)}, bf16[2,192,1152]{2,1,0:T(8,128)(2,1)S(1)}, u32[]{:S(2)}, u32[]{:S(2)}) %collective-permute-start.75) | collective-permute-done | bytes 884768 | tf_op jit(solution)/shard_map/ppermute | solution.py:111
  492.4 7.7 collective-permute-done.83
  503.2 6.4 collective-permute-done.90
  511.2 7.1 collective-permute-done.76
  522.8 10.8 %collective-permute-done.87 = bf16[96,1152]{1,0:T(8,128)(2,1)S(1)} collective-permute-done((bf16[96,1152]{1,0:T(8,128)(2,1)S(1)}, bf16[96,1152]{1,0:T(8,128)(2,1)S(1)}, u32[]{:S(2)}, u32[]{:S(2)}) %collective-permute-start.87) | collective-permute-done | bytes 221216 | tf_op jit(solution)/shard_map/ppermute | solution.py:107
  538.0 9.7 %collective-permute-done.94 = bf16[96,1152]{1,0:T(8,128)(2,1)S(1)} collective-permute-done((bf16[96,1152]{1,0:T(8,128)(2,1)S(1)}, bf16[96,1152]{1,0:T(8,128)(2,1)S(1)}, u32[]{:S(2)}, u32[]{:S(2)}) %collective-permute-start.94) | collective-permute-done | bytes 221216 | tf_op jit(solution)/shard_map/ppermute | solution.py:107
  562.2 7.4 collective-permute-done.80
  579.7 7.3 collective-permute-done.53
  589.6 5.8 collective-permute-done.45
  666.4 6.6 collective-permute-done.59
  693.7 46.9 %all-reduce.3 = (f32[1536]{0:T(1024)}, f32[256]{0:T(256)}, f32[256]{0:T(256)}, f32[1536]{0:T(1024)}, f32[1536]{0:T(1024)}) all-reduce(f32[1536]{0:T(1024)S(1)} %bitcast_dynamic-update-slice_fusion.66, f32[256]{0:T(256)S(1)} %dynamic_update_slice.304, ...), channel_id=1, replica_groups=mesh['dp'=4,'ctx'=4,'tensor'=2] {'dp','ctx','tensor'}, use_global_device_ids=true, to_apply=%region_9.10 | all-reduce | flops 5120 | bytes 40960 | tf_op jit(solution)/shard_map/psum | solution.py:407
  760.1 6.1 collective-permute-done.65
  (697 shorter events, 394.7 us)
Async XLA Ops:
  3.4 39.7 %collective-permute-start.23 = (bf16[96,1152]{1,0:T(8,128)(2,1)}, bf16[96,1152]{1,0:T(8,128)(2,1)}, u32[]{:S(2)}, u32[]{:S(2)}) collective-permute-start(bf16[96,1152]{1,0:T(8,128)(2,1)} %get-tuple-element.83), channel_id=1, source_target_pairs={{0,2},{2,4},{4,6},{6,0},{1,3},{3,5},{5,7},{7,1},{8,10},{10,12},{12... | collective-permute-start | bytes 663560 | tf_op jit(solution)/shard_map/ppermute | solution.py:107
  6.5 39.5 %collective-permute-start.24 = (bf16[96,1152]{1,0:T(8,128)(2,1)}, bf16[96,1152]{1,0:T(8,128)(2,1)}, u32[]{:S(2)}, u32[]{:S(2)}) collective-permute-start(bf16[96,1152]{1,0:T(8,128)(2,1)} %get-tuple-element.82), channel_id=1, source_target_pairs={{0,4},{2,6},{4,0},{6,2},{1,5},{3,7},{5,1},{7,3},{8,12},{10,14},{12... | collective-permute-start | bytes 663560 | tf_op jit(solution)/shard_map/ppermute | solution.py:107
  9.1 40.9 %collective-permute-start.25 = (bf16[96,1152]{1,0:T(8,128)(2,1)}, bf16[96,1152]{1,0:T(8,128)(2,1)}, u32[]{:S(2)}, u32[]{:S(2)}) collective-permute-start(bf16[96,1152]{1,0:T(8,128)(2,1)} %get-tuple-element.81), channel_id=1, source_target_pairs={{0,6},{2,0},{4,2},{6,4},{1,7},{3,1},{5,3},{7,5},{8,14},{10,8},{12,... | collective-permute-start | bytes 663560 | tf_op jit(solution)/shard_map/ppermute | solution.py:107
  11.8 90.0 %collective-permute-start.48 = (bf16[2,64,1536]{2,1,0:T(8,128)(2,1)S(1)}, bf16[2,64,1536]{2,1,0:T(8,128)(2,1)}, u32[]{:S(2)}, u32[]{:S(2)}) collective-permute-start(bf16[2,64,1536]{2,1,0:T(8,128)(2,1)S(1)} %copy-done.14), channel_id=1, source_target_pairs={{0,2},{2,4},{4,6},{6,0},{1,3},{3,5},{5,7},{7,1},{8,10},{10,12},{12... | collective-permute-start | bytes 1179656 | tf_op jit(solution)/shard_map/ppermute | solution.py:107
  50.0 48.0 %collective-permute-start = (bf16[2,64,1536]{2,1,0:T(8,128)(2,1)S(1)}, bf16[2,64,1536]{2,1,0:T(8,128)(2,1)S(1)}, u32[]{:S(2)}, u32[]{:S(2)}) collective-permute-start(bf16[2,64,1536]{2,1,0:T(8,128)(2,1)S(1)} %copy-done.56), channel_id=1, source_target_pairs={{0,1},{1,0},{2,3},{3,2},{4,5},{5,4},{6,7},{7,6},{8,9},{9,8},{10,11... | collective-permute-start | bytes 1179656 | tf_op jit(solution)/shard_map/ppermute | solution.py:102
  85.4 35.5 %collective-permute-start.26 = (bf16[192,1152]{1,0:T(8,128)(2,1)}, bf16[192,1152]{1,0:T(8,128)(2,1)}, u32[]{:S(2)}, u32[]{:S(2)}) collective-permute-start(bf16[192,1152]{1,0:T(8,128)(2,1)} %bitcast.89), channel_id=1, source_target_pairs={{0,8},{8,0},{16,24},{24,16},{1,9},{9,1},{17,25},{25,17},{2,10},{10... | collective-permute-start | bytes 1327112 | tf_op jit(solution)/shard_map/ppermute | solution.py:111
  96.3 39.0 %collective-permute-start.28 = (bf16[192,1152]{1,0:T(8,128)(2,1)}, bf16[192,1152]{1,0:T(8,128)(2,1)}, u32[]{:S(2)}, u32[]{:S(2)}) collective-permute-start(bf16[192,1152]{1,0:T(8,128)(2,1)} %bitcast.96), channel_id=1, source_target_pairs={{0,16},{8,24},{16,0},{24,8},{1,17},{9,25},{17,1},{25,9},{2,18},{10... | collective-permute-start | bytes 1327112 | tf_op jit(solution)/shard_map/ppermute | solution.py:111
  101.8 36.0 %collective-permute-start.35 = (bf16[192,1152]{1,0:T(8,128)(2,1)}, bf16[192,1152]{1,0:T(8,128)(2,1)S(1)}, u32[]{:S(2)}, u32[]{:S(2)}) collective-permute-start(bf16[192,1152]{1,0:T(8,128)(2,1)} %bitcast.825), channel_id=1, source_target_pairs={{0,16},{8,24},{16,0},{24,8},{1,17},{9,25},{17,1},{25,9},{2,18},{10... | collective-permute-start | bytes 1327112 | tf_op jit(solution)/shard_map/ppermute | solution.py:111
  140.2 79.7 %collective-permute-start.27 = (bf16[2,192,1152]{2,1,0:T(8,128)(2,1)S(1)}, bf16[2,192,1152]{2,1,0:T(8,128)(2,1)S(1)}, u32[]{:S(2)}, u32[]{:S(2)}) collective-permute-start(bf16[2,192,1152]{2,1,0:T(8,128)(2,1)S(1)} %bitcast_dynamic-update-slice_fusion.30), channel_id=1, source_target_pairs={{0,16},{8,24},{16,0},{24,8},{1,17},{9,25},{17,1},{25,9},{2,18},{10... | collective-permute-start | bytes 2654216 | tf_op jit(solution)/shard_map/ppermute | solution.py:111
  145.3 75.0 %collective-permute-start.34 = (bf16[2,192,1152]{2,1,0:T(8,128)(2,1)S(1)}, bf16[2,192,1152]{2,1,0:T(8,128)(2,1)S(1)}, u32[]{:S(2)}, u32[]{:S(2)}) collective-permute-start(bf16[2,192,1152]{2,1,0:T(8,128)(2,1)S(1)} %bitcast_dynamic-update-slice_fusion.26), channel_id=1, source_target_pairs={{0,16},{8,24},{16,0},{24,8},{1,17},{9,25},{17,1},{25,9},{2,18},{10... | collective-permute-start | bytes 2654216 | tf_op jit(solution)/shard_map/ppermute | solution.py:111
  146.8 76.9 %collective-permute-start.41 = (bf16[2,192,1152]{2,1,0:T(8,128)(2,1)S(1)}, bf16[2,192,1152]{2,1,0:T(8,128)(2,1)S(1)}, u32[]{:S(2)}, u32[]{:S(2)}) collective-permute-start(bf16[2,192,1152]{2,1,0:T(8,128)(2,1)S(1)} %bitcast_dynamic-update-slice_fusion.22), channel_id=1, source_target_pairs={{0,16},{8,24},{16,0},{24,8},{1,17},{9,25},{17,1},{25,9},{2,18},{10... | collective-permute-start | bytes 2654216 | tf_op jit(solution)/shard_map/ppermute | solution.py:111
  153.7 64.0 %collective-permute-start.15 = (bf16[2,192,768]{2,1,0:T(8,128)(2,1)S(1)}, bf16[2,192,768]{2,1,0:T(8,128)(2,1)S(1)}, u32[]{:S(2)}, u32[]{:S(2)}) collective-permute-start(bf16[2,192,768]{2,1,0:T(8,128)(2,1)S(1)} %bitcast_dynamic-update-slice_fusion.38), channel_id=1, source_target_pairs={{0,16},{8,24},{16,0},{24,8},{1,17},{9,25},{17,1},{25,9},{2,18},{10... | collective-permute-start | bytes 1769480 | tf_op jit(solution)/shard_map/ppermute | solution.py:111
  157.9 59.8 %collective-permute-start.17 = (bf16[2,192,768]{2,1,0:T(8,128)(2,1)S(1)}, bf16[2,192,768]{2,1,0:T(8,128)(2,1)S(1)}, u32[]{:S(2)}, u32[]{:S(2)}) collective-permute-start(bf16[2,192,768]{2,1,0:T(8,128)(2,1)S(1)} %bitcast_dynamic-update-slice_fusion.36), channel_id=1, source_target_pairs={{0,8},{8,0},{16,24},{24,16},{1,9},{9,1},{17,25},{25,17},{2,10},{10... | collective-permute-start | bytes 1769480 | tf_op jit(solution)/shard_map/ppermute | solution.py:111
  217.6 70.1 %collective-permute-start.29 = (bf16[2,192,1152]{2,1,0:T(8,128)(2,1)S(1)}, bf16[2,192,1152]{2,1,0:T(8,128)(2,1)S(1)}, u32[]{:S(2)}, u32[]{:S(2)}) collective-permute-start(bf16[2,192,1152]{2,1,0:T(8,128)(2,1)S(1)} %bitcast_dynamic-update-slice_fusion.28), channel_id=1, source_target_pairs={{0,8},{8,0},{16,24},{24,16},{1,9},{9,1},{17,25},{25,17},{2,10},{10... | collective-permute-start | bytes 2654216 | tf_op jit(solution)/shard_map/ppermute | solution.py:111
  217.8 98.1 %collective-permute-start.36 = (bf16[2,192,1152]{2,1,0:T(8,128)(2,1)}, bf16[2,192,1152]{2,1,0:T(8,128)(2,1)}, u32[]{:S(2)}, u32[]{:S(2)}) collective-permute-start(bf16[2,192,1152]{2,1,0:T(8,128)(2,1)} %bitcast_dynamic-update-slice_fusion.24), channel_id=1, source_target_pairs={{0,8},{8,0},{16,24},{24,16},{1,9},{9,1},{17,25},{25,17},{2,10},{10... | collective-permute-start | bytes 2654216 | tf_op jit(solution)/shard_map/ppermute | solution.py:111
  219.9 99.5 %collective-permute-start.43 = (bf16[2,192,1152]{2,1,0:T(8,128)(2,1)}, bf16[2,192,1152]{2,1,0:T(8,128)(2,1)}, u32[]{:S(2)}, u32[]{:S(2)}) collective-permute-start(bf16[2,192,1152]{2,1,0:T(8,128)(2,1)} %bitcast_dynamic-update-slice_fusion.20), channel_id=1, source_target_pairs={{0,8},{8,0},{16,24},{24,16},{1,9},{9,1},{17,25},{25,17},{2,10},{10... | collective-permute-start | bytes 2654216 | tf_op jit(solution)/shard_map/ppermute | solution.py:111
  223.7 57.8 %collective-permute-start.7 = (bf16[2,192,1024]{2,1,0:T(8,128)(2,1)S(1)}, bf16[2,192,1024]{2,1,0:T(8,128)(2,1)S(1)}, u32[]{:S(2)}, u32[]{:S(2)}) collective-permute-start(bf16[2,192,1024]{2,1,0:T(8,128)(2,1)S(1)} %bitcast_dynamic-update-slice_fusion.32), channel_id=1, source_target_pairs={{0,8},{8,0},{16,24},{24,16},{1,9},{9,1},{17,25},{25,17},{2,10},{10... | collective-permute-start | bytes 2359304 | tf_op jit(solution)/shard_map/ppermute | solution.py:111
  232.3 113.3 %collective-permute-start.51 = (bf16[512,1536]{1,0:T(8,128)(2,1)}, bf16[512,1536]{1,0:T(8,128)(2,1)}, u32[]{:S(2)}, u32[]{:S(2)}) collective-permute-start(bf16[512,1536]{1,0:T(8,128)(2,1)} %pad_maximum_fusion.1), channel_id=1, source_target_pairs={{0,1},{1,0},{2,3},{3,2},{4,5},{5,4},{6,7},{7,6},{8,9},{9,8},{10,11... | collective-permute-start | bytes 4718600 | tf_op jit(solution)/shard_map/ppermute | solution.py:102
  424.9 146.1 %collective-permute-start.52 = (bf16[512,1536]{1,0:T(8,128)(2,1)S(1)}, bf16[512,1536]{1,0:T(8,128)(2,1)}, u32[]{:S(2)}, u32[]{:S(2)}) collective-permute-start(bf16[512,1536]{1,0:T(8,128)(2,1)S(1)} %slice.668), channel_id=1, source_target_pairs={{0,1},{1,0},{2,3},{3,2},{4,5},{5,4},{6,7},{7,6},{8,9},{9,8},{10,11... | collective-permute-start | bytes 4718600 | tf_op jit(solution)/shard_map/ppermute | solution.py:102
  436.1 33.5 %collective-permute-start.89 = (bf16[2,192,1152]{2,1,0:T(8,128)(2,1)}, bf16[2,192,1152]{2,1,0:T(8,128)(2,1)}, u32[]{:S(2)}, u32[]{:S(2)}) collective-permute-start(bf16[2,192,1152]{2,1,0:T(8,128)(2,1)} %fusion.19), channel_id=1, source_target_pairs={{0,8},{8,0},{16,24},{24,16},{1,9},{9,1},{17,25},{25,17},{2,10},{10... | collective-permute-start | bytes 2654216 | tf_op jit(solution)/shard_map/ppermute | solution.py:111
  438.2 33.5 %collective-permute-start.91 = (bf16[2,192,1152]{2,1,0:T(8,128)(2,1)}, bf16[2,192,1152]{2,1,0:T(8,128)(2,1)S(1)}, u32[]{:S(2)}, u32[]{:S(2)}) collective-permute-start(bf16[2,192,1152]{2,1,0:T(8,128)(2,1)} %fusion.16), channel_id=1, source_target_pairs={{0,16},{8,24},{16,0},{24,8},{1,17},{9,25},{17,1},{25,9},{2,18},{10... | collective-permute-start | bytes 2654216 | tf_op jit(solution)/shard_map/ppermute | solution.py:111
  451.4 36.6 %collective-permute-start.75 = (bf16[2,192,1152]{2,1,0:T(8,128)(2,1)S(1)}, bf16[2,192,1152]{2,1,0:T(8,128)(2,1)S(1)}, u32[]{:S(2)}, u32[]{:S(2)}) collective-permute-start(bf16[2,192,1152]{2,1,0:T(8,128)(2,1)S(1)} %fusion.17), channel_id=1, source_target_pairs={{0,8},{8,0},{16,24},{24,16},{1,9},{9,1},{17,25},{25,17},{2,10},{10... | collective-permute-start | bytes 2654216 | tf_op jit(solution)/shard_map/ppermute | solution.py:111
  453.7 36.9 %collective-permute-start.77 = (bf16[2,192,1152]{2,1,0:T(8,128)(2,1)S(1)}, bf16[2,192,1152]{2,1,0:T(8,128)(2,1)S(1)}, u32[]{:S(2)}, u32[]{:S(2)}) collective-permute-start(bf16[2,192,1152]{2,1,0:T(8,128)(2,1)S(1)} %fusion.14), channel_id=1, source_target_pairs={{0,16},{8,24},{16,0},{24,8},{1,17},{9,25},{17,1},{25,9},{2,18},{10... | collective-permute-start | bytes 2654216 | tf_op jit(solution)/shard_map/ppermute | solution.py:111
  469.6 107.8 %collective-permute-start.44 = (bf16[512,1536]{1,0:T(8,128)(2,1)S(1)}, bf16[512,1536]{1,0:T(8,128)(2,1)}, u32[]{:S(2)}, u32[]{:S(2)}) collective-permute-start(bf16[512,1536]{1,0:T(8,128)(2,1)S(1)} %slice.669), channel_id=1, source_target_pairs={{0,1},{1,0},{2,3},{3,2},{4,5},{5,4},{6,7},{7,6},{8,9},{9,8},{10,11... | collective-permute-start | bytes 4718600 | tf_op jit(solution)/shard_map/ppermute | solution.py:102
  471.6 28.4 %collective-permute-start.83 = (bf16[192,1152]{1,0:T(8,128)(2,1)S(1)}, bf16[192,1152]{1,0:T(8,128)(2,1)S(1)}, u32[]{:S(2)}, u32[]{:S(2)}) collective-permute-start(bf16[192,1152]{1,0:T(8,128)(2,1)S(1)} %fusion.77), channel_id=1, source_target_pairs={{0,16},{8,24},{16,0},{24,8},{1,17},{9,25},{17,1},{25,9},{2,18},{10... | collective-permute-start | bytes 1327112 | tf_op jit(solution)/shard_map/ppermute | solution.py:111
  520.3 31.9 %collective-permute-start.88 = (bf16[96,1152]{1,0:T(8,128)(2,1)S(1)}, bf16[96,1152]{1,0:T(8,128)(2,1)S(1)}, u32[]{:S(2)}, u32[]{:S(2)}) collective-permute-start(bf16[96,1152]{1,0:T(8,128)(2,1)S(1)} %get-tuple-element.61), channel_id=1, source_target_pairs={{0,6},{2,0},{4,2},{6,4},{1,7},{3,1},{5,3},{7,5},{8,14},{10,8},{12,... | collective-permute-start | bytes 663560 | tf_op jit(solution)/shard_map/ppermute | solution.py:107
  646.5 36.7 %collective-permute-start.68 = (bf16[2,192,768]{2,1,0:T(8,128)(2,1)}, bf16[2,192,768]{2,1,0:T(8,128)(2,1)}, u32[]{:S(2)}, u32[]{:S(2)}) collective-permute-start(bf16[2,192,768]{2,1,0:T(8,128)(2,1)} %fusion.63), channel_id=1, source_target_pairs={{0,8},{8,0},{16,24},{24,16},{1,9},{9,1},{17,25},{25,17},{2,10},{10... | collective-permute-start | bytes 1769480 | tf_op jit(solution)/shard_map/ppermute | solution.py:111
  648.5 38.2 %collective-permute-start.70 = (bf16[2,192,768]{2,1,0:T(8,128)(2,1)}, bf16[2,192,768]{2,1,0:T(8,128)(2,1)}, u32[]{:S(2)}, u32[]{:S(2)}) collective-permute-start(bf16[2,192,768]{2,1,0:T(8,128)(2,1)} %fusion.62), channel_id=1, source_target_pairs={{0,16},{8,24},{16,0},{24,8},{1,17},{9,25},{17,1},{25,9},{2,18},{10... | collective-permute-start | bytes 1769480 | tf_op jit(solution)/shard_map/ppermute | solution.py:111
  680.2 62.9 %collective-permute-start.61 = (bf16[2,192,1024]{2,1,0:T(8,128)(2,1)}, bf16[2,192,1024]{2,1,0:T(8,128)(2,1)}, u32[]{:S(2)}, u32[]{:S(2)}) collective-permute-start(bf16[2,192,1024]{2,1,0:T(8,128)(2,1)} %fusion.34), channel_id=1, source_target_pairs={{0,8},{8,0},{16,24},{24,16},{1,9},{9,1},{17,25},{25,17},{2,10},{10... | collective-permute-start | bytes 2359304 | tf_op jit(solution)/shard_map/ppermute | solution.py:111
  682.1 65.5 %collective-permute-start.63 = (bf16[2,192,1024]{2,1,0:T(8,128)(2,1)}, bf16[2,192,1024]{2,1,0:T(8,128)(2,1)}, u32[]{:S(2)}, u32[]{:S(2)}) collective-permute-start(bf16[2,192,1024]{2,1,0:T(8,128)(2,1)} %fusion.33), channel_id=1, source_target_pairs={{0,16},{8,24},{16,0},{24,8},{1,17},{9,25},{17,1},{25,9},{2,18},{10... | collective-permute-start | bytes 2359304 | tf_op jit(solution)/shard_map/ppermute | solution.py:111
  685.1 55.5 %collective-permute-start.69 = (bf16[192,768]{1,0:T(8,128)(2,1)S(1)}, bf16[192,768]{1,0:T(8,128)(2,1)}, u32[]{:S(2)}, u32[]{:S(2)}) collective-permute-start(bf16[192,768]{1,0:T(8,128)(2,1)S(1)} %fusion.91), channel_id=1, source_target_pairs={{0,16},{8,24},{16,0},{24,8},{1,17},{9,25},{17,1},{25,9},{2,18},{10... | collective-permute-start | bytes 884744 | tf_op jit(solution)/shard_map/ppermute | solution.py:111
  688.8 53.0 %collective-permute-start.71 = (bf16[192,768]{1,0:T(8,128)(2,1)}, bf16[192,768]{1,0:T(8,128)(2,1)}, u32[]{:S(2)}, u32[]{:S(2)}) collective-permute-start(bf16[192,768]{1,0:T(8,128)(2,1)} %fusion.92), channel_id=1, source_target_pairs={{0,8},{8,0},{16,24},{24,16},{1,9},{9,1},{17,25},{25,17},{2,10},{10... | collective-permute-start | bytes 884744 | tf_op jit(solution)/shard_map/ppermute | solution.py:111
  (170 other events, 2180.6 us)

commit v2 on v1

v2 whole, which is shorter than its diff:
```python
import functools

import jax
import jax.numpy as jnp
from jax import lax
from jax.experimental import pallas as pl
from jax.experimental.pallas import tpu as pltpu
from jax.sharding import PartitionSpec as P

HD = 128


epsilon = 1e-06
rope_base = 1000000.0


def inverse_root(value):
    return lax.rsqrt(jnp.mean(value * value, axis=-1, keepdims=True) + epsilon)


def rotary_tables(positions):
    half_dim = HD // 2
    frequency = rope_base ** (-2.0 * jnp.arange(half_dim, dtype=jnp.float32) / HD)
    angles = positions.astype(jnp.float32)[:, None] * frequency[None, :]
    angles = jnp.concatenate([angles, angles], axis=1)
    return (jnp.cos(angles)[:, None, :], jnp.sin(angles)[:, None, :])


VMEM_LIMIT = 44 * 1024 * 1024


def params():
    return pltpu.CompilerParams(vmem_limit_bytes=VMEM_LIMIT)


def cost(flops, arrays):
    moved = sum(a.size * a.dtype.itemsize for a in arrays)
    return pl.CostEstimate(flops=flops, bytes_accessed=moved, transcendentals=0)


def contract(left, right, dims):
    return lax.dot_general(left, right, (dims, ((), ())), preferred_element_type=jnp.float32)


def half_sign(shape):
    return jnp.where(lax.broadcasted_iota(jnp.int32, shape, 1) < shape[1] // 2, 1.0, -1.0)


def qkv_kernel(rope_heads, x_ref, w_ref, b_ref, cos_ref, sin_ref, out_ref):
    at = pl.program_id(0)
    heads = w_ref.shape[1] // HD
    total = contract(x_ref[...], w_ref[...], ((1,), (0,))) + b_ref[...]
    cosine, sine = cos_ref[...], sin_ref[...]
    signed = -half_sign(sine.shape) * sine
    for head in range(heads):
        value = total[:, head * HD : (head + 1) * HD]
        turned = value * cosine + pltpu.roll(value, HD // 2, 1) * signed
        kept = jnp.where(at * heads + head < rope_heads, turned, value)
        out_ref[:, head * HD : (head + 1) * HD] = kept.astype(out_ref.dtype)


def qkv_heads(x, weight, bias, cosine, sine, rope_heads):
    rows, columns = x.shape[0], weight.shape[1]
    out = jax.ShapeDtypeStruct((rows, columns), jnp.bfloat16)
    whole = lambda a: pl.BlockSpec(a.shape, lambda i: (0, 0))
    return pl.pallas_call(
        functools.partial(qkv_kernel, rope_heads),
        out_shape=out,
        grid=(columns // 256,),
        in_specs=[
            whole(x),
            pl.BlockSpec((weight.shape[0], 256), lambda i: (0, i)),
            pl.BlockSpec((1, 256), lambda i: (0, i)),
            whole(cosine),
            whole(sine),
        ],
        out_specs=pl.BlockSpec((rows, 256), lambda i: (0, i)),
        compiler_params=params(),
        cost_estimate=cost(2 * x.size * columns, [x, weight, out]),
        name="qkv_heads",
    )(x, weight, bias, cosine, sine)


def probabilities_of(query, keys, allowed):
    scores = contract(query, keys, ((1,), (1,))) * HD ** (-0.5)
    scores = jnp.where(allowed, scores, -1e30)
    weights = jnp.exp(scores - jnp.max(scores, axis=-1, keepdims=True))
    return weights / jnp.sum(weights, axis=-1, keepdims=True)


def allowed_of(prefix_ref, row_ref, key_ref):
    keys = key_ref[...]
    return (keys <= row_ref[...]) | (keys < prefix_ref[pl.program_id(0)])


def attend_kernel(prefix_ref, row_ref, key_ref, q_ref, kv_ref, out_ref):
    allowed = allowed_of(prefix_ref, row_ref, key_ref)
    keys, values = kv_ref[0, :, :HD], kv_ref[0, :, HD:]
    for head in range(q_ref.shape[1] // HD):
        columns = slice(head * HD, (head + 1) * HD)
        chances = probabilities_of(q_ref[:, columns], keys, allowed).astype(jnp.bfloat16)
        out_ref[:, columns] = contract(chances, values, ((1,), (0,))).astype(out_ref.dtype)


def attend_back_kernel(
    prefix_ref, row_ref, key_ref, q_ref, kv_ref, grad_ref, cos_ref, sin_ref, dq_ref, dkv_ref
):
    allowed = allowed_of(prefix_ref, row_ref, key_ref)
    keys, values = kv_ref[0, :, :HD], kv_ref[0, :, HD:]
    sign = half_sign(cos_ref.shape)
    scale = HD ** (-0.5)
    grad_keys = jnp.zeros(keys.shape, jnp.float32)
    grad_values = jnp.zeros(keys.shape, jnp.float32)
    for head in range(q_ref.shape[1] // HD):
        columns = slice(head * HD, (head + 1) * HD)
        query, grad = q_ref[:, columns], grad_ref[:, columns]
        chances = probabilities_of(query, keys, allowed)
        rounded = chances.astype(jnp.bfloat16)
        grad_chances = contract(grad, values, ((1,), (1,)))
        offset = jnp.sum(rounded.astype(jnp.float32) * grad_chances, axis=-1, keepdims=True)
        grad_scores = (chances * (grad_chances - offset)).astype(jnp.bfloat16)
        turned = contract(grad_scores, keys, ((1,), (0,))) * scale
        back = turned * cos_ref[...] + pltpu.roll(turned * sin_ref[...], HD // 2, 1) * sign
        dq_ref[:, columns] = back.astype(dq_ref.dtype)
        grad_keys += contract(grad_scores, query, ((0,), (0,)))
        grad_values += contract(rounded, grad, ((0,), (0,)))
    dkv_ref[0, :, :HD] = (grad_keys * scale).astype(dkv_ref.dtype)
    dkv_ref[0, :, HD:] = grad_values.astype(dkv_ref.dtype)


def attention_specs(query, kv, row_pos, key_pos):
    rows = query.shape[0] // kv.shape[0]
    heads = pl.BlockSpec((rows, query.shape[1]), lambda i: (i, 0))
    both = pl.BlockSpec((1,) + kv.shape[1:], lambda i: (i, 0, 0))
    return heads, [
        pl.BlockSpec(memory_space=pltpu.SMEM),
        pl.BlockSpec(row_pos.shape, lambda i: (0, 0)),
        pl.BlockSpec(key_pos.shape, lambda i: (0, 0)),
        heads,
        both,
    ], both


def attend(prefix, row_pos, key_pos, query, kv):
    heads, specs, _ = attention_specs(query, kv, row_pos, key_pos)
    return pl.pallas_call(
        attend_kernel,
        out_shape=jax.ShapeDtypeStruct(query.shape, jnp.bfloat16),
        grid=(kv.shape[0],),
        in_specs=specs,
        out_specs=heads,
        compiler_params=params(),
        cost_estimate=cost(4 * query.size * kv.shape[1], [query, kv, query]),
        name="attend",
    )(prefix, row_pos, key_pos, query, kv)


def attend_back(prefix, row_pos, key_pos, query, kv, grad, cosine, sine):
    heads, specs, both = attention_specs(query, kv, row_pos, key_pos)
    table = pl.BlockSpec(cosine.shape, lambda i: (0, 0))
    return pl.pallas_call(
        attend_back_kernel,
        out_shape=(
            jax.ShapeDtypeStruct(query.shape, jnp.bfloat16),
            jax.ShapeDtypeStruct(kv.shape, jnp.bfloat16),
        ),
        grid=(kv.shape[0],),
        in_specs=specs + [heads, table, table],
        out_specs=(heads, both),
        compiler_params=params(),
        cost_estimate=cost(10 * query.size * kv.shape[1], [query, kv, grad, query, kv]),
        name="attend_back",
    )(prefix, row_pos, key_pos, query, kv, grad, cosine, sine)


STEP = 384
ROWS = 1024


def whole_block(array):
    return pl.BlockSpec(array.shape, lambda i: (0, 0))


def column_block(array, columns):
    return pl.BlockSpec((array.shape[0], columns), lambda i: (0, i))


def row_block(array, rows):
    return pl.BlockSpec((rows, array.shape[1]), lambda i: (i, 0))


def hidden_kernel(x_ref, gate_ref, up_ref, act_ref, silu_ref, slope_ref):
    x = x_ref[...]
    gate = contract(x, gate_ref[...], ((1,), (0,)))
    up = contract(x, up_ref[...], ((1,), (0,)))
    sigmoid = jax.nn.sigmoid(gate)
    silu = gate * sigmoid
    act_ref[...] = (silu * up).astype(act_ref.dtype)
    silu_ref[...] = silu.astype(silu_ref.dtype)
    slope_ref[...] = (up * sigmoid * (1.0 + gate * (1.0 - sigmoid))).astype(slope_ref.dtype)


def row_tile(array):
    return pl.BlockSpec((ROWS, array.shape[1]), lambda i, j: (i, 0))


def both_tile():
    return pl.BlockSpec((ROWS, STEP), lambda i, j: (i, j))


def column_tile(array, offset=0):
    return pl.BlockSpec((array.shape[0], STEP), lambda i, j: (0, j + offset))


def hidden_units(x, pair):
    rows, hidden = x.shape[0], pair.shape[1] // 2
    out = jax.ShapeDtypeStruct((rows, hidden), jnp.bfloat16)
    return pl.pallas_call(
        hidden_kernel,
        out_shape=(out, out, out),
        grid=(rows // ROWS, hidden // STEP),
        in_specs=[row_tile(x), column_tile(pair), column_tile(pair, hidden // STEP)],
        out_specs=(both_tile(),) * 3,
        compiler_params=params(),
        cost_estimate=cost(2 * rows * pair.size, [x, pair, out, out, out]),
        name="hidden_units",
    )(x, pair, pair)


def hidden_back_kernel(
    dy_ref, silu_ref, slope_ref, down_ref, gate_ref, up_ref, dgate_ref, dup_ref, dx_ref, total_ref
):
    grad = contract(dy_ref[...], down_ref[...], ((1,), (0,)))
    dup = (grad * silu_ref[...].astype(jnp.float32)).astype(jnp.bfloat16)
    dgate = (grad * slope_ref[...].astype(jnp.float32)).astype(jnp.bfloat16)
    dup_ref[...] = dup
    dgate_ref[...] = dgate
    both = jnp.concatenate([dgate, dup], axis=1)
    weights = jnp.concatenate([gate_ref[...], up_ref[...]], axis=1)
    at, last = pl.program_id(1), pl.num_programs(1) - 1
    term = contract(both, weights, ((1,), (1,)))

    @pl.when(at == 0)
    def _():
        total_ref[...] = term

    @pl.when((at > 0) & (at < last))
    def _():
        total_ref[...] += term

    @pl.when((at > 0) & (at == last))
    def _():
        dx_ref[...] = (total_ref[...] + term).astype(dx_ref.dtype)

    @pl.when((at == 0) & (at == last))
    def _():
        dx_ref[...] = term.astype(dx_ref.dtype)


def hidden_back(dy, silu, slope, down, pair):
    rows, hidden = silu.shape
    out = jax.ShapeDtypeStruct((rows, hidden), jnp.bfloat16)
    out_x = jax.ShapeDtypeStruct(dy.shape, jnp.bfloat16)
    tile = both_tile()
    return pl.pallas_call(
        hidden_back_kernel,
        out_shape=(out, out, out_x),
        grid=(rows // ROWS, hidden // STEP),
        in_specs=[
            row_tile(dy),
            tile,
            tile,
            column_tile(down),
            column_tile(pair),
            column_tile(pair, hidden // STEP),
        ],
        out_specs=(tile, tile, row_tile(dy)),
        scratch_shapes=[pltpu.VMEM((ROWS, dy.shape[1]), jnp.float32)],
        compiler_params=params(),
        cost_estimate=cost(6 * rows * down.size, [dy, silu, slope, down, pair, out, out, dy]),
        name="hidden_back",
    )(dy, silu, slope, down, pair, pair)


def pair_kernel(left_ref, dgate_ref, dup_ref, act_ref, down_ref, term_ref, out_ref):
    hidden = dgate_ref.shape[1]
    left = left_ref[...]
    term_ref[:, :hidden] = contract(left, dgate_ref[...], ((0,), (0,))).astype(term_ref.dtype)
    term_ref[:, hidden:] = contract(left, dup_ref[...], ((0,), (0,))).astype(term_ref.dtype)
    out_ref[...] = contract(act_ref[...], down_ref[...], ((1,), (1,))).astype(out_ref.dtype)


def pair_terms(left, dgate, dup, act, down):
    rows, columns = left.shape
    hidden = act.shape[1]
    term = jax.ShapeDtypeStruct((columns, 2 * hidden), jnp.bfloat16)
    out = jax.ShapeDtypeStruct((rows, columns), jnp.bfloat16)
    return pl.pallas_call(
        pair_kernel,
        out_shape=(term, out),
        grid=(columns // 512,),
        in_specs=[column_block(left, 512)]
        + [whole_block(a) for a in (dgate, dup, act)]
        + [row_block(down, 512)],
        out_specs=(row_block(term, 512), column_block(out, 512)),
        compiler_params=params(),
        cost_estimate=cost(6 * rows * down.size, [left, dgate, dup, act, down, term, out]),
        name="pair_terms",
    )(left, dgate, dup, act, down)


def weight_kernel(left_ref, *refs):
    left, out_ref = left_ref[...], refs[-1]
    start = 0
    for right_ref in refs[:-1]:
        columns = slice(start, start + right_ref.shape[1])
        out_ref[:, columns] = contract(left, right_ref[...], ((0,), (0,))).astype(out_ref.dtype)
        start = columns.stop


def weight_terms(left, *rights):
    rows, columns = left.shape
    out = jax.ShapeDtypeStruct((columns, sum(r.shape[1] for r in rights)), jnp.bfloat16)
    return pl.pallas_call(
        weight_kernel,
        out_shape=out,
        grid=(columns // 512,),
        in_specs=[column_block(left, 512)] + [whole_block(r) for r in rights],
        out_specs=row_block(out, 512),
        compiler_params=params(),
        cost_estimate=cost(2 * rows * out.size, [left, *rights, out]),
        name="weight_terms",
    )(left, *rights)


def attn_weight_kernel(left_ref, right_ref, left2_ref, right2_ref, out_ref):
    columns = right_ref.shape[1]
    first = contract(left_ref[...], right_ref[...], ((0,), (0,)))
    second = contract(left2_ref[...], right2_ref[...], ((0,), (0,)))
    out_ref[:, :columns] = first.astype(out_ref.dtype)
    out_ref[:, columns:] = second.astype(out_ref.dtype)


def attn_weight_terms(left, right, left2, right2):
    columns = left.shape[1]
    out = jax.ShapeDtypeStruct((columns, right.shape[1] + right2.shape[1]), jnp.bfloat16)
    return pl.pallas_call(
        attn_weight_kernel,
        out_shape=out,
        grid=(columns // 512,),
        in_specs=[
            column_block(left, 512),
            whole_block(right),
            column_block(left2, 512),
            whole_block(right2),
        ],
        out_specs=row_block(out, 512),
        compiler_params=params(),
        cost_estimate=cost(2 * left.shape[0] * out.size, [left, right, left2, right2, out]),
        name="attn_weight_terms",
    )(left, right, left2, right2)


def rotate_back(grad_rows, cosine_table, sine_table):
    half_dim = grad_rows.shape[-1] // 2
    scaled = grad_rows * sine_table
    turned = jnp.concatenate([scaled[..., half_dim:], -scaled[..., :half_dim]], axis=-1)
    return grad_rows * cosine_table + turned


def project_back(left, right):
    return jnp.einsum("rf,df->rd", left, right, preferred_element_type=jnp.float32)


def weight_term(left, right):
    return jnp.einsum("rd,rc->dc", left, right, preferred_element_type=jnp.float32)


def after(value, *earlier):
    return lax.optimization_barrier((value, earlier))[0]


def pick(source, index, axis=0):
    return lax.dynamic_index_in_dim(source, index, axis, keepdims=False)


def swap_tensor(value):
    return lax.ppermute(value, "tensor", [(0, 1), (1, 0)])


def shift_ctx(value, distance=1):
    size = lax.axis_size("ctx")
    return lax.ppermute(value, "ctx", [(i, (i + distance) % size) for i in range(size)])


def swap_x(value):
    return lax.ppermute(value, "dp", [(i, i ^ 1) for i in range(4)])


def swap_y(value):
    return lax.ppermute(value, "dp", [(i, i ^ 2) for i in range(4)])


def ring_blocks(value):
    blocks = [value]
    for _ in range(lax.axis_size("ctx") - 1):
        blocks.append(shift_ctx(blocks[-1]))
    return blocks


def direct_blocks(value):
    return [value] + [shift_ctx(value, d) for d in range(1, lax.axis_size("ctx"))]


def direct_terms(blocks):
    sent = [blocks[j].astype(jnp.bfloat16) for j in range(1, len(blocks))]
    return [blocks[0]] + [shift_ctx(block, -j) for j, block in enumerate(sent, 1)]


def sum_terms(terms):
    total = terms[0].astype(jnp.float32)
    for term in terms[1:]:
        total = total + term.astype(jnp.float32)
    return total


def natural_ctx(blocks):
    size = lax.axis_size("ctx")
    own = lax.axis_index("ctx")
    return jnp.stack([lax.select_n((own - c) % size, *blocks) for c in range(size)])


def spread_ctx(columns):
    size = lax.axis_size("ctx")
    own = lax.axis_index("ctx")
    return [pick(columns, own)] + [
        shift_ctx(pick(columns, (own + distance) % size), distance) for distance in range(1, size)
    ]


def in_order(at, own, other):
    return jnp.stack([jnp.where(at == 0, own, other), jnp.where(at == 0, other, own)])


def gather_near_send(value):
    half = value.shape[0] // 2
    first, second = value[:half], value[half:]
    return first, second, swap_x(first), swap_y(second)


def gather_far_send(first, second, got_x, got_y):
    own = lax.axis_index("dp")
    pair_x = in_order(own % 2, first, got_x)
    pair_y = in_order(own // 2, second, got_y)
    return pair_x, pair_y, swap_y(pair_x), swap_x(pair_y)


def gather_whole(pair_x, pair_y, far_x, far_y):
    own = lax.axis_index("dp")
    full_x = in_order(own // 2, pair_x, far_x)
    full_y = jnp.swapaxes(in_order(own % 2, pair_y, far_y), 0, 1)
    return jnp.stack([full_x, full_y], axis=2).reshape(-1, pair_x.shape[-1])


def add(left, right):
    return (left.astype(jnp.float32) + right.astype(jnp.float32)).astype(jnp.bfloat16)


def scatter_near_send(value):
    rows, columns = value.shape[0] // 4, value.shape[1]
    own = lax.axis_index("dp")
    low, high = own % 2, own // 2
    terms = value.reshape(2, 2, 2, rows // 2, columns)
    first, second = terms[:, :, 0], terms[:, :, 1]
    sent_x, sent_y = pick(first, 1 - low, 1), pick(second, 1 - high, 0)
    return pick(first, low, 1), pick(second, high, 0), swap_x(sent_x), swap_y(sent_y)


def scatter_far_send(kept_x, kept_y, got_x, got_y):
    own = lax.axis_index("dp")
    low, high = own % 2, own // 2
    pair_x, pair_y = add(kept_x, got_x), add(kept_y, got_y)
    far_x, far_y = swap_y(pick(pair_x, 1 - high)), swap_x(pick(pair_y, 1 - low))
    return pick(pair_x, high), pick(pair_y, low), far_x, far_y


def scatter_whole(kept_x, kept_y, far_x, far_y):
    whole = jnp.concatenate([add(kept_x, far_x), add(kept_y, far_y)], axis=0)
    return whole.reshape(lax.axis_size("ctx"), -1, whole.shape[1])


def column_parts(weight, ff_part):
    rows, columns = weight.shape
    size = lax.axis_size("ctx")
    wide = jnp.pad(weight.astype(jnp.bfloat16), ((0, 0), (0, size * ff_part - columns)))
    return jnp.stack([wide[:, c * ff_part : (c + 1) * ff_part] for c in range(size)])


def hidden_grad(parts, columns):
    wide = jnp.concatenate([parts[c] for c in range(parts.shape[0])], axis=1)
    return wide[:, :columns].astype(jnp.float32)


def ctx_terms(parts):
    size = lax.axis_size("ctx")
    own = lax.axis_index("ctx")
    return direct_terms([pick(parts, (own - j) % size) for j in range(size)])


def span_rows(blocks):
    mine = jnp.concatenate([b.reshape(-1, b.shape[-1]) for b in blocks], axis=0)
    return jnp.concatenate([mine, swap_tensor(mine)], axis=0)


def core_sum(term):
    half = term.shape[0] // 2
    other = swap_tensor(term[half:].astype(jnp.bfloat16)).astype(jnp.float32)
    mine = (term[:half].astype(jnp.float32) + other).astype(jnp.bfloat16)
    return list(mine.reshape(lax.axis_size("ctx"), -1, mine.shape[1]))


def sum_everywhere(value):
    for axis in ("tensor", "dp", "ctx"):
        size, bit = lax.axis_size(axis), 1
        while bit < size:
            value = value + lax.ppermute(value, axis, [(i, i ^ bit) for i in range(size)])
            bit *= 2
    return value


def per_device(
    tokens,
    prefix,
    w_query,
    w_key,
    w_value,
    w_out,
    w_gate,
    w_up,
    w_down,
    b_query,
    b_key,
    b_value,
    norm_attn,
    norm_mlp,
    cotangent,
):
    bf16, f32 = jnp.bfloat16, jnp.float32
    seq_dev, own_rows, model_width = tokens.shape
    ctx_size = lax.axis_size("ctx")
    span_len = own_rows * 2
    seq_len = span_len * ctx_size
    row_count = seq_dev * span_len
    q_cols = w_query.shape[1]
    kv_cols = w_key.shape[1]
    ff_cols = w_gate.shape[1]
    ff_part = -(-ff_cols // (128 * ctx_size)) * 128
    kv_heads = kv_cols // HD
    group_size = q_cols // kv_cols
    score_scale = HD ** (-0.5)
    tensor_at = lax.axis_index("tensor")
    ctx_at = lax.axis_index("ctx")
    own_pos = jnp.arange(own_rows, dtype=jnp.int32)
    in_span = jnp.concatenate([tensor_at * own_rows + own_pos, (1 - tensor_at) * own_rows + own_pos])
    local_pos = ctx_at * span_len + in_span
    key_pos = jnp.concatenate(
        [((ctx_at - j) % ctx_size) * span_len + in_span for j in range(ctx_size)]
    )
    row_pos, col_pos = local_pos[:, None], key_pos[None, :]
    cosine_table, sine_table = rotary_tables(local_pos)
    cosine_flat, sine_flat = cosine_table[:, 0], sine_table[:, 0]
    bias_query = lax.dynamic_slice_in_dim(b_query, tensor_at * q_cols, q_cols)
    bias_key = lax.dynamic_slice_in_dim(b_key, tensor_at * kv_cols, kv_cols)
    bias_value = lax.dynamic_slice_in_dim(b_value, tensor_at * kv_cols, kv_cols)
    bias_all = jnp.concatenate([bias_query, bias_key, bias_value])
    cast_qkv = jnp.concatenate([w.astype(bf16) for w in (w_query, w_key, w_value)], axis=1)
    qkv_blocks = direct_blocks(cast_qkv)
    out_blocks = direct_blocks(after(w_out, qkv_blocks).astype(bf16))
    x_own = tokens.astype(f32)
    attn_root = inverse_root(x_own)
    normed_own = (x_own * attn_root * norm_attn).astype(bf16)
    normed1 = jnp.concatenate([normed_own, swap_tensor(normed_own)], axis=1).reshape(
        row_count, model_width
    )
    qkv_near = gather_near_send(natural_ctx(qkv_blocks).reshape(-1, cast_qkv.shape[1]))
    pair_parts = jnp.concatenate([column_parts(w, ff_part) for w in (w_gate, w_up)], axis=2)
    pair_blocks = spread_ctx(after(pair_parts, out_blocks))
    qkv_far = gather_far_send(*qkv_near)
    full_qkv = gather_whole(*qkv_far)
    out_near = gather_near_send(after(natural_ctx(out_blocks).reshape(-1, q_cols), qkv_far))
    qkv = qkv_heads(
        normed1,
        full_qkv,
        bias_all[None],
        jnp.tile(cosine_flat, (seq_dev, 1)),
        jnp.tile(sine_flat, (seq_dev, 1)),
        (q_cols + kv_cols) // HD,
    )
    queries = qkv[:, :q_cols]
    out_far = gather_far_send(*after(out_near, qkv))
    pair_blocks = after(pair_blocks, qkv)
    kv_sent = qkv[:, q_cols:].reshape(seq_dev, span_len, 2 * kv_cols)
    kv_blocks = direct_blocks(after(kv_sent, pair_blocks, out_near))
    pair_mine = natural_ctx(pair_blocks).reshape(-1, 2 * ff_part)
    pair_near = gather_near_send(after(pair_mine, out_far))
    kv_rows = jnp.concatenate(after(kv_blocks, pair_mine), axis=1)
    down_blocks = spread_ctx(after(column_parts(w_down, ff_part), kv_blocks))
    mixed_low = attend(prefix, row_pos, col_pos, queries, kv_rows)
    pair_near = after(pair_near, mixed_low)
    pair_far = gather_far_send(*pair_near)
    full_out = gather_whole(*out_far)
    attn_term = project_back(after(mixed_low, pair_near), full_out)
    attn_term = attn_term.reshape(seq_dev, span_len, model_width)
    hidden1 = (
        x_own
        + attn_term[:, :own_rows]
        + swap_tensor(attn_term[:, own_rows:].astype(bf16)).astype(f32)
    )
    mlp_root = inverse_root(hidden1)
    normed2_own = (hidden1 * mlp_root * norm_mlp).astype(bf16)
    down_blocks = after(down_blocks, normed2_own)
    normed2_blocks = direct_blocks(after(normed2_own, down_blocks))
    down_mine = natural_ctx(down_blocks).reshape(-1, ff_part)
    normed2_blocks, pair_far = after((normed2_blocks, pair_far), down_mine)
    cotangent_blocks = direct_blocks(after(cotangent, normed2_blocks))
    down_near = gather_near_send(after(down_mine, pair_far))
    full_pair = gather_whole(*pair_far)
    normed2 = span_rows(normed2_blocks)
    activation, silu, slope = hidden_units(normed2, full_pair)
    down_near, cotangent_blocks = after((down_near, cotangent_blocks), activation)
    down_far = gather_far_send(*down_near)
    grad_mlp = span_rows(cotangent_blocks)
    down_term = weight_terms(grad_mlp, after(activation, down_near))
    down_sums = scatter_near_send(down_term)
    full_down = gather_whole(*after(down_far, down_term))
    down_sums = scatter_far_send(*down_sums)
    grad_gate, grad_up, mlp_back = hidden_back(
        after(grad_mlp, down_sums[:2]), silu, slope, full_down, full_pair
    )
    back_cores = core_sum(mlp_back)
    back_terms = direct_terms(back_cores)
    pair_term, mlp_rows = pair_terms(
        after(normed2, back_cores), grad_gate, grad_up, activation, full_down
    )
    pair_sums = scatter_near_send(pair_term)
    back_terms, down_sums = after((back_terms, down_sums), pair_term)
    down_parts = spread_ctx(after(scatter_whole(*down_sums), back_terms))
    grad_normed2 = sum_terms(back_terms).reshape(tokens.shape)
    grad_out = cotangent.astype(f32)
    scaled2 = norm_mlp * grad_normed2
    grad_hidden1 = (
        grad_out
        + mlp_root * scaled2
        - hidden1 * mlp_root**3 * jnp.mean(scaled2 * hidden1, axis=-1, keepdims=True)
    )
    gain_mlp = jnp.sum(grad_normed2 * hidden1 * mlp_root, axis=(0, 1))
    grad_own = grad_hidden1.astype(bf16)
    grad_attn = jnp.concatenate([grad_own, swap_tensor(grad_own)], axis=1).reshape(
        row_count, model_width
    )
    grad_mixed = jnp.dot(grad_attn, full_out, preferred_element_type=f32).astype(bf16)
    grad_q, kv_terms = attend_back(
        prefix, row_pos, col_pos, queries, kv_rows, grad_mixed, cosine_flat, sine_flat
    )
    down_parts, pair_sums = after((down_parts, pair_sums), kv_terms)
    pair_sums = scatter_far_send(*pair_sums)
    kv_sent = after(kv_terms, down_parts)
    kv_own = direct_terms(
        [kv_sent[:, j * span_len : (j + 1) * span_len] for j in range(ctx_size)]
    )
    mlp_cores = core_sum(after(mlp_rows, back_terms))
    kv_own = after(kv_own, mlp_cores)
    mlp_terms = direct_terms(after(mlp_cores, kv_own))
    kv_sum = sum_terms(kv_own)
    grad_k = rotate_back(kv_sum[:, :, None, :kv_cols], cosine_table, sine_table)
    grad_k = grad_k.reshape(row_count, kv_cols).astype(bf16)
    grad_v = kv_sum[:, :, kv_cols:].reshape(row_count, kv_cols).astype(bf16)
    grad_qkv = jnp.concatenate([grad_q, grad_k, grad_v], axis=1)
    attn_term = attn_weight_terms(normed1, after(grad_qkv, pair_sums), grad_attn, mixed_low)
    attn_sums = scatter_near_send(attn_term)
    grad_w_down = hidden_grad(natural_ctx(down_parts), ff_cols)
    attn_back = project_back(grad_qkv, full_qkv).reshape(seq_dev, span_len, model_width)
    grad_normed1 = attn_back[:, :own_rows] + swap_tensor(
        attn_back[:, own_rows:].astype(bf16)
    ).astype(f32)
    scaled1 = norm_attn * grad_normed1
    grad_tokens = (
        grad_hidden1
        + attn_root * scaled1
        - x_own * attn_root**3 * jnp.mean(scaled1 * x_own, axis=-1, keepdims=True)
    ).astype(bf16)
    attn_sums = scatter_far_send(*after(attn_sums, grad_tokens, mlp_terms))
    output = (hidden1 + sum_terms(mlp_terms).reshape(tokens.shape)).astype(bf16)
    pair_grads = spread_ctx(after(scatter_whole(*pair_sums), mlp_terms))
    gain_attn = jnp.sum(grad_normed1 * x_own * attn_root, axis=(0, 1))
    place_query = lax.dynamic_update_slice_in_dim(
        jnp.zeros_like(b_query), jnp.sum(grad_q, axis=0, dtype=f32), tensor_at * q_cols, 0
    )
    place_key = lax.dynamic_update_slice_in_dim(
        jnp.zeros_like(b_key), jnp.sum(grad_k, axis=0, dtype=f32), tensor_at * kv_cols, 0
    )
    place_value = lax.dynamic_update_slice_in_dim(
        jnp.zeros_like(b_value), jnp.sum(grad_v, axis=0, dtype=f32), tensor_at * kv_cols, 0
    )
    sums = jnp.concatenate([gain_attn, gain_mlp, place_query, place_key, place_value])
    sums = sum_everywhere(after(sums, attn_sums).reshape(-1, 128)).reshape(-1)
    splits = [model_width, 2 * model_width]
    splits += [splits[1] + b_query.shape[0], splits[1] + b_query.shape[0] + b_key.shape[0]]
    sum_attn, sum_mlp, sum_query, sum_key, sum_value = jnp.split(sums, splits)
    attn_grads = sum_terms(ctx_terms(scatter_whole(*attn_sums)))
    grad_w_qkv, grad_w_out = attn_grads[:, :-q_cols], attn_grads[:, -q_cols:]
    pair_grads = natural_ctx(pair_grads)
    grad_w_gate = hidden_grad(pair_grads[:, :, :ff_part], ff_cols)
    grad_w_up = hidden_grad(pair_grads[:, :, ff_part:], ff_cols)
    grad_w_query = grad_w_qkv[:, :q_cols]
    grad_w_key = grad_w_qkv[:, q_cols : q_cols + kv_cols]
    grad_w_value = grad_w_qkv[:, q_cols + kv_cols :]
    return (
        output,
        grad_tokens,
        grad_w_query,
        grad_w_key,
        grad_w_value,
        grad_w_out,
        grad_w_gate,
        grad_w_up,
        grad_w_down,
        sum_query,
        sum_key,
        sum_value,
        sum_attn,
        sum_mlp,
    )


def solution(mesh):
    placed = (
        P("dp", ("ctx", "tensor"), None),
        P("dp"),
        P(("dp", "ctx"), "tensor"),
        P(("dp", "ctx"), "tensor"),
        P(("dp", "ctx"), "tensor"),
        P(("dp", "ctx"), "tensor"),
        P(("dp", "ctx"), "tensor"),
        P(("dp", "ctx"), "tensor"),
        P(("dp", "ctx"), "tensor"),
        P(),
        P(),
        P(),
        P(),
        P(),
        P("dp", ("ctx", "tensor"), None),
    )
    return jax.shard_map(
        per_device,
        mesh=mesh,
        in_specs=placed,
        out_specs=(
            P("dp", ("ctx", "tensor"), None),
            P("dp", ("ctx", "tensor"), None),
            P(("dp", "ctx"), "tensor"),
            P(("dp", "ctx"), "tensor"),
            P(("dp", "ctx"), "tensor"),
            P(("dp", "ctx"), "tensor"),
            P(("dp", "ctx"), "tensor"),
            P(("dp", "ctx"), "tensor"),
            P(("dp", "ctx"), "tensor"),
            P(),
            P(),
            P(),
            P(),
            P(),
        ),
        check_vma=False,
    )
```

time: 793 us -> 547 us (0.69)
  waiting for transfers between devices: 344 us -> 225 us
  matrix products: 78.6 us -> 2.59 us
  Pallas kernels: 0 us -> 71.2 us
  local copies, waits for them, and re-layouts: 112 us -> 54 us
  blocking collectives: 46.9 us -> 0 us
  starting transfers between devices: 140 us -> 125 us
    ppermute x40 -> x33, waiting for transfers between devices: 187 us -> 99.6 us  [the longest x14 59.1 us: swap_y(): return lax.ppermute(value, 'dp', [(i, i ^ 2) for i in range(4)])]
    pallas_call x0 -> x8, Pallas kernels: none -> 71.2 us  [the longest x1 20.3 us: hidden_back(): pl.pallas_call(hidden_back_kernel, out_shape=(out, out, out_x), grid=(row...]
    dot_general x21 -> x0, matrix products: 51.1 us -> none  [the longest x5 18.8 us: weight_term(): jnp.einsum('rd,rc->dc', left, right, preferred_element_type=jnp.float32)]
    psum x1 -> x0, blocking collectives: 46.9 us -> none  [per_device(): lax.psum((gain_attn, gain_mlp, place_query, place_key, place_value), ('dp...]
    ppermute x48 -> x39, waiting for transfers between devices: 157 us -> 121 us  [shift_ctx(): lax.ppermute(value, 'ctx', [(i, (i + distance) % size) for i in range(siz...]
    dynamic_update_slice x63 -> x0, local copies, waits for them, and re-layouts: 29 us -> none  [the longest x43 18 us: update_at(): return lax.dynamic_update_index_in_dim(target, block, index, 0)]
    dot_general x5 -> x2, matrix products: 26.7 us -> 1.82 us  [project_back(): jnp.einsum('rf,df->rd', left, right, preferred_element_type=jnp.float32)]
    add x24 -> x10, other arithmetic: 21.1 us -> 1.94 us  [the longest x4 1.91 us: sum_terms(): total = total + term.astype(jnp.float32)]
  transfers between devices with their start and end apart: 96 -> 80, of which waited for: 47 -> 37; matrix products, arithmetic and copies ran while one was open for 21% -> 16% of each run, Pallas kernels for 0% -> 9%
where the time goes in v2:
time: 547 us; the launch traced here: 537 us
  waiting for transfers between devices  225 us (41%)
  starting transfers between devices  125 us (23%)
  Pallas kernels  71.2 us (13%)
  other arithmetic  56.3 us (10%)
  local copies, waits for them, and re-layouts  54 us (10%)
    ppermute x39, waiting for transfers between devices, shift_ctx(): lax.ppermute(value, 'ctx', [(i, (i + distance) % size) for i in range(siz...  121 us
    ppermute x39, starting transfers between devices, shift_ctx(): lax.ppermute(value, 'ctx', [(i, (i + distance) % size) for i in range(siz...  81.2 us
    ppermute x14, waiting for transfers between devices, swap_y(): return lax.ppermute(value, 'dp', [(i, i ^ 2) for i in range(4)])  59.1 us
    ppermute x14, waiting for transfers between devices, swap_x(): return lax.ppermute(value, 'dp', [(i, i ^ 1) for i in range(4)])  33.8 us
    pallas_call x1, Pallas kernels, hidden_back(): pl.pallas_call(hidden_back_kernel, out_shape=(out, out, out_x), grid=(row...  20.3 us
    unnamed x215, local copies, waits for them, and re-layouts  19.9 us
    ppermute x14, starting transfers between devices, swap_x(): return lax.ppermute(value, 'dp', [(i, i ^ 1) for i in range(4)])  17.3 us
    ppermute x14, starting transfers between devices, swap_y(): return lax.ppermute(value, 'dp', [(i, i ^ 2) for i in range(4)])  16.7 us
  transfers between devices with their start and end apart: 80, of which 37 were waited for; matrix products, arithmetic and copies ran while one was open for 16% of the time, Pallas kernels for 9%

profile of v2, /device:TPU:0, one launch (start us, length us, event | category | flops | bytes accessed | tf_op | source)
XLA Modules:
  0.0 537.2 jit_solution(6322932357667161470)
XLA Ops:
  22.9 5.8 %collective-permute-start.10 = (bf16[96,768]{1,0:T(8,128)(2,1)S(1)}, bf16[96,768]{1,0:T(8,128)(2,1)S(1)}, u32[]{:S(2)}, u32[]{:S(2)}) collective-permute-start(bf16[96,768]{1,0:T(8,128)(2,1)S(1)} %convert_element_type.291), channel_id=1, source_target_pairs={{0,6},{2,0},{4,2},{6,4},{1,7},{3,1},{5,3},{7,5},{8,14},{10,8},{12,... | collective-permute-start | bytes 442376 | tf_op jit(solution)/shard_map/ppermute | solution.py:393
  36.7 5.7 %collective-permute-done.9 = bf16[96,768]{1,0:T(8,128)(2,1)S(1)} collective-permute-done((bf16[96,768]{1,0:T(8,128)(2,1)S(1)}, bf16[96,768]{1,0:T(8,128)(2,1)S(1)}, u32[]{:S(2)}, u32[]{:S(2)}) %collective-permute-start.9) | collective-permute-done | bytes 147488 | tf_op jit(solution)/shard_map/ppermute | solution.py:393
  51.1 13.5 %collective-permute-done.5 = bf16[2,192,1024]{2,1,0:T(8,128)(2,1)S(1)} collective-permute-done((bf16[2,192,1024]{2,1,0:T(8,128)(2,1)S(1)}, bf16[2,192,1024]{2,1,0:T(8,128)(2,1)S(1)}, u32[]{:S(2)}, u32[]{:S(2)}) %collective-permute-start.5) | collective-permute-done | bytes 786464 | tf_op jit(solution)/shard_map/ppermute | solution.py:401
  77.7 10.2 %collective-permute-start.16 = (bf16[2,128,256]{2,1,0:T(8,128)(2,1)S(1)}, bf16[2,128,256]{2,1,0:T(8,128)(2,1)S(1)}, u32[]{:S(2)}, u32[]{:S(2)}) collective-permute-start(bf16[2,128,256]{2,1,0:T(8,128)(2,1)S(1)} %bitcast.422), channel_id=1, source_target_pairs={{0,2},{2,4},{4,6},{6,0},{1,3},{3,5},{5,7},{7,1},{8,10},{10,12},{12... | collective-permute-start | bytes 393224 | tf_op jit(solution)/shard_map/ppermute | solution.py:393
  96.5 4.4 collective-permute-start.24
  103.5 5.1 attend.1.right2_ref
  112.5 14.7 %collective-permute-done.21 = bf16[192,2304]{1,0:T(8,128)(2,1)S(1)} collective-permute-done((bf16[192,2304]{1,0:T(8,128)(2,1)S(1)}, bf16[192,2304]{1,0:T(8,128)(2,1)S(1)}, u32[]{:S(2)}, u32[]{:S(2)}) %collective-permute-start.21) | collective-permute-done | bytes 884768 | tf_op jit(solution)/shard_map/ppermute | solution.py:397
  137.9 11.6 %collective-permute-start.29 = (bf16[2,64,1536]{2,1,0:T(8,128)(2,1)S(1)}, bf16[2,64,1536]{2,1,0:T(8,128)(2,1)S(1)}, u32[]{:S(2)}, u32[]{:S(2)}) collective-permute-start(bf16[2,64,1536]{2,1,0:T(8,128)(2,1)S(1)} %multiply_convert_fusion), channel_id=1, source_target_pairs={{0,6},{2,0},{4,2},{6,4},{1,7},{3,1},{5,3},{7,5},{8,14},{10,8},{12,... | collective-permute-start | bytes 1179656 | tf_op jit(solution)/shard_map/ppermute | solution.py:393
  149.9 15.3 %collective-permute-done.28 = bf16[2,64,1536]{2,1,0:T(8,128)(2,1)S(1)} collective-permute-done((bf16[2,64,1536]{2,1,0:T(8,128)(2,1)S(1)}, bf16[2,64,1536]{2,1,0:T(8,128)(2,1)S(1)}, u32[]{:S(2)}, u32[]{:S(2)}) %collective-permute-start.28) | collective-permute-done | bytes 393248 | tf_op jit(solution)/shard_map/ppermute | solution.py:393
  166.4 7.0 %collective-permute-done.30 = bf16[2,192,2304]{2,1,0:T(8,128)(2,1)S(1)} collective-permute-done((bf16[2,192,2304]{2,1,0:T(8,128)(2,1)S(1)}, bf16[2,192,2304]{2,1,0:T(8,128)(2,1)S(1)}, u32[]{:S(2)}, u32[]{:S(2)}) %collective-permute-start.30) | collective-permute-done | bytes 1769504 | tf_op jit(solution)/shard_map/ppermute | solution.py:401
  180.7 3.5 pad_maximum_fusion
  187.3 14.3 %hidden_units.1 = (bf16[1024,1152]{1,0:T(8,128)(2,1)S(1)}, bf16[1024,1152]{1,0:T(8,128)(2,1)S(1)}, bf16[1024,1152]{1,0:T(8,128)(2,1)S(1)}) custom-call(bf16[1024,1536]{1,0:T(8,128)(2,1)S(1)} %constant_dynamic-update-slice_fusion.4.x_ref.left_ref, bf16[1536,2304]{1,0:T(8,128)(2,1)} %bitcast.394, bf16[1536,2304]{1,0:T(8,128)(2,1)} %bitcast.395), custom_call_target="tpu_custom_call" | custom-call | flops 7247757312 | bytes 17301504 | tf_op jit(solution)/shard_map/hidden_units/pallas_call | solution.py:218
  213.3 4.9 weight_terms.1
  218.3 8.5 %collective-permute-done.42 = bf16[2,192,1152]{2,1,0:T(8,128)(2,1)} collective-permute-done((bf16[2,192,1152]{2,1,0:T(8,128)(2,1)S(1)}, bf16[2,192,1152]{2,1,0:T(8,128)(2,1)}, u32[]{:S(2)}, u32[]{:S(2)}) %collective-permute-start.42) | collective-permute-done | bytes 884768 | tf_op jit(solution)/shard_map/ppermute | solution.py:397
  226.7 4.9 collective-permute-done.41
  237.9 16.0 %collective-permute-done.40 = bf16[2,192,1152]{2,1,0:T(8,128)(2,1)S(1)} collective-permute-done((bf16[2,192,1152]{2,1,0:T(8,128)(2,1)S(1)}, bf16[2,192,1152]{2,1,0:T(8,128)(2,1)S(1)}, u32[]{:S(2)}, u32[]{:S(2)}) %collective-permute-start.40) | collective-permute-done | bytes 884768 | tf_op jit(solution)/shard_map/ppermute | solution.py:401
  257.3 20.3 %hidden_back.1 = (bf16[1024,1152]{1,0:T(8,128)(2,1)S(1)}, bf16[1024,1152]{1,0:T(8,128)(2,1)S(1)}, bf16[1024,1536]{1,0:T(8,128)(2,1)}) custom-call(bf16[1024,1536]{1,0:T(8,128)(2,1)} %copy-done.22, bf16[1024,1152]{1,0:T(8,128)(2,1)S(1)} %copy-done.29, bf16[1024,1152]{1,0:T(8,128)(2,1)S(1)} %copy-done.31, bf16[1536,1152]{1,0:T(8,128)(2,1)} %bitcast.406, ...), custom_call_target="tpu_custom_call" | custom-call | flops 10871635968 | bytes 26345472 | tf_op jit(solution)/shard_map/hidden_back/pallas_call | solution.py:265
  289.4 3.8 collective-permute-start.44
  295.1 14.7 %pair_terms.1 = (bf16[1536,2304]{1,0:T(8,128)(2,1)}, bf16[1024,1536]{1,0:T(8,128)(2,1)S(1)}) custom-call(bf16[1024,1536]{1,0:T(8,128)(2,1)} %copy-done.21, bf16[1024,1152]{1,0:T(8,128)(2,1)S(1)} %copy-done.33, bf16[1024,1152]{1,0:T(8,128)(2,1)S(1)} %copy-done.35, bf16[1024,1152]{1,0:T(8,128)(2,1)S(1)} %copy-done.27, bf16[1536,1152]{1,0:T(8,128)(2,1)} %bitcast.407), custom_call_target="tpu_custom_call" | custom-call | flops 10871635968 | bytes 23986176 | tf_op jit(solution)/shard_map/pair_terms/pallas_call | solution.py:298
  309.8 4.7 fusion.37
  322.3 7.2 %collective-permute-done.45 = bf16[128,1536]{1,0:T(8,128)(2,1)S(1)} collective-permute-done((bf16[128,1536]{1,0:T(8,128)(2,1)S(1)}, bf16[128,1536]{1,0:T(8,128)(2,1)S(1)}, u32[]{:S(2)}, u32[]{:S(2)}) %collective-permute-start.45) | collective-permute-done | bytes 393248 | tf_op jit(solution)/shard_map/ppermute | solution.py:393
  340.0 7.4 %attend_back.1 = (bf16[256,768]{1,0:T(8,128)(2,1)S(1)}, bf16[2,512,256]{2,1,0:T(8,128)(2,1)S(1)}) custom-call(s32[2]{0:T(128)S(1)} %copy-done.25, s32[128,1]{1,0:T(8,128)S(1)} %copy-done.20, s32[1,512]{1,0:T(1,128)S(1)} %bitcast.390, bf16[256,768]{1,0:T(8,128)(2,1)S(1)} %copy-done.18, bf16[2,512,256]{2,1,0:T(8,128)(2,1)S(1)} %copy-done.24, ...), custom_call_target="tpu_custom_call" | custom-call | flops 1006632960 | bytes 2228224 | tf_op jit(solution)/shard_map/attend_back/pallas_call | solution.py:161
  353.4 6.0 %collective-permute-done.54 = bf16[2,192,2304]{2,1,0:T(8,128)(2,1)} collective-permute-done((bf16[2,192,2304]{2,1,0:T(8,128)(2,1)}, bf16[2,192,2304]{2,1,0:T(8,128)(2,1)}, u32[]{:S(2)}, u32[]{:S(2)}) %collective-permute-start.54) | collective-permute-done | bytes 1769504 | tf_op jit(solution)/shard_map/ppermute | solution.py:397
  362.0 3.6 collective-permute-start.56
  397.3 26.4 %collective-permute-done.60 = bf16[128,1536]{1,0:T(8,128)(2,1)} collective-permute-done((bf16[128,1536]{1,0:T(8,128)(2,1)}, bf16[128,1536]{1,0:T(8,128)(2,1)}, u32[]{:S(2)}, u32[]{:S(2)}) %collective-permute-start.60) | collective-permute-done | bytes 393248 | tf_op jit(solution)/shard_map/ppermute | solution.py:393
  439.3 9.3 %collective-permute-done.72 = bf16[96,2304]{1,0:T(8,128)(2,1)S(1)} collective-permute-done((bf16[96,2304]{1,0:T(8,128)(2,1)S(1)}, bf16[96,2304]{1,0:T(8,128)(2,1)S(1)}, u32[]{:S(2)}, u32[]{:S(2)}) %collective-permute-start.72) | collective-permute-done | bytes 442400 | tf_op jit(solution)/shard_map/ppermute | solution.py:393
  448.6 17.8 %collective-permute-done.73 = bf16[96,2304]{1,0:T(8,128)(2,1)S(1)} collective-permute-done((bf16[96,2304]{1,0:T(8,128)(2,1)S(1)}, bf16[96,2304]{1,0:T(8,128)(2,1)S(1)}, u32[]{:S(2)}, u32[]{:S(2)}) %collective-permute-start.73) | collective-permute-done | bytes 442400 | tf_op jit(solution)/shard_map/ppermute | solution.py:393
  472.5 12.5 %collective-permute-done.67 = bf16[192,1792]{1,0:T(8,128)(2,1)S(1)} collective-permute-done((bf16[192,1792]{1,0:T(8,128)(2,1)S(1)}, bf16[192,1792]{1,0:T(8,128)(2,1)S(1)}, u32[]{:S(2)}, u32[]{:S(2)}) %collective-permute-start.67) | collective-permute-done | bytes 688160 | tf_op jit(solution)/shard_map/ppermute | solution.py:401
  495.7 6.7 %collective-permute-start.78 = (f32[40,128]{1,0:T(8,128)S(1)}, f32[40,128]{1,0:T(8,128)S(1)}, u32[]{:S(2)}, u32[]{:S(2)}) collective-permute-start(f32[40,128]{1,0:T(8,128)S(1)} %add.478), channel_id=1, source_target_pairs={{0,2},{2,0},{4,6},{6,4},{1,3},{3,1},{5,7},{7,5},{8,10},{10,8},{12,... | collective-permute-start | bytes 61448 | tf_op jit(solution)/shard_map/ppermute | solution.py:526
  505.3 3.4 collective-permute-start.69
  510.6 6.7 %collective-permute-done.69 = bf16[96,1792]{1,0:T(8,128)(2,1)S(1)} collective-permute-done((bf16[96,1792]{1,0:T(8,128)(2,1)S(1)}, bf16[96,1792]{1,0:T(8,128)(2,1)S(1)}, u32[]{:S(2)}, u32[]{:S(2)}) %collective-permute-start.69) | collective-permute-done | bytes 344096 | tf_op jit(solution)/shard_map/ppermute | solution.py:393
  517.3 18.0 %collective-permute-done.70 = bf16[96,1792]{1,0:T(8,128)(2,1)S(1)} collective-permute-done((bf16[96,1792]{1,0:T(8,128)(2,1)S(1)}, bf16[96,1792]{1,0:T(8,128)(2,1)S(1)}, u32[]{:S(2)}, u32[]{:S(2)}) %collective-permute-start.70) | collective-permute-done | bytes 344096 | tf_op jit(solution)/shard_map/ppermute | solution.py:393
  (532 shorter events, 220.2 us)
Async XLA Ops:
  13.9 35.1 %collective-permute-start = (bf16[2,64,1536]{2,1,0:T(8,128)(2,1)S(1)}, bf16[2,64,1536]{2,1,0:T(8,128)(2,1)}, u32[]{:S(2)}, u32[]{:S(2)}) collective-permute-start(bf16[2,64,1536]{2,1,0:T(8,128)(2,1)S(1)} %fusion.7), channel_id=1, source_target_pairs={{0,1},{1,0},{2,3},{3,2},{4,5},{5,4},{6,7},{7,6},{8,9},{9,8},{10,11... | collective-permute-start | bytes 1179656 | tf_op jit(solution)/shard_map/ppermute | solution.py:388
  42.5 28.8 %collective-permute-start.11 = (bf16[96,2304]{1,0:T(8,128)(2,1)S(1)}, bf16[96,2304]{1,0:T(8,128)(2,1)S(1)}, u32[]{:S(2)}, u32[]{:S(2)}) collective-permute-start(bf16[96,2304]{1,0:T(8,128)(2,1)S(1)} %get-tuple-element.269), channel_id=1, source_target_pairs={{0,2},{2,4},{4,6},{6,0},{1,3},{3,5},{5,7},{7,1},{8,10},{10,12},{12... | collective-permute-start | bytes 1327112 | tf_op jit(solution)/shard_map/ppermute | solution.py:393
  42.5 32.1 %collective-permute-start.12 = (bf16[96,2304]{1,0:T(8,128)(2,1)S(1)}, bf16[96,2304]{1,0:T(8,128)(2,1)S(1)}, u32[]{:S(2)}, u32[]{:S(2)}) collective-permute-start(bf16[96,2304]{1,0:T(8,128)(2,1)S(1)} %get-tuple-element.268), channel_id=1, source_target_pairs={{0,4},{2,6},{4,0},{6,2},{1,5},{3,7},{5,1},{7,3},{8,12},{10,14},{12... | collective-permute-start | bytes 1327112 | tf_op jit(solution)/shard_map/ppermute | solution.py:393
  49.1 25.6 %collective-permute-start.13 = (bf16[96,2304]{1,0:T(8,128)(2,1)S(1)}, bf16[96,2304]{1,0:T(8,128)(2,1)S(1)}, u32[]{:S(2)}, u32[]{:S(2)}) collective-permute-start(bf16[96,2304]{1,0:T(8,128)(2,1)S(1)} %get-tuple-element.267), channel_id=1, source_target_pairs={{0,6},{2,0},{4,2},{6,4},{1,7},{3,1},{5,3},{7,5},{8,14},{10,8},{12,... | collective-permute-start | bytes 1327112 | tf_op jit(solution)/shard_map/ppermute | solution.py:393
  96.5 38.8 %collective-permute-start.24 = (bf16[96,1152]{1,0:T(8,128)(2,1)S(1)}, bf16[96,1152]{1,0:T(8,128)(2,1)S(1)}, u32[]{:S(2)}, u32[]{:S(2)}) collective-permute-start(bf16[96,1152]{1,0:T(8,128)(2,1)S(1)} %get-tuple-element.314), channel_id=1, source_target_pairs={{0,2},{2,4},{4,6},{6,0},{1,3},{3,5},{5,7},{7,1},{8,10},{10,12},{12... | collective-permute-start | bytes 663560 | tf_op jit(solution)/shard_map/ppermute | solution.py:393
  100.9 34.4 %collective-permute-start.25 = (bf16[96,1152]{1,0:T(8,128)(2,1)S(1)}, bf16[96,1152]{1,0:T(8,128)(2,1)S(1)}, u32[]{:S(2)}, u32[]{:S(2)}) collective-permute-start(bf16[96,1152]{1,0:T(8,128)(2,1)S(1)} %get-tuple-element.313), channel_id=1, source_target_pairs={{0,4},{2,6},{4,0},{6,2},{1,5},{3,7},{5,1},{7,3},{8,12},{10,14},{12... | collective-permute-start | bytes 663560 | tf_op jit(solution)/shard_map/ppermute | solution.py:393
  101.9 33.4 %collective-permute-start.26 = (bf16[96,1152]{1,0:T(8,128)(2,1)S(1)}, bf16[96,1152]{1,0:T(8,128)(2,1)S(1)}, u32[]{:S(2)}, u32[]{:S(2)}) collective-permute-start(bf16[96,1152]{1,0:T(8,128)(2,1)S(1)} %get-tuple-element.312), channel_id=1, source_target_pairs={{0,6},{2,0},{4,2},{6,4},{1,7},{3,1},{5,3},{7,5},{8,14},{10,8},{12,... | collective-permute-start | bytes 663560 | tf_op jit(solution)/shard_map/ppermute | solution.py:393
  127.8 38.6 %collective-permute-start.31 = (bf16[2,192,2304]{2,1,0:T(8,128)(2,1)S(1)}, bf16[2,192,2304]{2,1,0:T(8,128)(2,1)S(1)}, u32[]{:S(2)}, u32[]{:S(2)}) collective-permute-start(bf16[2,192,2304]{2,1,0:T(8,128)(2,1)S(1)} %pad_maximum_fusion.6), channel_id=1, source_target_pairs={{0,8},{8,0},{16,24},{24,16},{1,9},{9,1},{17,25},{25,17},{2,10},{10... | collective-permute-start | bytes 5308424 | tf_op jit(solution)/shard_map/ppermute | solution.py:397
  132.8 40.6 %collective-permute-start.30 = (bf16[2,192,2304]{2,1,0:T(8,128)(2,1)S(1)}, bf16[2,192,2304]{2,1,0:T(8,128)(2,1)S(1)}, u32[]{:S(2)}, u32[]{:S(2)}) collective-permute-start(bf16[2,192,2304]{2,1,0:T(8,128)(2,1)S(1)} %pad_maximum_fusion.5), channel_id=1, source_target_pairs={{0,16},{8,24},{16,0},{24,8},{1,17},{9,25},{17,1},{25,9},{2,18},{10... | collective-permute-start | bytes 5308424 | tf_op jit(solution)/shard_map/ppermute | solution.py:401
  136.0 29.1 %collective-permute-start.28 = (bf16[2,64,1536]{2,1,0:T(8,128)(2,1)S(1)}, bf16[2,64,1536]{2,1,0:T(8,128)(2,1)S(1)}, u32[]{:S(2)}, u32[]{:S(2)}) collective-permute-start(bf16[2,64,1536]{2,1,0:T(8,128)(2,1)S(1)} %multiply_convert_fusion), channel_id=1, source_target_pairs={{0,4},{2,6},{4,0},{6,2},{1,5},{3,7},{5,1},{7,3},{8,12},{10,14},{12... | collective-permute-start | bytes 1179656 | tf_op jit(solution)/shard_map/ppermute | solution.py:393
  137.9 28.5 %collective-permute-start.29 = (bf16[2,64,1536]{2,1,0:T(8,128)(2,1)S(1)}, bf16[2,64,1536]{2,1,0:T(8,128)(2,1)S(1)}, u32[]{:S(2)}, u32[]{:S(2)}) collective-permute-start(bf16[2,64,1536]{2,1,0:T(8,128)(2,1)S(1)} %multiply_convert_fusion), channel_id=1, source_target_pairs={{0,6},{2,0},{4,2},{6,4},{1,7},{3,1},{5,3},{7,5},{8,14},{10,8},{12,... | collective-permute-start | bytes 1179656 | tf_op jit(solution)/shard_map/ppermute | solution.py:393
  173.4 31.1 %collective-permute-start.35 = (bf16[2,64,1536]{2,1,0:T(8,128)(2,1)S(1)}, bf16[2,64,1536]{2,1,0:T(8,128)(2,1)}, u32[]{:S(2)}, u32[]{:S(2)}) collective-permute-start(bf16[2,64,1536]{2,1,0:T(8,128)(2,1)S(1)} %copy-done.52), channel_id=1, source_target_pairs={{0,2},{2,4},{4,6},{6,0},{1,3},{3,5},{5,7},{7,1},{8,10},{10,12},{12... | collective-permute-start | bytes 1179656 | tf_op jit(solution)/shard_map/ppermute | solution.py:393
  174.0 30.5 %collective-permute-start.36 = (bf16[2,64,1536]{2,1,0:T(8,128)(2,1)S(1)}, bf16[2,64,1536]{2,1,0:T(8,128)(2,1)}, u32[]{:S(2)}, u32[]{:S(2)}) collective-permute-start(bf16[2,64,1536]{2,1,0:T(8,128)(2,1)S(1)} %copy-done.52), channel_id=1, source_target_pairs={{0,4},{2,6},{4,0},{6,2},{1,5},{3,7},{5,1},{7,3},{8,12},{10,14},{12... | collective-permute-start | bytes 1179656 | tf_op jit(solution)/shard_map/ppermute | solution.py:393
  175.9 28.6 %collective-permute-start.37 = (bf16[2,64,1536]{2,1,0:T(8,128)(2,1)S(1)}, bf16[2,64,1536]{2,1,0:T(8,128)(2,1)}, u32[]{:S(2)}, u32[]{:S(2)}) collective-permute-start(bf16[2,64,1536]{2,1,0:T(8,128)(2,1)S(1)} %copy-done.52), channel_id=1, source_target_pairs={{0,6},{2,0},{4,2},{6,4},{1,7},{3,1},{5,3},{7,5},{8,14},{10,8},{12,... | collective-permute-start | bytes 1179656 | tf_op jit(solution)/shard_map/ppermute | solution.py:393
  283.1 35.3 %collective-permute-start.48 = (bf16[192,1152]{1,0:T(8,128)(2,1)}, bf16[192,1152]{1,0:T(8,128)(2,1)S(1)}, u32[]{:S(2)}, u32[]{:S(2)}) collective-permute-start(bf16[192,1152]{1,0:T(8,128)(2,1)} %get-tuple-element.298), channel_id=1, source_target_pairs={{0,8},{8,0},{16,24},{24,16},{1,9},{9,1},{17,25},{25,17},{2,10},{10... | collective-permute-start | bytes 1327112 | tf_op jit(solution)/shard_map/ppermute | solution.py:397
  283.6 37.1 %collective-permute-start.47 = (bf16[192,1152]{1,0:T(8,128)(2,1)}, bf16[192,1152]{1,0:T(8,128)(2,1)S(1)}, u32[]{:S(2)}, u32[]{:S(2)}) collective-permute-start(bf16[192,1152]{1,0:T(8,128)(2,1)} %get-tuple-element.300), channel_id=1, source_target_pairs={{0,16},{8,24},{16,0},{24,8},{1,17},{9,25},{17,1},{25,9},{2,18},{10... | collective-permute-start | bytes 1327112 | tf_op jit(solution)/shard_map/ppermute | solution.py:401
  289.4 32.8 %collective-permute-start.44 = (bf16[128,1536]{1,0:T(8,128)(2,1)S(1)}, bf16[128,1536]{1,0:T(8,128)(2,1)S(1)}, u32[]{:S(2)}, u32[]{:S(2)}) collective-permute-start(bf16[128,1536]{1,0:T(8,128)(2,1)S(1)} %get-tuple-element.277), channel_id=1, source_target_pairs={{0,6},{2,0},{4,2},{6,4},{1,7},{3,1},{5,3},{7,5},{8,14},{10,8},{12,... | collective-permute-start | bytes 1179656 | tf_op jit(solution)/shard_map/ppermute | solution.py:393
  293.2 36.2 %collective-permute-start.45 = (bf16[128,1536]{1,0:T(8,128)(2,1)S(1)}, bf16[128,1536]{1,0:T(8,128)(2,1)S(1)}, u32[]{:S(2)}, u32[]{:S(2)}) collective-permute-start(bf16[128,1536]{1,0:T(8,128)(2,1)S(1)} %get-tuple-element.276), channel_id=1, source_target_pairs={{0,4},{2,6},{4,0},{6,2},{1,5},{3,7},{5,1},{7,3},{8,12},{10,14},{12... | collective-permute-start | bytes 1179656 | tf_op jit(solution)/shard_map/ppermute | solution.py:393
  295.1 34.3 %collective-permute-start.46 = (bf16[128,1536]{1,0:T(8,128)(2,1)S(1)}, bf16[128,1536]{1,0:T(8,128)(2,1)S(1)}, u32[]{:S(2)}, u32[]{:S(2)}) collective-permute-start(bf16[128,1536]{1,0:T(8,128)(2,1)S(1)} %get-tuple-element.275), channel_id=1, source_target_pairs={{0,2},{2,4},{4,6},{6,0},{1,3},{3,5},{5,7},{7,1},{8,10},{10,12},{12... | collective-permute-start | bytes 1179656 | tf_op jit(solution)/shard_map/ppermute | solution.py:393
  318.4 41.0 %collective-permute-start.54 = (bf16[2,192,2304]{2,1,0:T(8,128)(2,1)}, bf16[2,192,2304]{2,1,0:T(8,128)(2,1)}, u32[]{:S(2)}, u32[]{:S(2)}) collective-permute-start(bf16[2,192,2304]{2,1,0:T(8,128)(2,1)} %get-tuple-element.234), channel_id=1, source_target_pairs={{0,8},{8,0},{16,24},{24,16},{1,9},{9,1},{17,25},{25,17},{2,10},{10... | collective-permute-start | bytes 5308424 | tf_op jit(solution)/shard_map/ppermute | solution.py:397
  320.7 40.1 %collective-permute-start.55 = (bf16[2,192,2304]{2,1,0:T(8,128)(2,1)}, bf16[2,192,2304]{2,1,0:T(8,128)(2,1)}, u32[]{:S(2)}, u32[]{:S(2)}) collective-permute-start(bf16[2,192,2304]{2,1,0:T(8,128)(2,1)} %get-tuple-element.232), channel_id=1, source_target_pairs={{0,16},{8,24},{16,0},{24,8},{1,17},{9,25},{17,1},{25,9},{2,18},{10... | collective-permute-start | bytes 5308424 | tf_op jit(solution)/shard_map/ppermute | solution.py:401
  350.5 25.9 %collective-permute-start.49 = (bf16[512,1536]{1,0:T(8,128)(2,1)}, bf16[512,1536]{1,0:T(8,128)(2,1)S(1)}, u32[]{:S(2)}, u32[]{:S(2)}) collective-permute-start(bf16[512,1536]{1,0:T(8,128)(2,1)} %slice.256), channel_id=1, source_target_pairs={{0,1},{1,0},{2,3},{3,2},{4,5},{5,4},{6,7},{7,6},{8,9},{9,8},{10,11... | collective-permute-start | bytes 4718600 | tf_op jit(solution)/shard_map/ppermute | solution.py:388
  369.8 57.7 %collective-permute-start.64 = (bf16[192,2304]{1,0:T(8,128)(2,1)}, bf16[192,2304]{1,0:T(8,128)(2,1)}, u32[]{:S(2)}, u32[]{:S(2)}) collective-permute-start(bf16[192,2304]{1,0:T(8,128)(2,1)} %dynamic-slice_bitcast_fusion.8), channel_id=1, source_target_pairs={{0,8},{8,0},{16,24},{24,16},{1,9},{9,1},{17,25},{25,17},{2,10},{10... | collective-permute-start | bytes 2654216 | tf_op jit(solution)/shard_map/ppermute | solution.py:397
  376.4 52.5 %collective-permute-start.63 = (bf16[192,2304]{1,0:T(8,128)(2,1)}, bf16[192,2304]{1,0:T(8,128)(2,1)}, u32[]{:S(2)}, u32[]{:S(2)}) collective-permute-start(bf16[192,2304]{1,0:T(8,128)(2,1)} %dynamic-slice_bitcast_fusion.9), channel_id=1, source_target_pairs={{0,16},{8,24},{16,0},{24,8},{1,17},{9,25},{17,1},{25,9},{2,18},{10... | collective-permute-start | bytes 2654216 | tf_op jit(solution)/shard_map/ppermute | solution.py:401
  387.5 36.2 %collective-permute-start.60 = (bf16[128,1536]{1,0:T(8,128)(2,1)}, bf16[128,1536]{1,0:T(8,128)(2,1)}, u32[]{:S(2)}, u32[]{:S(2)}) collective-permute-start(bf16[128,1536]{1,0:T(8,128)(2,1)} %get-tuple-element.194), channel_id=1, source_target_pairs={{0,4},{2,6},{4,0},{6,2},{1,5},{3,7},{5,1},{7,3},{8,12},{10,14},{12... | collective-permute-start | bytes 1179656 | tf_op jit(solution)/shard_map/ppermute | solution.py:393
  390.8 32.9 %collective-permute-start.61 = (bf16[128,1536]{1,0:T(8,128)(2,1)S(1)}, bf16[128,1536]{1,0:T(8,128)(2,1)S(1)}, u32[]{:S(2)}, u32[]{:S(2)}) collective-permute-start(bf16[128,1536]{1,0:T(8,128)(2,1)S(1)} %copy-done.77), channel_id=1, source_target_pairs={{0,2},{2,4},{4,6},{6,0},{1,3},{3,5},{5,7},{7,1},{8,10},{10,12},{12... | collective-permute-start | bytes 1179656 | tf_op jit(solution)/shard_map/ppermute | solution.py:393
  433.7 32.7 %collective-permute-start.73 = (bf16[96,2304]{1,0:T(8,128)(2,1)S(1)}, bf16[96,2304]{1,0:T(8,128)(2,1)S(1)}, u32[]{:S(2)}, u32[]{:S(2)}) collective-permute-start(bf16[96,2304]{1,0:T(8,128)(2,1)S(1)} %get-tuple-element.251), channel_id=1, source_target_pairs={{0,4},{2,6},{4,0},{6,2},{1,5},{3,7},{5,1},{7,3},{8,12},{10,14},{12... | collective-permute-start | bytes 1327112 | tf_op jit(solution)/shard_map/ppermute | solution.py:393
  434.8 31.5 %collective-permute-start.74 = (bf16[96,2304]{1,0:T(8,128)(2,1)S(1)}, bf16[96,2304]{1,0:T(8,128)(2,1)S(1)}, u32[]{:S(2)}, u32[]{:S(2)}) collective-permute-start(bf16[96,2304]{1,0:T(8,128)(2,1)S(1)} %get-tuple-element.250), channel_id=1, source_target_pairs={{0,6},{2,0},{4,2},{6,4},{1,7},{3,1},{5,3},{7,5},{8,14},{10,8},{12,... | collective-permute-start | bytes 1327112 | tf_op jit(solution)/shard_map/ppermute | solution.py:393
  437.9 31.1 %collective-permute-start.66 = (bf16[2,192,1792]{2,1,0:T(8,128)(2,1)S(1)}, bf16[2,192,1792]{2,1,0:T(8,128)(2,1)S(1)}, u32[]{:S(2)}, u32[]{:S(2)}) collective-permute-start(bf16[2,192,1792]{2,1,0:T(8,128)(2,1)S(1)} %get-tuple-element.246), channel_id=1, source_target_pairs={{0,16},{8,24},{16,0},{24,8},{1,17},{9,25},{17,1},{25,9},{2,18},{10... | collective-permute-start | bytes 4128776 | tf_op jit(solution)/shard_map/ppermute | solution.py:401
  438.6 30.8 %collective-permute-start.65 = (bf16[2,192,1792]{2,1,0:T(8,128)(2,1)S(1)}, bf16[2,192,1792]{2,1,0:T(8,128)(2,1)S(1)}, u32[]{:S(2)}, u32[]{:S(2)}) collective-permute-start(bf16[2,192,1792]{2,1,0:T(8,128)(2,1)S(1)} %get-tuple-element.248), channel_id=1, source_target_pairs={{0,8},{8,0},{16,24},{24,16},{1,9},{9,1},{17,25},{25,17},{2,10},{10... | collective-permute-start | bytes 4128776 | tf_op jit(solution)/shard_map/ppermute | solution.py:397
  508.8 26.6 %collective-permute-start.70 = (bf16[96,1792]{1,0:T(8,128)(2,1)S(1)}, bf16[96,1792]{1,0:T(8,128)(2,1)S(1)}, u32[]{:S(2)}, u32[]{:S(2)}) collective-permute-start(bf16[96,1792]{1,0:T(8,128)(2,1)S(1)} %get-tuple-element.285), channel_id=1, source_target_pairs={{0,4},{2,6},{4,0},{6,2},{1,5},{3,7},{5,1},{7,3},{8,12},{10,14},{12... | collective-permute-start | bytes 1032200 | tf_op jit(solution)/shard_map/ppermute | solution.py:393
  508.8 26.6 %collective-permute-start.71 = (bf16[96,1792]{1,0:T(8,128)(2,1)S(1)}, bf16[96,1792]{1,0:T(8,128)(2,1)S(1)}, u32[]{:S(2)}, u32[]{:S(2)}) collective-permute-start(bf16[96,1792]{1,0:T(8,128)(2,1)S(1)} %get-tuple-element.284), channel_id=1, source_target_pairs={{0,2},{2,4},{4,6},{6,0},{1,3},{3,5},{5,7},{7,1},{8,10},{10,12},{12... | collective-permute-start | bytes 1032200 | tf_op jit(solution)/shard_map/ppermute | solution.py:393
  (148 other events, 1661.2 us)

commit v3 on v2

--- a/solution.py
+++ b/solution.py
@@ -520,7 +520,7 @@
 
 
 def sum_everywhere(value):
-    for axis in ("tensor", "dp", "ctx"):
+    for axis in ("dp", "ctx"):
         size, bit = lax.axis_size(axis), 1
         while bit < size:
             value = value + lax.ppermute(value, axis, [(i, i ^ bit) for i in range(size)])
@@ -602,14 +602,13 @@
     kv_sent = qkv[:, q_cols:].reshape(seq_dev, span_len, 2 * kv_cols)
     kv_blocks = direct_blocks(after(kv_sent, pair_blocks, out_near))
     pair_mine = natural_ctx(pair_blocks).reshape(-1, 2 * ff_part)
+    kv_blocks = after(kv_blocks, pair_mine)
+    out_far = after(out_far, kv_blocks)
     pair_near = gather_near_send(after(pair_mine, out_far))
-    kv_rows = jnp.concatenate(after(kv_blocks, pair_mine), axis=1)
-    down_blocks = spread_ctx(after(column_parts(w_down, ff_part), kv_blocks))
+    kv_rows = jnp.concatenate(kv_blocks, axis=1)
     mixed_low = attend(prefix, row_pos, col_pos, queries, kv_rows)
-    pair_near = after(pair_near, mixed_low)
-    pair_far = gather_far_send(*pair_near)
     full_out = gather_whole(*out_far)
-    attn_term = project_back(after(mixed_low, pair_near), full_out)
+    attn_term = project_back(mixed_low, full_out)
     attn_term = attn_term.reshape(seq_dev, span_len, model_width)
     hidden1 = (
         x_own
@@ -618,14 +617,15 @@
     )
     mlp_root = inverse_root(hidden1)
     normed2_own = (hidden1 * mlp_root * norm_mlp).astype(bf16)
-    down_blocks = after(down_blocks, normed2_own)
-    normed2_blocks = direct_blocks(after(normed2_own, down_blocks))
+    normed2_blocks = direct_blocks(normed2_own)
+    pair_far = gather_far_send(*after(pair_near, normed2_own))
+    normed2 = span_rows(after(normed2_blocks, pair_far[:2]))
+    down_blocks = spread_ctx(after(column_parts(w_down, ff_part), normed2))
     down_mine = natural_ctx(down_blocks).reshape(-1, ff_part)
-    normed2_blocks, pair_far = after((normed2_blocks, pair_far), down_mine)
-    cotangent_blocks = direct_blocks(after(cotangent, normed2_blocks))
+    cotangent_blocks = direct_blocks(after(cotangent, down_blocks))
+    pair_far = after(pair_far, down_mine)
     down_near = gather_near_send(after(down_mine, pair_far))
     full_pair = gather_whole(*pair_far)
-    normed2 = span_rows(normed2_blocks)
     activation, silu, slope = hidden_units(normed2, full_pair)
     down_near, cotangent_blocks = after((down_near, cotangent_blocks), activation)
     down_far = gather_far_send(*down_near)
@@ -633,9 +633,8 @@
     down_term = weight_terms(grad_mlp, after(activation, down_near))
     down_sums = scatter_near_send(down_term)
     full_down = gather_whole(*after(down_far, down_term))
-    down_sums = scatter_far_send(*down_sums)
     grad_gate, grad_up, mlp_back = hidden_back(
-        after(grad_mlp, down_sums[:2]), silu, slope, full_down, full_pair
+        after(grad_mlp, down_term), silu, slope, full_down, full_pair
     )
     back_cores = core_sum(mlp_back)
     back_terms = direct_terms(back_cores)
@@ -643,7 +642,10 @@
         after(normed2, back_cores), grad_gate, grad_up, activation, full_down
     )
     pair_sums = scatter_near_send(pair_term)
-    back_terms, down_sums = after((back_terms, down_sums), pair_term)
+    down_sums = scatter_far_send(*after(down_sums, pair_term))
+    back_terms = after(back_terms, pair_term)
+    mlp_cores = core_sum(after(mlp_rows, pair_term))
+    back_terms, down_sums = after((back_terms, down_sums), mlp_cores)
     down_parts = spread_ctx(after(scatter_whole(*down_sums), back_terms))
     grad_normed2 = sum_terms(back_terms).reshape(tokens.shape)
     grad_out = cotangent.astype(f32)
@@ -662,14 +664,12 @@
     grad_q, kv_terms = attend_back(
         prefix, row_pos, col_pos, queries, kv_rows, grad_mixed, cosine_flat, sine_flat
     )
-    down_parts, pair_sums = after((down_parts, pair_sums), kv_terms)
-    pair_sums = scatter_far_send(*pair_sums)
+    down_parts = after(down_parts, kv_terms)
     kv_sent = after(kv_terms, down_parts)
+    pair_sums = scatter_far_send(*after(pair_sums, kv_sent))
     kv_own = direct_terms(
         [kv_sent[:, j * span_len : (j + 1) * span_len] for j in range(ctx_size)]
     )
-    mlp_cores = core_sum(after(mlp_rows, back_terms))
-    kv_own = after(kv_own, mlp_cores)
     mlp_terms = direct_terms(after(mlp_cores, kv_own))
     kv_sum = sum_terms(kv_own)
     grad_k = rotate_back(kv_sum[:, :, None, :kv_cols], cosine_table, sine_table)
@@ -678,6 +678,7 @@
     grad_qkv = jnp.concatenate([grad_q, grad_k, grad_v], axis=1)
     attn_term = attn_weight_terms(normed1, after(grad_qkv, pair_sums), grad_attn, mixed_low)
     attn_sums = scatter_near_send(attn_term)
+    mlp_terms = after(mlp_terms, attn_term)
     grad_w_down = hidden_grad(natural_ctx(down_parts), ff_cols)
     attn_back = project_back(grad_qkv, full_qkv).reshape(seq_dev, span_len, model_width)
     grad_normed1 = attn_back[:, :own_rows] + swap_tensor(
@@ -689,9 +690,9 @@
         + attn_root * scaled1
         - x_own * attn_root**3 * jnp.mean(scaled1 * x_own, axis=-1, keepdims=True)
     ).astype(bf16)
-    attn_sums = scatter_far_send(*after(attn_sums, grad_tokens, mlp_terms))
+    attn_sums = scatter_far_send(*after(attn_sums, grad_tokens))
     output = (hidden1 + sum_terms(mlp_terms).reshape(tokens.shape)).astype(bf16)
-    pair_grads = spread_ctx(after(scatter_whole(*pair_sums), mlp_terms))
+    pair_grads = spread_ctx(after(scatter_whole(*pair_sums), mlp_terms, attn_sums[:2]))
     gain_attn = jnp.sum(grad_normed1 * x_own * attn_root, axis=(0, 1))
     place_query = lax.dynamic_update_slice_in_dim(
         jnp.zeros_like(b_query), jnp.sum(grad_q, axis=0, dtype=f32), tensor_at * q_cols, 0
@@ -703,11 +704,13 @@
         jnp.zeros_like(b_value), jnp.sum(grad_v, axis=0, dtype=f32), tensor_at * kv_cols, 0
     )
     sums = jnp.concatenate([gain_attn, gain_mlp, place_query, place_key, place_value])
-    sums = sum_everywhere(after(sums, attn_sums).reshape(-1, 128)).reshape(-1)
+    attn_terms = ctx_terms(scatter_whole(*after(attn_sums, pair_grads[1])))
+    sums = after(sums, attn_terms[1]).reshape(-1, 128)
+    sums = sum_everywhere(sums + swap_tensor(sums)).reshape(-1)
     splits = [model_width, 2 * model_width]
     splits += [splits[1] + b_query.shape[0], splits[1] + b_query.shape[0] + b_key.shape[0]]
     sum_attn, sum_mlp, sum_query, sum_key, sum_value = jnp.split(sums, splits)
-    attn_grads = sum_terms(ctx_terms(scatter_whole(*attn_sums)))
+    attn_grads = sum_terms(attn_terms)
     grad_w_qkv, grad_w_out = attn_grads[:, :-q_cols], attn_grads[:, -q_cols:]
     pair_grads = natural_ctx(pair_grads)
     grad_w_gate = hidden_grad(pair_grads[:, :, :ff_part], ff_cols)

time: 547 us -> 523 us (0.956)
  waiting for transfers between devices: 225 us -> 190 us
  starting transfers between devices: 125 us -> 143 us
  local copies, waits for them, and re-layouts: 54 us -> 45.2 us
    ppermute x14, waiting for transfers between devices: 59.1 us -> 13.6 us  [swap_y(): return lax.ppermute(value, 'dp', [(i, i ^ 2) for i in range(4)])]
    ppermute x39, starting transfers between devices: 81.2 us -> 111 us  [shift_ctx(): lax.ppermute(value, 'ctx', [(i, (i + distance) % size) for i in range(siz...]
    ppermute x39, waiting for transfers between devices: 121 us -> 132 us  [shift_ctx(): lax.ppermute(value, 'ctx', [(i, (i + distance) % size) for i in range(siz...]
    ppermute x5 -> x4, starting transfers between devices: 8.92 us -> 1.99 us  [sum_everywhere(): lax.ppermute(value, axis, [(i, i ^ bit) for i in range(size)])]
    unnamed x215 -> x213, local copies, waits for them, and re-layouts: 19.9 us -> 20.1 us
  transfers between devices with their start and end apart: 80 -> 80, of which waited for: 37 -> 37; matrix products, arithmetic and copies ran while one was open for 16% -> 15% of each run, Pallas kernels for 9% -> 10%
where the time goes in v3:
time: 523 us; the launch traced here: 516 us
  waiting for transfers between devices  190 us (36%)
  starting transfers between devices  143 us (27%)
  Pallas kernels  70.1 us (13%)
  other arithmetic  61.3 us (12%)
  local copies, waits for them, and re-layouts  45.2 us (9%)
    ppermute x39, waiting for transfers between devices, shift_ctx(): lax.ppermute(value, 'ctx', [(i, (i + distance) % size) for i in range(siz...  132 us
    ppermute x39, starting transfers between devices, shift_ctx(): lax.ppermute(value, 'ctx', [(i, (i + distance) % size) for i in range(siz...  111 us
    ppermute x14, waiting for transfers between devices, swap_x(): return lax.ppermute(value, 'dp', [(i, i ^ 1) for i in range(4)])  35.2 us
    pallas_call x1, Pallas kernels, hidden_back(): pl.pallas_call(hidden_back_kernel, out_shape=(out, out, out_x), grid=(row...  20.3 us
    unnamed x213, local copies, waits for them, and re-layouts  20.1 us
    ppermute x14, starting transfers between devices, swap_y(): return lax.ppermute(value, 'dp', [(i, i ^ 2) for i in range(4)])  16.4 us
    pallas_call x1, Pallas kernels, pair_terms(): pl.pallas_call(pair_kernel, out_shape=(term, out), grid=(columns // 512,)...  14.7 us
    ppermute x14, waiting for transfers between devices, swap_y(): return lax.ppermute(value, 'dp', [(i, i ^ 2) for i in range(4)])  13.6 us
  transfers between devices with their start and end apart: 80, of which 37 were waited for; matrix products, arithmetic and copies ran while one was open for 15% of the time, Pallas kernels for 10%

profile of v3, /device:TPU:0, one launch (start us, length us, event | category | flops | bytes accessed | tf_op | source)
XLA Modules:
  0.0 515.9 jit_solution(14483687383161631613)
XLA Ops:
  25.7 5.8 %collective-permute-start.10 = (bf16[96,768]{1,0:T(8,128)(2,1)S(1)}, bf16[96,768]{1,0:T(8,128)(2,1)S(1)}, u32[]{:S(2)}, u32[]{:S(2)}) collective-permute-start(bf16[96,768]{1,0:T(8,128)(2,1)S(1)} %convert_element_type.285), channel_id=1, source_target_pairs={{0,6},{2,0},{4,2},{6,4},{1,7},{3,1},{5,3},{7,5},{8,14},{10,8},{12,... | collective-permute-start | bytes 442376 | tf_op jit(solution)/shard_map/ppermute | solution.py:393
  39.5 5.4 %collective-permute-done.9 = bf16[96,768]{1,0:T(8,128)(2,1)S(1)} collective-permute-done((bf16[96,768]{1,0:T(8,128)(2,1)S(1)}, bf16[96,768]{1,0:T(8,128)(2,1)S(1)}, u32[]{:S(2)}, u32[]{:S(2)}) %collective-permute-start.9) | collective-permute-done | bytes 147488 | tf_op jit(solution)/shard_map/ppermute | solution.py:393
  49.2 5.6 %collective-permute-start.11 = (bf16[96,2304]{1,0:T(8,128)(2,1)S(1)}, bf16[96,2304]{1,0:T(8,128)(2,1)S(1)}, u32[]{:S(2)}, u32[]{:S(2)}) collective-permute-start(bf16[96,2304]{1,0:T(8,128)(2,1)S(1)} %get-tuple-element.291), channel_id=1, source_target_pairs={{0,2},{2,4},{4,6},{6,0},{1,3},{3,5},{5,7},{7,1},{8,10},{10,12},{12... | collective-permute-start | bytes 1327112 | tf_op jit(solution)/shard_map/ppermute | solution.py:393
  58.7 6.3 %collective-permute-done.5 = bf16[2,192,1024]{2,1,0:T(8,128)(2,1)S(1)} collective-permute-done((bf16[2,192,1024]{2,1,0:T(8,128)(2,1)S(1)}, bf16[2,192,1024]{2,1,0:T(8,128)(2,1)S(1)}, u32[]{:S(2)}, u32[]{:S(2)}) %collective-permute-start.5) | collective-permute-done | bytes 786464 | tf_op jit(solution)/shard_map/ppermute | solution.py:401
  70.9 9.5 %collective-permute-done.12 = bf16[96,2304]{1,0:T(8,128)(2,1)S(1)} collective-permute-done((bf16[96,2304]{1,0:T(8,128)(2,1)S(1)}, bf16[96,2304]{1,0:T(8,128)(2,1)S(1)}, u32[]{:S(2)}, u32[]{:S(2)}) %collective-permute-start.12) | collective-permute-done | bytes 442400 | tf_op jit(solution)/shard_map/ppermute | solution.py:393
  80.8 11.4 %collective-permute-start.16 = (bf16[2,128,256]{2,1,0:T(8,128)(2,1)S(1)}, bf16[2,128,256]{2,1,0:T(8,128)(2,1)S(1)}, u32[]{:S(2)}, u32[]{:S(2)}) collective-permute-start(bf16[2,128,256]{2,1,0:T(8,128)(2,1)S(1)} %bitcast.419), channel_id=1, source_target_pairs={{0,2},{2,4},{4,6},{6,0},{1,3},{3,5},{5,7},{7,1},{8,10},{10,12},{12... | collective-permute-start | bytes 393224 | tf_op jit(solution)/shard_map/ppermute | solution.py:393
  97.3 3.6 collective-permute-done.17
  101.0 5.1 attend.1.right2_ref
  106.1 3.4 collective-permute-done.20
  119.9 15.4 %collective-permute-done.25 = bf16[192,2304]{1,0:T(8,128)(2,1)S(1)} collective-permute-done((bf16[192,2304]{1,0:T(8,128)(2,1)S(1)}, bf16[192,2304]{1,0:T(8,128)(2,1)S(1)}, u32[]{:S(2)}, u32[]{:S(2)}) %collective-permute-start.25) | collective-permute-done | bytes 884768 | tf_op jit(solution)/shard_map/ppermute | solution.py:397
  136.3 9.6 %collective-permute-done.23 = bf16[2,64,1536]{2,1,0:T(8,128)(2,1)S(1)} collective-permute-done((bf16[2,64,1536]{2,1,0:T(8,128)(2,1)S(1)}, bf16[2,64,1536]{2,1,0:T(8,128)(2,1)S(1)}, u32[]{:S(2)}, u32[]{:S(2)}) %collective-permute-start.23) | collective-permute-done | bytes 393248 | tf_op jit(solution)/shard_map/ppermute | solution.py:393
  149.7 17.9 %collective-permute-start.28 = (bf16[96,1152]{1,0:T(8,128)(2,1)S(1)}, bf16[96,1152]{1,0:T(8,128)(2,1)S(1)}, u32[]{:S(2)}, u32[]{:S(2)}) collective-permute-start(bf16[96,1152]{1,0:T(8,128)(2,1)S(1)} %get-tuple-element.337), channel_id=1, source_target_pairs={{0,2},{2,4},{4,6},{6,0},{1,3},{3,5},{5,7},{7,1},{8,10},{10,12},{12... | collective-permute-start | bytes 663560 | tf_op jit(solution)/shard_map/ppermute | solution.py:393
  170.1 3.7 collective-permute-done.28
  173.8 9.0 %collective-permute-done.29 = bf16[96,1152]{1,0:T(8,128)(2,1)S(1)} collective-permute-done((bf16[96,1152]{1,0:T(8,128)(2,1)S(1)}, bf16[96,1152]{1,0:T(8,128)(2,1)S(1)}, u32[]{:S(2)}, u32[]{:S(2)}) %collective-permute-start.29) | collective-permute-done | bytes 221216 | tf_op jit(solution)/shard_map/ppermute | solution.py:393
  182.9 5.3 %collective-permute-start.35 = (bf16[2,64,1536]{2,1,0:T(8,128)(2,1)S(1)}, bf16[2,64,1536]{2,1,0:T(8,128)(2,1)}, u32[]{:S(2)}, u32[]{:S(2)}) collective-permute-start(bf16[2,64,1536]{2,1,0:T(8,128)(2,1)S(1)} %copy-done.49), channel_id=1, source_target_pairs={{0,2},{2,4},{4,6},{6,0},{1,3},{3,5},{5,7},{7,1},{8,10},{10,12},{12... | collective-permute-start | bytes 1179656 | tf_op jit(solution)/shard_map/ppermute | solution.py:393
  195.2 3.6 pad_maximum_fusion
  198.8 13.1 %hidden_units.1 = (bf16[1024,1152]{1,0:T(8,128)(2,1)S(1)}, bf16[1024,1152]{1,0:T(8,128)(2,1)S(1)}, bf16[1024,1152]{1,0:T(8,128)(2,1)S(1)}) custom-call(bf16[1024,1536]{1,0:T(8,128)(2,1)S(1)} %constant_dynamic-update-slice_fusion.4.x_ref.left_ref, bf16[1536,2304]{1,0:T(8,128)(2,1)} %bitcast.391, bf16[1536,2304]{1,0:T(8,128)(2,1)} %bitcast.392), custom_call_target="tpu_custom_call" | custom-call | flops 7247757312 | bytes 17301504 | tf_op jit(solution)/shard_map/hidden_units/pallas_call | solution.py:218
  225.8 4.9 weight_terms.1
  230.7 8.2 %collective-permute-done.40 = bf16[2,192,1152]{2,1,0:T(8,128)(2,1)S(1)} collective-permute-done((bf16[2,192,1152]{2,1,0:T(8,128)(2,1)S(1)}, bf16[2,192,1152]{2,1,0:T(8,128)(2,1)S(1)}, u32[]{:S(2)}, u32[]{:S(2)}) %collective-permute-start.40) | collective-permute-done | bytes 884768 | tf_op jit(solution)/shard_map/ppermute | solution.py:397
  248.4 20.3 %hidden_back.1 = (bf16[1024,1152]{1,0:T(8,128)(2,1)S(1)}, bf16[1024,1152]{1,0:T(8,128)(2,1)S(1)}, bf16[1024,1536]{1,0:T(8,128)(2,1)}) custom-call(bf16[1024,1536]{1,0:T(8,128)(2,1)} %copy-done.19, bf16[1024,1152]{1,0:T(8,128)(2,1)S(1)} %copy-done.26, bf16[1024,1152]{1,0:T(8,128)(2,1)S(1)} %copy-done.28, bf16[1536,1152]{1,0:T(8,128)(2,1)} %bitcast.403, ...), custom_call_target="tpu_custom_call" | custom-call | flops 10871635968 | bytes 26345472 | tf_op jit(solution)/shard_map/hidden_back/pallas_call | solution.py:265
  284.5 9.1 %collective-permute-start.43 = (bf16[128,1536]{1,0:T(8,128)(2,1)}, bf16[128,1536]{1,0:T(8,128)(2,1)}, u32[]{:S(2)}, u32[]{:S(2)}) collective-permute-start(bf16[128,1536]{1,0:T(8,128)(2,1)} %get-tuple-element.299), channel_id=1, source_target_pairs={{0,6},{2,0},{4,2},{6,4},{1,7},{3,1},{5,3},{7,5},{8,14},{10,8},{12,... | collective-permute-start | bytes 1179656 | tf_op jit(solution)/shard_map/ppermute | solution.py:393
  294.9 14.7 %pair_terms.1 = (bf16[1536,2304]{1,0:T(8,128)(2,1)}, bf16[1024,1536]{1,0:T(8,128)(2,1)S(1)}) custom-call(bf16[1024,1536]{1,0:T(8,128)(2,1)} %copy-done.18, bf16[1024,1152]{1,0:T(8,128)(2,1)S(1)} %copy-done.30, bf16[1024,1152]{1,0:T(8,128)(2,1)S(1)} %copy-done.32, bf16[1024,1152]{1,0:T(8,128)(2,1)S(1)} %copy-done.24, bf16[1536,1152]{1,0:T(8,128)(2,1)} %bitcast.404), custom_call_target="tpu_custom_call" | custom-call | flops 10871635968 | bytes 23986176 | tf_op jit(solution)/shard_map/pair_terms/pallas_call | solution.py:298
  320.7 8.9 %collective-permute-done.44 = bf16[128,1536]{1,0:T(8,128)(2,1)} collective-permute-done((bf16[128,1536]{1,0:T(8,128)(2,1)}, bf16[128,1536]{1,0:T(8,128)(2,1)}, u32[]{:S(2)}, u32[]{:S(2)}) %collective-permute-start.44) | collective-permute-done | bytes 393248 | tf_op jit(solution)/shard_map/ppermute | solution.py:393
  346.6 7.5 %attend_back.1 = (bf16[256,768]{1,0:T(8,128)(2,1)S(1)}, bf16[2,512,256]{2,1,0:T(8,128)(2,1)S(1)}) custom-call(s32[2]{0:T(128)S(1)} %copy-done.22, s32[128,1]{1,0:T(8,128)S(1)} %copy-done.17, s32[1,512]{1,0:T(1,128)S(1)} %bitcast.387, bf16[256,768]{1,0:T(8,128)(2,1)S(1)} %copy-done.15, bf16[2,512,256]{2,1,0:T(8,128)(2,1)S(1)} %copy-done.21, ...), custom_call_target="tpu_custom_call" | custom-call | flops 1006632960 | bytes 2228224 | tf_op jit(solution)/shard_map/attend_back/pallas_call | solution.py:161
  354.1 5.8 %collective-permute-done.52 = bf16[96,1152]{1,0:T(8,128)(2,1)S(1)} collective-permute-done((bf16[96,1152]{1,0:T(8,128)(2,1)}, bf16[96,1152]{1,0:T(8,128)(2,1)S(1)}, u32[]{:S(2)}, u32[]{:S(2)}) %collective-permute-start.52) | collective-permute-done | bytes 221216 | tf_op jit(solution)/shard_map/ppermute | solution.py:393
  360.6 3.9 collective-permute-start.54
  401.1 21.0 %collective-permute-done.58 = bf16[128,1536]{1,0:T(8,128)(2,1)} collective-permute-done((bf16[128,1536]{1,0:T(8,128)(2,1)}, bf16[128,1536]{1,0:T(8,128)(2,1)}, u32[]{:S(2)}, u32[]{:S(2)}) %collective-permute-start.58) | collective-permute-done | bytes 393248 | tf_op jit(solution)/shard_map/ppermute | solution.py:393
  436.7 8.2 %collective-permute-done.69 = bf16[96,2304]{1,0:T(8,128)(2,1)S(1)} collective-permute-done((bf16[96,2304]{1,0:T(8,128)(2,1)S(1)}, bf16[96,2304]{1,0:T(8,128)(2,1)S(1)}, u32[]{:S(2)}, u32[]{:S(2)}) %collective-permute-start.69) | collective-permute-done | bytes 442400 | tf_op jit(solution)/shard_map/ppermute | solution.py:393
  444.9 14.3 %collective-permute-done.73 = bf16[96,2304]{1,0:T(8,128)(2,1)S(1)} collective-permute-done((bf16[96,2304]{1,0:T(8,128)(2,1)S(1)}, bf16[96,2304]{1,0:T(8,128)(2,1)S(1)}, u32[]{:S(2)}, u32[]{:S(2)}) %collective-permute-start.73) | collective-permute-done | bytes 442400 | tf_op jit(solution)/shard_map/ppermute | solution.py:393
  460.1 12.1 %collective-permute-start.70 = (bf16[96,1792]{1,0:T(8,128)(2,1)S(1)}, bf16[96,1792]{1,0:T(8,128)(2,1)S(1)}, u32[]{:S(2)}, u32[]{:S(2)}) collective-permute-start(bf16[96,1792]{1,0:T(8,128)(2,1)S(1)} %get-tuple-element.305), channel_id=1, source_target_pairs={{0,6},{2,0},{4,2},{6,4},{1,7},{3,1},{5,3},{7,5},{8,14},{10,8},{12,... | collective-permute-start | bytes 1032200 | tf_op jit(solution)/shard_map/ppermute | solution.py:393
  472.2 6.1 %collective-permute-done.70 = bf16[96,1792]{1,0:T(8,128)(2,1)S(1)} collective-permute-done((bf16[96,1792]{1,0:T(8,128)(2,1)S(1)}, bf16[96,1792]{1,0:T(8,128)(2,1)S(1)}, u32[]{:S(2)}, u32[]{:S(2)}) %collective-permute-start.70) | collective-permute-done | bytes 344096 | tf_op jit(solution)/shard_map/ppermute | solution.py:393
  487.8 18.0 %collective-permute-done.71 = bf16[96,1792]{1,0:T(8,128)(2,1)S(1)} collective-permute-done((bf16[96,1792]{1,0:T(8,128)(2,1)S(1)}, bf16[96,1792]{1,0:T(8,128)(2,1)S(1)}, u32[]{:S(2)}, u32[]{:S(2)}) %collective-permute-start.71) | collective-permute-done | bytes 344096 | tf_op jit(solution)/shard_map/ppermute | solution.py:393
  (531 shorter events, 216.2 us)
Async XLA Ops:
  13.9 41.1 %collective-permute-start = (bf16[2,64,1536]{2,1,0:T(8,128)(2,1)}, bf16[2,64,1536]{2,1,0:T(8,128)(2,1)}, u32[]{:S(2)}, u32[]{:S(2)}) collective-permute-start(bf16[2,64,1536]{2,1,0:T(8,128)(2,1)} %fusion.5), channel_id=1, source_target_pairs={{0,1},{1,0},{2,3},{3,2},{4,5},{5,4},{6,7},{7,6},{8,9},{9,8},{10,11... | collective-permute-start | bytes 1179656 | tf_op jit(solution)/shard_map/ppermute | solution.py:388
  54.8 25.7 %collective-permute-start.12 = (bf16[96,2304]{1,0:T(8,128)(2,1)S(1)}, bf16[96,2304]{1,0:T(8,128)(2,1)S(1)}, u32[]{:S(2)}, u32[]{:S(2)}) collective-permute-start(bf16[96,2304]{1,0:T(8,128)(2,1)S(1)} %get-tuple-element.290), channel_id=1, source_target_pairs={{0,4},{2,6},{4,0},{6,2},{1,5},{3,7},{5,1},{7,3},{8,12},{10,14},{12... | collective-permute-start | bytes 1327112 | tf_op jit(solution)/shard_map/ppermute | solution.py:393
  55.0 25.5 %collective-permute-start.13 = (bf16[96,2304]{1,0:T(8,128)(2,1)S(1)}, bf16[96,2304]{1,0:T(8,128)(2,1)S(1)}, u32[]{:S(2)}, u32[]{:S(2)}) collective-permute-start(bf16[96,2304]{1,0:T(8,128)(2,1)S(1)} %get-tuple-element.289), channel_id=1, source_target_pairs={{0,6},{2,0},{4,2},{6,4},{1,7},{3,1},{5,3},{7,5},{8,14},{10,8},{12,... | collective-permute-start | bytes 1327112 | tf_op jit(solution)/shard_map/ppermute | solution.py:393
  113.2 22.1 %collective-permute-start.25 = (bf16[192,2304]{1,0:T(8,128)(2,1)S(1)}, bf16[192,2304]{1,0:T(8,128)(2,1)S(1)}, u32[]{:S(2)}, u32[]{:S(2)}) collective-permute-start(bf16[192,2304]{1,0:T(8,128)(2,1)S(1)} %get-tuple-element.142), channel_id=1, source_target_pairs={{0,8},{8,0},{16,24},{24,16},{1,9},{9,1},{17,25},{25,17},{2,10},{10... | collective-permute-start | bytes 2654216 | tf_op jit(solution)/shard_map/ppermute | solution.py:397
  116.1 29.8 %collective-permute-start.23 = (bf16[2,64,1536]{2,1,0:T(8,128)(2,1)S(1)}, bf16[2,64,1536]{2,1,0:T(8,128)(2,1)S(1)}, u32[]{:S(2)}, u32[]{:S(2)}) collective-permute-start(bf16[2,64,1536]{2,1,0:T(8,128)(2,1)S(1)} %multiply_convert_fusion), channel_id=1, source_target_pairs={{0,4},{2,6},{4,0},{6,2},{1,5},{3,7},{5,1},{7,3},{8,12},{10,14},{12... | collective-permute-start | bytes 1179656 | tf_op jit(solution)/shard_map/ppermute | solution.py:393
  118.3 27.6 %collective-permute-start.24 = (bf16[2,64,1536]{2,1,0:T(8,128)(2,1)S(1)}, bf16[2,64,1536]{2,1,0:T(8,128)(2,1)S(1)}, u32[]{:S(2)}, u32[]{:S(2)}) collective-permute-start(bf16[2,64,1536]{2,1,0:T(8,128)(2,1)S(1)} %multiply_convert_fusion), channel_id=1, source_target_pairs={{0,6},{2,0},{4,2},{6,4},{1,7},{3,1},{5,3},{7,5},{8,14},{10,8},{12,... | collective-permute-start | bytes 1179656 | tf_op jit(solution)/shard_map/ppermute | solution.py:393
  146.4 44.6 %collective-permute-start.32 = (bf16[2,192,2304]{2,1,0:T(8,128)(2,1)S(1)}, bf16[2,192,2304]{2,1,0:T(8,128)(2,1)S(1)}, u32[]{:S(2)}, u32[]{:S(2)}) collective-permute-start(bf16[2,192,2304]{2,1,0:T(8,128)(2,1)S(1)} %pad_maximum_fusion.6), channel_id=1, source_target_pairs={{0,8},{8,0},{16,24},{24,16},{1,9},{9,1},{17,25},{25,17},{2,10},{10... | collective-permute-start | bytes 5308424 | tf_op jit(solution)/shard_map/ppermute | solution.py:397
  147.4 43.5 %collective-permute-start.31 = (bf16[2,192,2304]{2,1,0:T(8,128)(2,1)S(1)}, bf16[2,192,2304]{2,1,0:T(8,128)(2,1)S(1)}, u32[]{:S(2)}, u32[]{:S(2)}) collective-permute-start(bf16[2,192,2304]{2,1,0:T(8,128)(2,1)S(1)} %pad_maximum_fusion.5), channel_id=1, source_target_pairs={{0,16},{8,24},{16,0},{24,8},{1,17},{9,25},{17,1},{25,9},{2,18},{10... | collective-permute-start | bytes 5308424 | tf_op jit(solution)/shard_map/ppermute | solution.py:401
  149.7 24.1 %collective-permute-start.28 = (bf16[96,1152]{1,0:T(8,128)(2,1)S(1)}, bf16[96,1152]{1,0:T(8,128)(2,1)S(1)}, u32[]{:S(2)}, u32[]{:S(2)}) collective-permute-start(bf16[96,1152]{1,0:T(8,128)(2,1)S(1)} %get-tuple-element.337), channel_id=1, source_target_pairs={{0,2},{2,4},{4,6},{6,0},{1,3},{3,5},{5,7},{7,1},{8,10},{10,12},{12... | collective-permute-start | bytes 663560 | tf_op jit(solution)/shard_map/ppermute | solution.py:393
  182.9 31.9 %collective-permute-start.35 = (bf16[2,64,1536]{2,1,0:T(8,128)(2,1)S(1)}, bf16[2,64,1536]{2,1,0:T(8,128)(2,1)}, u32[]{:S(2)}, u32[]{:S(2)}) collective-permute-start(bf16[2,64,1536]{2,1,0:T(8,128)(2,1)S(1)} %copy-done.49), channel_id=1, source_target_pairs={{0,2},{2,4},{4,6},{6,0},{1,3},{3,5},{5,7},{7,1},{8,10},{10,12},{12... | collective-permute-start | bytes 1179656 | tf_op jit(solution)/shard_map/ppermute | solution.py:393
  188.1 27.9 %collective-permute-start.36 = (bf16[2,64,1536]{2,1,0:T(8,128)(2,1)S(1)}, bf16[2,64,1536]{2,1,0:T(8,128)(2,1)}, u32[]{:S(2)}, u32[]{:S(2)}) collective-permute-start(bf16[2,64,1536]{2,1,0:T(8,128)(2,1)S(1)} %copy-done.49), channel_id=1, source_target_pairs={{0,4},{2,6},{4,0},{6,2},{1,5},{3,7},{5,1},{7,3},{8,12},{10,14},{12... | collective-permute-start | bytes 1179656 | tf_op jit(solution)/shard_map/ppermute | solution.py:393
  190.6 25.4 %collective-permute-start.37 = (bf16[2,64,1536]{2,1,0:T(8,128)(2,1)S(1)}, bf16[2,64,1536]{2,1,0:T(8,128)(2,1)}, u32[]{:S(2)}, u32[]{:S(2)}) collective-permute-start(bf16[2,64,1536]{2,1,0:T(8,128)(2,1)S(1)} %copy-done.49), channel_id=1, source_target_pairs={{0,6},{2,0},{4,2},{6,4},{1,7},{3,1},{5,3},{7,5},{8,14},{10,8},{12,... | collective-permute-start | bytes 1179656 | tf_op jit(solution)/shard_map/ppermute | solution.py:393
  192.2 23.8 %collective-permute-start.33 = (bf16[192,1152]{1,0:T(8,128)(2,1)S(1)}, bf16[192,1152]{1,0:T(8,128)(2,1)}, u32[]{:S(2)}, u32[]{:S(2)}) collective-permute-start(bf16[192,1152]{1,0:T(8,128)(2,1)S(1)} %get-tuple-element.162), channel_id=1, source_target_pairs={{0,8},{8,0},{16,24},{24,16},{1,9},{9,1},{17,25},{25,17},{2,10},{10... | collective-permute-start | bytes 1327112 | tf_op jit(solution)/shard_map/ppermute | solution.py:397
  193.1 23.0 %collective-permute-start.34 = (bf16[192,1152]{1,0:T(8,128)(2,1)}, bf16[192,1152]{1,0:T(8,128)(2,1)}, u32[]{:S(2)}, u32[]{:S(2)}) collective-permute-start(bf16[192,1152]{1,0:T(8,128)(2,1)} %get-tuple-element.163), channel_id=1, source_target_pairs={{0,16},{8,24},{16,0},{24,8},{1,17},{9,25},{17,1},{25,9},{2,18},{10... | collective-permute-start | bytes 1327112 | tf_op jit(solution)/shard_map/ppermute | solution.py:401
  220.9 22.1 %collective-permute-start.39 = (bf16[2,192,1152]{2,1,0:T(8,128)(2,1)S(1)}, bf16[2,192,1152]{2,1,0:T(8,128)(2,1)S(1)}, u32[]{:S(2)}, u32[]{:S(2)}) collective-permute-start(bf16[2,192,1152]{2,1,0:T(8,128)(2,1)S(1)} %pad_maximum_fusion.13), channel_id=1, source_target_pairs={{0,16},{8,24},{16,0},{24,8},{1,17},{9,25},{17,1},{25,9},{2,18},{10... | collective-permute-start | bytes 2654216 | tf_op jit(solution)/shard_map/ppermute | solution.py:401
  277.6 33.1 %collective-permute-start.46 = (bf16[2,192,1152]{2,1,0:T(8,128)(2,1)S(1)}, bf16[2,192,1152]{2,1,0:T(8,128)(2,1)S(1)}, u32[]{:S(2)}, u32[]{:S(2)}) collective-permute-start(bf16[2,192,1152]{2,1,0:T(8,128)(2,1)S(1)} %get-tuple-element.273), channel_id=1, source_target_pairs={{0,8},{8,0},{16,24},{24,16},{1,9},{9,1},{17,25},{25,17},{2,10},{10... | collective-permute-start | bytes 2654216 | tf_op jit(solution)/shard_map/ppermute | solution.py:397
  280.2 30.6 %collective-permute-start.47 = (bf16[2,192,1152]{2,1,0:T(8,128)(2,1)}, bf16[2,192,1152]{2,1,0:T(8,128)(2,1)}, u32[]{:S(2)}, u32[]{:S(2)}) collective-permute-start(bf16[2,192,1152]{2,1,0:T(8,128)(2,1)} %get-tuple-element.271), channel_id=1, source_target_pairs={{0,16},{8,24},{16,0},{24,8},{1,17},{9,25},{17,1},{25,9},{2,18},{10... | collective-permute-start | bytes 2654216 | tf_op jit(solution)/shard_map/ppermute | solution.py:401
  284.5 34.3 %collective-permute-start.43 = (bf16[128,1536]{1,0:T(8,128)(2,1)}, bf16[128,1536]{1,0:T(8,128)(2,1)}, u32[]{:S(2)}, u32[]{:S(2)}) collective-permute-start(bf16[128,1536]{1,0:T(8,128)(2,1)} %get-tuple-element.299), channel_id=1, source_target_pairs={{0,6},{2,0},{4,2},{6,4},{1,7},{3,1},{5,3},{7,5},{8,14},{10,8},{12,... | collective-permute-start | bytes 1179656 | tf_op jit(solution)/shard_map/ppermute | solution.py:393
  293.6 36.1 %collective-permute-start.44 = (bf16[128,1536]{1,0:T(8,128)(2,1)}, bf16[128,1536]{1,0:T(8,128)(2,1)}, u32[]{:S(2)}, u32[]{:S(2)}) collective-permute-start(bf16[128,1536]{1,0:T(8,128)(2,1)} %get-tuple-element.298), channel_id=1, source_target_pairs={{0,4},{2,6},{4,0},{6,2},{1,5},{3,7},{5,1},{7,3},{8,12},{10,14},{12... | collective-permute-start | bytes 1179656 | tf_op jit(solution)/shard_map/ppermute | solution.py:393
  294.8 35.7 %collective-permute-start.45 = (bf16[128,1536]{1,0:T(8,128)(2,1)}, bf16[128,1536]{1,0:T(8,128)(2,1)}, u32[]{:S(2)}, u32[]{:S(2)}) collective-permute-start(bf16[128,1536]{1,0:T(8,128)(2,1)} %get-tuple-element.297), channel_id=1, source_target_pairs={{0,2},{2,4},{4,6},{6,0},{1,3},{3,5},{5,7},{7,1},{8,10},{10,12},{12... | collective-permute-start | bytes 1179656 | tf_op jit(solution)/shard_map/ppermute | solution.py:393
  329.7 39.9 %collective-permute-start.60 = (bf16[2,192,2304]{2,1,0:T(8,128)(2,1)S(1)}, bf16[2,192,2304]{2,1,0:T(8,128)(2,1)S(1)}, u32[]{:S(2)}, u32[]{:S(2)}) collective-permute-start(bf16[2,192,2304]{2,1,0:T(8,128)(2,1)S(1)} %get-tuple-element.252), channel_id=1, source_target_pairs={{0,8},{8,0},{16,24},{24,16},{1,9},{9,1},{17,25},{25,17},{2,10},{10... | collective-permute-start | bytes 5308424 | tf_op jit(solution)/shard_map/ppermute | solution.py:397
  330.6 39.4 %collective-permute-start.61 = (bf16[2,192,2304]{2,1,0:T(8,128)(2,1)S(1)}, bf16[2,192,2304]{2,1,0:T(8,128)(2,1)S(1)}, u32[]{:S(2)}, u32[]{:S(2)}) collective-permute-start(bf16[2,192,2304]{2,1,0:T(8,128)(2,1)S(1)} %get-tuple-element.250), channel_id=1, source_target_pairs={{0,16},{8,24},{16,0},{24,8},{1,17},{9,25},{17,1},{25,9},{2,18},{10... | collective-permute-start | bytes 5308424 | tf_op jit(solution)/shard_map/ppermute | solution.py:401
  386.5 35.7 %collective-permute-start.58 = (bf16[128,1536]{1,0:T(8,128)(2,1)}, bf16[128,1536]{1,0:T(8,128)(2,1)}, u32[]{:S(2)}, u32[]{:S(2)}) collective-permute-start(bf16[128,1536]{1,0:T(8,128)(2,1)} %get-tuple-element.206), channel_id=1, source_target_pairs={{0,4},{2,6},{4,0},{6,2},{1,5},{3,7},{5,1},{7,3},{8,12},{10,14},{12... | collective-permute-start | bytes 1179656 | tf_op jit(solution)/shard_map/ppermute | solution.py:393
  387.5 34.7 %collective-permute-start.59 = (bf16[128,1536]{1,0:T(8,128)(2,1)}, bf16[128,1536]{1,0:T(8,128)(2,1)S(1)}, u32[]{:S(2)}, u32[]{:S(2)}) collective-permute-start(bf16[128,1536]{1,0:T(8,128)(2,1)} %get-tuple-element.207), channel_id=1, source_target_pairs={{0,2},{2,4},{4,6},{6,0},{1,3},{3,5},{5,7},{7,1},{8,10},{10,12},{12... | collective-permute-start | bytes 1179656 | tf_op jit(solution)/shard_map/ppermute | solution.py:393
  398.5 29.3 %collective-permute-start.65 = (bf16[2,192,1792]{2,1,0:T(8,128)(2,1)S(1)}, bf16[2,192,1792]{2,1,0:T(8,128)(2,1)S(1)}, u32[]{:S(2)}, u32[]{:S(2)}) collective-permute-start(bf16[2,192,1792]{2,1,0:T(8,128)(2,1)S(1)} %get-tuple-element.266), channel_id=1, source_target_pairs={{0,8},{8,0},{16,24},{24,16},{1,9},{9,1},{17,25},{25,17},{2,10},{10... | collective-permute-start | bytes 4128776 | tf_op jit(solution)/shard_map/ppermute | solution.py:397
  399.6 29.3 %collective-permute-start.66 = (bf16[2,192,1792]{2,1,0:T(8,128)(2,1)S(1)}, bf16[2,192,1792]{2,1,0:T(8,128)(2,1)S(1)}, u32[]{:S(2)}, u32[]{:S(2)}) collective-permute-start(bf16[2,192,1792]{2,1,0:T(8,128)(2,1)S(1)} %get-tuple-element.264), channel_id=1, source_target_pairs={{0,16},{8,24},{16,0},{24,8},{1,17},{9,25},{17,1},{25,9},{2,18},{10... | collective-permute-start | bytes 4128776 | tf_op jit(solution)/shard_map/ppermute | solution.py:401
  431.4 27.9 %collective-permute-start.73 = (bf16[96,2304]{1,0:T(8,128)(2,1)S(1)}, bf16[96,2304]{1,0:T(8,128)(2,1)S(1)}, u32[]{:S(2)}, u32[]{:S(2)}) collective-permute-start(bf16[96,2304]{1,0:T(8,128)(2,1)S(1)} %get-tuple-element.269), channel_id=1, source_target_pairs={{0,4},{2,6},{4,0},{6,2},{1,5},{3,7},{5,1},{7,3},{8,12},{10,14},{12... | collective-permute-start | bytes 1327112 | tf_op jit(solution)/shard_map/ppermute | solution.py:393
  433.3 26.0 %collective-permute-start.74 = (bf16[96,2304]{1,0:T(8,128)(2,1)S(1)}, bf16[96,2304]{1,0:T(8,128)(2,1)S(1)}, u32[]{:S(2)}, u32[]{:S(2)}) collective-permute-start(bf16[96,2304]{1,0:T(8,128)(2,1)S(1)} %get-tuple-element.268), channel_id=1, source_target_pairs={{0,6},{2,0},{4,2},{6,4},{1,7},{3,1},{5,3},{7,5},{8,14},{10,8},{12,... | collective-permute-start | bytes 1327112 | tf_op jit(solution)/shard_map/ppermute | solution.py:393
  435.2 24.4 %collective-permute-start.68 = (bf16[192,1792]{1,0:T(8,128)(2,1)S(1)}, bf16[192,1792]{1,0:T(8,128)(2,1)S(1)}, u32[]{:S(2)}, u32[]{:S(2)}) collective-permute-start(bf16[192,1792]{1,0:T(8,128)(2,1)S(1)} %get-tuple-element.308), channel_id=1, source_target_pairs={{0,8},{8,0},{16,24},{24,16},{1,9},{9,1},{17,25},{25,17},{2,10},{10... | collective-permute-start | bytes 2064392 | tf_op jit(solution)/shard_map/ppermute | solution.py:397
  435.6 24.0 %collective-permute-start.67 = (bf16[192,1792]{1,0:T(8,128)(2,1)S(1)}, bf16[192,1792]{1,0:T(8,128)(2,1)S(1)}, u32[]{:S(2)}, u32[]{:S(2)}) collective-permute-start(bf16[192,1792]{1,0:T(8,128)(2,1)S(1)} %get-tuple-element.310), channel_id=1, source_target_pairs={{0,16},{8,24},{16,0},{24,8},{1,17},{9,25},{17,1},{25,9},{2,18},{10... | collective-permute-start | bytes 2064392 | tf_op jit(solution)/shard_map/ppermute | solution.py:401
  479.7 26.1 %collective-permute-start.71 = (bf16[96,1792]{1,0:T(8,128)(2,1)S(1)}, bf16[96,1792]{1,0:T(8,128)(2,1)S(1)}, u32[]{:S(2)}, u32[]{:S(2)}) collective-permute-start(bf16[96,1792]{1,0:T(8,128)(2,1)S(1)} %get-tuple-element.307), channel_id=1, source_target_pairs={{0,4},{2,6},{4,0},{6,2},{1,5},{3,7},{5,1},{7,3},{8,12},{10,14},{12... | collective-permute-start | bytes 1032200 | tf_op jit(solution)/shard_map/ppermute | solution.py:393
  480.4 25.4 %collective-permute-start.72 = (bf16[96,1792]{1,0:T(8,128)(2,1)S(1)}, bf16[96,1792]{1,0:T(8,128)(2,1)S(1)}, u32[]{:S(2)}, u32[]{:S(2)}) collective-permute-start(bf16[96,1792]{1,0:T(8,128)(2,1)S(1)} %get-tuple-element.306), channel_id=1, source_target_pairs={{0,2},{2,4},{4,6},{6,0},{1,3},{3,5},{5,7},{7,1},{8,10},{10,12},{12... | collective-permute-start | bytes 1032200 | tf_op jit(solution)/shard_map/ppermute | solution.py:393
  (147 other events, 1265.7 us)

commit v4 on v3

--- a/solution.py
+++ b/solution.py
@@ -26,7 +26,7 @@
     return (jnp.cos(angles)[:, None, :], jnp.sin(angles)[:, None, :])
 
 
-VMEM_LIMIT = 44 * 1024 * 1024
+VMEM_LIMIT = 32 * 1024 * 1024
 
 
 def params():
@@ -705,7 +705,7 @@
     )
     sums = jnp.concatenate([gain_attn, gain_mlp, place_query, place_key, place_value])
     attn_terms = ctx_terms(scatter_whole(*after(attn_sums, pair_grads[1])))
-    sums = after(sums, attn_terms[1]).reshape(-1, 128)
+    sums = after(sums, pair_grads[1]).reshape(-1, 128)
     sums = sum_everywhere(sums + swap_tensor(sums)).reshape(-1)
     splits = [model_width, 2 * model_width]
     splits += [splits[1] + b_query.shape[0], splits[1] + b_query.shape[0] + b_key.shape[0]]

time: 523 us -> 514 us (0.983)
  local copies, waits for them, and re-layouts: 45.2 us -> 36.4 us
    ppermute x39, starting transfers between devices: 111 us -> 98.7 us  [shift_ctx(): lax.ppermute(value, 'ctx', [(i, (i + distance) % size) for i in range(siz...]
    ppermute x4, starting transfers between devices: 1.99 us -> 13.5 us  [sum_everywhere(): lax.ppermute(value, axis, [(i, i ^ bit) for i in range(size)])]
    unnamed x213 -> x199, local copies, waits for them, and re-layouts: 20.1 us -> 14.3 us
where the time goes in v4:
time: 514 us; the launch traced here: 506 us
  waiting for transfers between devices  193 us (38%)
  starting transfers between devices  144 us (28%)
  Pallas kernels  66.6 us (13%)
  other arithmetic  60.7 us (12%)
  local copies, waits for them, and re-layouts  36.4 us (7%)
    ppermute x39, waiting for transfers between devices, shift_ctx(): lax.ppermute(value, 'ctx', [(i, (i + distance) % size) for i in range(siz...  134 us
    ppermute x39, starting transfers between devices, shift_ctx(): lax.ppermute(value, 'ctx', [(i, (i + distance) % size) for i in range(siz...  98.7 us
    ppermute x14, waiting for transfers between devices, swap_x(): return lax.ppermute(value, 'dp', [(i, i ^ 1) for i in range(4)])  35.7 us
    pallas_call x1, Pallas kernels, hidden_back(): pl.pallas_call(hidden_back_kernel, out_shape=(out, out, out_x), grid=(row...  18.4 us
    ppermute x14, starting transfers between devices, swap_y(): return lax.ppermute(value, 'dp', [(i, i ^ 2) for i in range(4)])  17.6 us
    ppermute x14, waiting for transfers between devices, swap_y(): return lax.ppermute(value, 'dp', [(i, i ^ 2) for i in range(4)])  14.5 us
    unnamed x199, local copies, waits for them, and re-layouts  14.3 us
    pallas_call x1, Pallas kernels, pair_terms(): pl.pallas_call(pair_kernel, out_shape=(term, out), grid=(columns // 512,)...  14 us
  transfers between devices with their start and end apart: 80, of which 37 were waited for; matrix products, arithmetic and copies ran while one was open for 15% of the time, Pallas kernels for 10%

profile of v4, /device:TPU:0, one launch (start us, length us, event | category | flops | bytes accessed | tf_op | source)
XLA Modules:
  0.0 506.3 jit_solution(904349627374424050)
XLA Ops:
  24.1 5.8 %collective-permute-start.10 = (bf16[96,768]{1,0:T(8,128)(2,1)S(1)}, bf16[96,768]{1,0:T(8,128)(2,1)S(1)}, u32[]{:S(2)}, u32[]{:S(2)}) collective-permute-start(bf16[96,768]{1,0:T(8,128)(2,1)S(1)} %convert_element_type.285), channel_id=1, source_target_pairs={{0,6},{2,0},{4,2},{6,4},{1,7},{3,1},{5,3},{7,5},{8,14},{10,8},{12,... | collective-permute-start | bytes 442376 | tf_op jit(solution)/shard_map/ppermute | solution.py:393
  37.9 5.4 %collective-permute-done.9 = bf16[96,768]{1,0:T(8,128)(2,1)S(1)} collective-permute-done((bf16[96,768]{1,0:T(8,128)(2,1)S(1)}, bf16[96,768]{1,0:T(8,128)(2,1)S(1)}, u32[]{:S(2)}, u32[]{:S(2)}) %collective-permute-start.9) | collective-permute-done | bytes 147488 | tf_op jit(solution)/shard_map/ppermute | solution.py:393
  47.6 5.6 %collective-permute-start.11 = (bf16[96,2304]{1,0:T(8,128)(2,1)S(1)}, bf16[96,2304]{1,0:T(8,128)(2,1)S(1)}, u32[]{:S(2)}, u32[]{:S(2)}) collective-permute-start(bf16[96,2304]{1,0:T(8,128)(2,1)S(1)} %get-tuple-element.291), channel_id=1, source_target_pairs={{0,2},{2,4},{4,6},{6,0},{1,3},{3,5},{5,7},{7,1},{8,10},{10,12},{12... | collective-permute-start | bytes 1327112 | tf_op jit(solution)/shard_map/ppermute | solution.py:393
  57.1 6.4 %collective-permute-done.5 = bf16[2,192,1024]{2,1,0:T(8,128)(2,1)S(1)} collective-permute-done((bf16[2,192,1024]{2,1,0:T(8,128)(2,1)S(1)}, bf16[2,192,1024]{2,1,0:T(8,128)(2,1)S(1)}, u32[]{:S(2)}, u32[]{:S(2)}) %collective-permute-start.5) | collective-permute-done | bytes 786464 | tf_op jit(solution)/shard_map/ppermute | solution.py:401
  69.3 9.5 %collective-permute-done.12 = bf16[96,2304]{1,0:T(8,128)(2,1)S(1)} collective-permute-done((bf16[96,2304]{1,0:T(8,128)(2,1)S(1)}, bf16[96,2304]{1,0:T(8,128)(2,1)S(1)}, u32[]{:S(2)}, u32[]{:S(2)}) %collective-permute-start.12) | collective-permute-done | bytes 442400 | tf_op jit(solution)/shard_map/ppermute | solution.py:393
  79.1 11.4 %collective-permute-start.16 = (bf16[2,128,256]{2,1,0:T(8,128)(2,1)S(1)}, bf16[2,128,256]{2,1,0:T(8,128)(2,1)S(1)}, u32[]{:S(2)}, u32[]{:S(2)}) collective-permute-start(bf16[2,128,256]{2,1,0:T(8,128)(2,1)S(1)} %bitcast.419), channel_id=1, source_target_pairs={{0,2},{2,4},{4,6},{6,0},{1,3},{3,5},{5,7},{7,1},{8,10},{10,12},{12... | collective-permute-start | bytes 393224 | tf_op jit(solution)/shard_map/ppermute | solution.py:393
  95.7 3.6 collective-permute-done.17
  99.4 5.0 attend.1.right2_ref
  118.3 15.4 %collective-permute-done.25 = bf16[192,2304]{1,0:T(8,128)(2,1)S(1)} collective-permute-done((bf16[192,2304]{1,0:T(8,128)(2,1)S(1)}, bf16[192,2304]{1,0:T(8,128)(2,1)S(1)}, u32[]{:S(2)}, u32[]{:S(2)}) %collective-permute-start.25) | collective-permute-done | bytes 884768 | tf_op jit(solution)/shard_map/ppermute | solution.py:397
  134.6 9.7 %collective-permute-done.23 = bf16[2,64,1536]{2,1,0:T(8,128)(2,1)S(1)} collective-permute-done((bf16[2,64,1536]{2,1,0:T(8,128)(2,1)S(1)}, bf16[2,64,1536]{2,1,0:T(8,128)(2,1)S(1)}, u32[]{:S(2)}, u32[]{:S(2)}) %collective-permute-start.23) | collective-permute-done | bytes 393248 | tf_op jit(solution)/shard_map/ppermute | solution.py:393
  148.1 18.2 %collective-permute-start.28 = (bf16[96,1152]{1,0:T(8,128)(2,1)S(1)}, bf16[96,1152]{1,0:T(8,128)(2,1)S(1)}, u32[]{:S(2)}, u32[]{:S(2)}) collective-permute-start(bf16[96,1152]{1,0:T(8,128)(2,1)S(1)} %get-tuple-element.337), channel_id=1, source_target_pairs={{0,2},{2,4},{4,6},{6,0},{1,3},{3,5},{5,7},{7,1},{8,10},{10,12},{12... | collective-permute-start | bytes 663560 | tf_op jit(solution)/shard_map/ppermute | solution.py:393
  168.7 3.7 collective-permute-done.28
  172.4 9.0 %collective-permute-done.29 = bf16[96,1152]{1,0:T(8,128)(2,1)S(1)} collective-permute-done((bf16[96,1152]{1,0:T(8,128)(2,1)S(1)}, bf16[96,1152]{1,0:T(8,128)(2,1)S(1)}, u32[]{:S(2)}, u32[]{:S(2)}) %collective-permute-start.29) | collective-permute-done | bytes 221216 | tf_op jit(solution)/shard_map/ppermute | solution.py:393
  181.5 5.3 %collective-permute-start.35 = (bf16[2,64,1536]{2,1,0:T(8,128)(2,1)S(1)}, bf16[2,64,1536]{2,1,0:T(8,128)(2,1)}, u32[]{:S(2)}, u32[]{:S(2)}) collective-permute-start(bf16[2,64,1536]{2,1,0:T(8,128)(2,1)S(1)} %copy-done.51), channel_id=1, source_target_pairs={{0,2},{2,4},{4,6},{6,0},{1,3},{3,5},{5,7},{7,1},{8,10},{10,12},{12... | collective-permute-start | bytes 1179656 | tf_op jit(solution)/shard_map/ppermute | solution.py:393
  197.5 3.9 pad_maximum_fusion
  201.5 12.2 %hidden_units.1 = (bf16[1024,1152]{1,0:T(8,128)(2,1)S(1)}, bf16[1024,1152]{1,0:T(8,128)(2,1)S(1)}, bf16[1024,1152]{1,0:T(8,128)(2,1)S(1)}) custom-call(bf16[1024,1536]{1,0:T(8,128)(2,1)S(1)} %copy-done.24, bf16[1536,2304]{1,0:T(8,128)(2,1)S(1)} %bitcast.376, bf16[1536,2304]{1,0:T(8,128)(2,1)S(1)} %bitcast.377), custom_call_target="tpu_custom_call" | custom-call | flops 7247757312 | bytes 17301504 | tf_op jit(solution)/shard_map/hidden_units/pallas_call | solution.py:218
  224.4 4.9 weight_terms.1
  229.4 8.3 %collective-permute-done.40 = bf16[2,192,1152]{2,1,0:T(8,128)(2,1)S(1)} collective-permute-done((bf16[2,192,1152]{2,1,0:T(8,128)(2,1)S(1)}, bf16[2,192,1152]{2,1,0:T(8,128)(2,1)S(1)}, u32[]{:S(2)}, u32[]{:S(2)}) %collective-permute-start.40) | collective-permute-done | bytes 884768 | tf_op jit(solution)/shard_map/ppermute | solution.py:397
  237.6 4.1 collective-permute-done.39
  242.8 18.4 %hidden_back.1 = (bf16[1024,1152]{1,0:T(8,128)(2,1)S(1)}, bf16[1024,1152]{1,0:T(8,128)(2,1)S(1)}, bf16[1024,1536]{1,0:T(8,128)(2,1)S(1)}) custom-call(bf16[1024,1536]{1,0:T(8,128)(2,1)S(1)} %constant_dynamic-update-slice_fusion.9.left_ref.dy_ref, bf16[1024,1152]{1,0:T(8,128)(2,1)S(1)} %get-tuple-element.168.silu_ref, ...), custom_call_target="tpu_custom_call" | custom-call | flops 10871635968 | bytes 26345472 | tf_op jit(solution)/shard_map/hidden_back/pallas_call | solution.py:265
  274.6 9.1 %collective-permute-start.43 = (bf16[128,1536]{1,0:T(8,128)(2,1)}, bf16[128,1536]{1,0:T(8,128)(2,1)}, u32[]{:S(2)}, u32[]{:S(2)}) collective-permute-start(bf16[128,1536]{1,0:T(8,128)(2,1)} %get-tuple-element.299), channel_id=1, source_target_pairs={{0,6},{2,0},{4,2},{6,4},{1,7},{3,1},{5,3},{7,5},{8,14},{10,8},{12,... | collective-permute-start | bytes 1179656 | tf_op jit(solution)/shard_map/ppermute | solution.py:393
  285.0 14.0 %pair_terms.1 = (bf16[1536,2304]{1,0:T(8,128)(2,1)}, bf16[1024,1536]{1,0:T(8,128)(2,1)S(1)}) custom-call(bf16[1024,1536]{1,0:T(8,128)(2,1)S(1)} %copy-done.25, bf16[1024,1152]{1,0:T(8,128)(2,1)S(1)} %copy-done.32, bf16[1024,1152]{1,0:T(8,128)(2,1)S(1)} %copy-done.34, bf16[1024,1152]{1,0:T(8,128)(2,1)S(1)} %copy-done.30, bf16[1536,1152]{1,0:T(8,128)(2,1)S(1)} %bitcast.384), custom_call_target="tpu_custom_call" | custom-call | flops 10871635968 | bytes 23986176 | tf_op jit(solution)/shard_map/pair_terms/pallas_call | solution.py:298
  309.1 10.7 %collective-permute-done.44 = bf16[128,1536]{1,0:T(8,128)(2,1)} collective-permute-done((bf16[128,1536]{1,0:T(8,128)(2,1)}, bf16[128,1536]{1,0:T(8,128)(2,1)}, u32[]{:S(2)}, u32[]{:S(2)}) %collective-permute-start.44) | collective-permute-done | bytes 393248 | tf_op jit(solution)/shard_map/ppermute | solution.py:393
  336.0 7.5 %attend_back.1 = (bf16[256,768]{1,0:T(8,128)(2,1)S(1)}, bf16[2,512,256]{2,1,0:T(8,128)(2,1)S(1)}) custom-call(s32[2]{0:T(128)S(1)} %copy-done.28, s32[128,1]{1,0:T(8,128)S(1)} %copy-done.22, s32[1,512]{1,0:T(1,128)S(1)} %bitcast.393, bf16[256,768]{1,0:T(8,128)(2,1)S(1)} %copy-done.20, bf16[2,512,256]{2,1,0:T(8,128)(2,1)S(1)} %copy-done.27, ...), custom_call_target="tpu_custom_call" | custom-call | flops 1006632960 | bytes 2228224 | tf_op jit(solution)/shard_map/attend_back/pallas_call | solution.py:161
  343.5 5.6 %collective-permute-done.52 = bf16[96,1152]{1,0:T(8,128)(2,1)S(1)} collective-permute-done((bf16[96,1152]{1,0:T(8,128)(2,1)S(1)}, bf16[96,1152]{1,0:T(8,128)(2,1)S(1)}, u32[]{:S(2)}, u32[]{:S(2)}) %collective-permute-start.52) | collective-permute-done | bytes 221216 | tf_op jit(solution)/shard_map/ppermute | solution.py:393
  349.9 3.9 collective-permute-start.54
  391.5 21.3 %collective-permute-done.58 = bf16[128,1536]{1,0:T(8,128)(2,1)} collective-permute-done((bf16[128,1536]{1,0:T(8,128)(2,1)}, bf16[128,1536]{1,0:T(8,128)(2,1)}, u32[]{:S(2)}, u32[]{:S(2)}) %collective-permute-start.58) | collective-permute-done | bytes 393248 | tf_op jit(solution)/shard_map/ppermute | solution.py:393
  426.8 8.2 %collective-permute-done.69 = bf16[96,2304]{1,0:T(8,128)(2,1)S(1)} collective-permute-done((bf16[96,2304]{1,0:T(8,128)(2,1)S(1)}, bf16[96,2304]{1,0:T(8,128)(2,1)S(1)}, u32[]{:S(2)}, u32[]{:S(2)}) %collective-permute-start.69) | collective-permute-done | bytes 442400 | tf_op jit(solution)/shard_map/ppermute | solution.py:393
  434.9 15.4 %collective-permute-done.73 = bf16[96,2304]{1,0:T(8,128)(2,1)S(1)} collective-permute-done((bf16[96,2304]{1,0:T(8,128)(2,1)S(1)}, bf16[96,2304]{1,0:T(8,128)(2,1)S(1)}, u32[]{:S(2)}, u32[]{:S(2)}) %collective-permute-start.73) | collective-permute-done | bytes 442400 | tf_op jit(solution)/shard_map/ppermute | solution.py:393
  458.3 9.9 %collective-permute-start.78 = (f32[40,128]{1,0:T(8,128)S(1)}, f32[40,128]{1,0:T(8,128)S(1)}, u32[]{:S(2)}, u32[]{:S(2)}) collective-permute-start(f32[40,128]{1,0:T(8,128)S(1)} %add.478), channel_id=1, source_target_pairs={{0,2},{2,0},{4,6},{6,4},{1,3},{3,1},{5,7},{7,5},{8,10},{10,8},{12,... | collective-permute-start | bytes 61448 | tf_op jit(solution)/shard_map/ppermute | solution.py:526
  480.2 5.2 %collective-permute-done.70 = bf16[96,1792]{1,0:T(8,128)(2,1)S(1)} collective-permute-done((bf16[96,1792]{1,0:T(8,128)(2,1)S(1)}, bf16[96,1792]{1,0:T(8,128)(2,1)S(1)}, u32[]{:S(2)}, u32[]{:S(2)}) %collective-permute-start.70) | collective-permute-done | bytes 344096 | tf_op jit(solution)/shard_map/ppermute | solution.py:393
  485.4 19.0 %collective-permute-done.71 = bf16[96,1792]{1,0:T(8,128)(2,1)S(1)} collective-permute-done((bf16[96,1792]{1,0:T(8,128)(2,1)S(1)}, bf16[96,1792]{1,0:T(8,128)(2,1)S(1)}, u32[]{:S(2)}, u32[]{:S(2)}) %collective-permute-start.71) | collective-permute-done | bytes 344096 | tf_op jit(solution)/shard_map/ppermute | solution.py:393
  (517 shorter events, 207.6 us)
Async XLA Ops:
  13.9 39.5 %collective-permute-start = (bf16[2,64,1536]{2,1,0:T(8,128)(2,1)}, bf16[2,64,1536]{2,1,0:T(8,128)(2,1)}, u32[]{:S(2)}, u32[]{:S(2)}) collective-permute-start(bf16[2,64,1536]{2,1,0:T(8,128)(2,1)} %fusion.5), channel_id=1, source_target_pairs={{0,1},{1,0},{2,3},{3,2},{4,5},{5,4},{6,7},{7,6},{8,9},{9,8},{10,11... | collective-permute-start | bytes 1179656 | tf_op jit(solution)/shard_map/ppermute | solution.py:388
  53.2 25.7 %collective-permute-start.12 = (bf16[96,2304]{1,0:T(8,128)(2,1)S(1)}, bf16[96,2304]{1,0:T(8,128)(2,1)S(1)}, u32[]{:S(2)}, u32[]{:S(2)}) collective-permute-start(bf16[96,2304]{1,0:T(8,128)(2,1)S(1)} %get-tuple-element.290), channel_id=1, source_target_pairs={{0,4},{2,6},{4,0},{6,2},{1,5},{3,7},{5,1},{7,3},{8,12},{10,14},{12... | collective-permute-start | bytes 1327112 | tf_op jit(solution)/shard_map/ppermute | solution.py:393
  53.4 25.5 %collective-permute-start.13 = (bf16[96,2304]{1,0:T(8,128)(2,1)S(1)}, bf16[96,2304]{1,0:T(8,128)(2,1)S(1)}, u32[]{:S(2)}, u32[]{:S(2)}) collective-permute-start(bf16[96,2304]{1,0:T(8,128)(2,1)S(1)} %get-tuple-element.289), channel_id=1, source_target_pairs={{0,6},{2,0},{4,2},{6,4},{1,7},{3,1},{5,3},{7,5},{8,14},{10,8},{12,... | collective-permute-start | bytes 1327112 | tf_op jit(solution)/shard_map/ppermute | solution.py:393
  111.6 22.1 %collective-permute-start.25 = (bf16[192,2304]{1,0:T(8,128)(2,1)S(1)}, bf16[192,2304]{1,0:T(8,128)(2,1)S(1)}, u32[]{:S(2)}, u32[]{:S(2)}) collective-permute-start(bf16[192,2304]{1,0:T(8,128)(2,1)S(1)} %get-tuple-element.142), channel_id=1, source_target_pairs={{0,8},{8,0},{16,24},{24,16},{1,9},{9,1},{17,25},{25,17},{2,10},{10... | collective-permute-start | bytes 2654216 | tf_op jit(solution)/shard_map/ppermute | solution.py:397
  114.5 29.8 %collective-permute-start.23 = (bf16[2,64,1536]{2,1,0:T(8,128)(2,1)S(1)}, bf16[2,64,1536]{2,1,0:T(8,128)(2,1)S(1)}, u32[]{:S(2)}, u32[]{:S(2)}) collective-permute-start(bf16[2,64,1536]{2,1,0:T(8,128)(2,1)S(1)} %multiply_convert_fusion), channel_id=1, source_target_pairs={{0,4},{2,6},{4,0},{6,2},{1,5},{3,7},{5,1},{7,3},{8,12},{10,14},{12... | collective-permute-start | bytes 1179656 | tf_op jit(solution)/shard_map/ppermute | solution.py:393
  116.7 27.6 %collective-permute-start.24 = (bf16[2,64,1536]{2,1,0:T(8,128)(2,1)S(1)}, bf16[2,64,1536]{2,1,0:T(8,128)(2,1)S(1)}, u32[]{:S(2)}, u32[]{:S(2)}) collective-permute-start(bf16[2,64,1536]{2,1,0:T(8,128)(2,1)S(1)} %multiply_convert_fusion), channel_id=1, source_target_pairs={{0,6},{2,0},{4,2},{6,4},{1,7},{3,1},{5,3},{7,5},{8,14},{10,8},{12,... | collective-permute-start | bytes 1179656 | tf_op jit(solution)/shard_map/ppermute | solution.py:393
  144.7 44.9 %collective-permute-start.32 = (bf16[2,192,2304]{2,1,0:T(8,128)(2,1)S(1)}, bf16[2,192,2304]{2,1,0:T(8,128)(2,1)S(1)}, u32[]{:S(2)}, u32[]{:S(2)}) collective-permute-start(bf16[2,192,2304]{2,1,0:T(8,128)(2,1)S(1)} %pad_maximum_fusion.6), channel_id=1, source_target_pairs={{0,8},{8,0},{16,24},{24,16},{1,9},{9,1},{17,25},{25,17},{2,10},{10... | collective-permute-start | bytes 5308424 | tf_op jit(solution)/shard_map/ppermute | solution.py:397
  145.7 43.9 %collective-permute-start.31 = (bf16[2,192,2304]{2,1,0:T(8,128)(2,1)S(1)}, bf16[2,192,2304]{2,1,0:T(8,128)(2,1)S(1)}, u32[]{:S(2)}, u32[]{:S(2)}) collective-permute-start(bf16[2,192,2304]{2,1,0:T(8,128)(2,1)S(1)} %pad_maximum_fusion.5), channel_id=1, source_target_pairs={{0,16},{8,24},{16,0},{24,8},{1,17},{9,25},{17,1},{25,9},{2,18},{10... | collective-permute-start | bytes 5308424 | tf_op jit(solution)/shard_map/ppermute | solution.py:401
  148.1 24.4 %collective-permute-start.28 = (bf16[96,1152]{1,0:T(8,128)(2,1)S(1)}, bf16[96,1152]{1,0:T(8,128)(2,1)S(1)}, u32[]{:S(2)}, u32[]{:S(2)}) collective-permute-start(bf16[96,1152]{1,0:T(8,128)(2,1)S(1)} %get-tuple-element.337), channel_id=1, source_target_pairs={{0,2},{2,4},{4,6},{6,0},{1,3},{3,5},{5,7},{7,1},{8,10},{10,12},{12... | collective-permute-start | bytes 663560 | tf_op jit(solution)/shard_map/ppermute | solution.py:393
  181.5 32.2 %collective-permute-start.35 = (bf16[2,64,1536]{2,1,0:T(8,128)(2,1)S(1)}, bf16[2,64,1536]{2,1,0:T(8,128)(2,1)}, u32[]{:S(2)}, u32[]{:S(2)}) collective-permute-start(bf16[2,64,1536]{2,1,0:T(8,128)(2,1)S(1)} %copy-done.51), channel_id=1, source_target_pairs={{0,2},{2,4},{4,6},{6,0},{1,3},{3,5},{5,7},{7,1},{8,10},{10,12},{12... | collective-permute-start | bytes 1179656 | tf_op jit(solution)/shard_map/ppermute | solution.py:393
  186.8 28.0 %collective-permute-start.36 = (bf16[2,64,1536]{2,1,0:T(8,128)(2,1)S(1)}, bf16[2,64,1536]{2,1,0:T(8,128)(2,1)}, u32[]{:S(2)}, u32[]{:S(2)}) collective-permute-start(bf16[2,64,1536]{2,1,0:T(8,128)(2,1)S(1)} %copy-done.51), channel_id=1, source_target_pairs={{0,4},{2,6},{4,0},{6,2},{1,5},{3,7},{5,1},{7,3},{8,12},{10,14},{12... | collective-permute-start | bytes 1179656 | tf_op jit(solution)/shard_map/ppermute | solution.py:393
  189.3 25.4 %collective-permute-start.37 = (bf16[2,64,1536]{2,1,0:T(8,128)(2,1)S(1)}, bf16[2,64,1536]{2,1,0:T(8,128)(2,1)}, u32[]{:S(2)}, u32[]{:S(2)}) collective-permute-start(bf16[2,64,1536]{2,1,0:T(8,128)(2,1)S(1)} %copy-done.51), channel_id=1, source_target_pairs={{0,6},{2,0},{4,2},{6,4},{1,7},{3,1},{5,3},{7,5},{8,14},{10,8},{12,... | collective-permute-start | bytes 1179656 | tf_op jit(solution)/shard_map/ppermute | solution.py:393
  190.9 23.8 %collective-permute-start.33 = (bf16[192,1152]{1,0:T(8,128)(2,1)S(1)}, bf16[192,1152]{1,0:T(8,128)(2,1)}, u32[]{:S(2)}, u32[]{:S(2)}) collective-permute-start(bf16[192,1152]{1,0:T(8,128)(2,1)S(1)} %get-tuple-element.162), channel_id=1, source_target_pairs={{0,8},{8,0},{16,24},{24,16},{1,9},{9,1},{17,25},{25,17},{2,10},{10... | collective-permute-start | bytes 1327112 | tf_op jit(solution)/shard_map/ppermute | solution.py:397
  191.7 23.0 %collective-permute-start.34 = (bf16[192,1152]{1,0:T(8,128)(2,1)}, bf16[192,1152]{1,0:T(8,128)(2,1)}, u32[]{:S(2)}, u32[]{:S(2)}) collective-permute-start(bf16[192,1152]{1,0:T(8,128)(2,1)} %get-tuple-element.163), channel_id=1, source_target_pairs={{0,16},{8,24},{16,0},{24,8},{1,17},{9,25},{17,1},{25,9},{2,18},{10... | collective-permute-start | bytes 1327112 | tf_op jit(solution)/shard_map/ppermute | solution.py:401
  219.6 22.1 %collective-permute-start.39 = (bf16[2,192,1152]{2,1,0:T(8,128)(2,1)S(1)}, bf16[2,192,1152]{2,1,0:T(8,128)(2,1)S(1)}, u32[]{:S(2)}, u32[]{:S(2)}) collective-permute-start(bf16[2,192,1152]{2,1,0:T(8,128)(2,1)S(1)} %pad_maximum_fusion.13), channel_id=1, source_target_pairs={{0,16},{8,24},{16,0},{24,8},{1,17},{9,25},{17,1},{25,9},{2,18},{10... | collective-permute-start | bytes 2654216 | tf_op jit(solution)/shard_map/ppermute | solution.py:401
  268.3 32.0 %collective-permute-start.46 = (bf16[2,192,1152]{2,1,0:T(8,128)(2,1)S(1)}, bf16[2,192,1152]{2,1,0:T(8,128)(2,1)S(1)}, u32[]{:S(2)}, u32[]{:S(2)}) collective-permute-start(bf16[2,192,1152]{2,1,0:T(8,128)(2,1)S(1)} %get-tuple-element.273), channel_id=1, source_target_pairs={{0,8},{8,0},{16,24},{24,16},{1,9},{9,1},{17,25},{25,17},{2,10},{10... | collective-permute-start | bytes 2654216 | tf_op jit(solution)/shard_map/ppermute | solution.py:397
  269.7 30.6 %collective-permute-start.47 = (bf16[2,192,1152]{2,1,0:T(8,128)(2,1)S(1)}, bf16[2,192,1152]{2,1,0:T(8,128)(2,1)S(1)}, u32[]{:S(2)}, u32[]{:S(2)}) collective-permute-start(bf16[2,192,1152]{2,1,0:T(8,128)(2,1)S(1)} %get-tuple-element.271), channel_id=1, source_target_pairs={{0,16},{8,24},{16,0},{24,8},{1,17},{9,25},{17,1},{25,9},{2,18},{10... | collective-permute-start | bytes 2654216 | tf_op jit(solution)/shard_map/ppermute | solution.py:401
  274.6 32.2 %collective-permute-start.43 = (bf16[128,1536]{1,0:T(8,128)(2,1)}, bf16[128,1536]{1,0:T(8,128)(2,1)}, u32[]{:S(2)}, u32[]{:S(2)}) collective-permute-start(bf16[128,1536]{1,0:T(8,128)(2,1)} %get-tuple-element.299), channel_id=1, source_target_pairs={{0,6},{2,0},{4,2},{6,4},{1,7},{3,1},{5,3},{7,5},{8,14},{10,8},{12,... | collective-permute-start | bytes 1179656 | tf_op jit(solution)/shard_map/ppermute | solution.py:393
  283.7 36.1 %collective-permute-start.44 = (bf16[128,1536]{1,0:T(8,128)(2,1)}, bf16[128,1536]{1,0:T(8,128)(2,1)}, u32[]{:S(2)}, u32[]{:S(2)}) collective-permute-start(bf16[128,1536]{1,0:T(8,128)(2,1)} %get-tuple-element.298), channel_id=1, source_target_pairs={{0,4},{2,6},{4,0},{6,2},{1,5},{3,7},{5,1},{7,3},{8,12},{10,14},{12... | collective-permute-start | bytes 1179656 | tf_op jit(solution)/shard_map/ppermute | solution.py:393
  284.9 35.6 %collective-permute-start.45 = (bf16[128,1536]{1,0:T(8,128)(2,1)}, bf16[128,1536]{1,0:T(8,128)(2,1)}, u32[]{:S(2)}, u32[]{:S(2)}) collective-permute-start(bf16[128,1536]{1,0:T(8,128)(2,1)} %get-tuple-element.297), channel_id=1, source_target_pairs={{0,2},{2,4},{4,6},{6,0},{1,3},{3,5},{5,7},{7,1},{8,10},{10,12},{12... | collective-permute-start | bytes 1179656 | tf_op jit(solution)/shard_map/ppermute | solution.py:393
  319.7 39.9 %collective-permute-start.60 = (bf16[2,192,2304]{2,1,0:T(8,128)(2,1)S(1)}, bf16[2,192,2304]{2,1,0:T(8,128)(2,1)S(1)}, u32[]{:S(2)}, u32[]{:S(2)}) collective-permute-start(bf16[2,192,2304]{2,1,0:T(8,128)(2,1)S(1)} %get-tuple-element.252), channel_id=1, source_target_pairs={{0,8},{8,0},{16,24},{24,16},{1,9},{9,1},{17,25},{25,17},{2,10},{10... | collective-permute-start | bytes 5308424 | tf_op jit(solution)/shard_map/ppermute | solution.py:397
  320.6 39.6 %collective-permute-start.61 = (bf16[2,192,2304]{2,1,0:T(8,128)(2,1)S(1)}, bf16[2,192,2304]{2,1,0:T(8,128)(2,1)S(1)}, u32[]{:S(2)}, u32[]{:S(2)}) collective-permute-start(bf16[2,192,2304]{2,1,0:T(8,128)(2,1)S(1)} %get-tuple-element.250), channel_id=1, source_target_pairs={{0,16},{8,24},{16,0},{24,8},{1,17},{9,25},{17,1},{25,9},{2,18},{10... | collective-permute-start | bytes 5308424 | tf_op jit(solution)/shard_map/ppermute | solution.py:401
  376.3 36.6 %collective-permute-start.58 = (bf16[128,1536]{1,0:T(8,128)(2,1)}, bf16[128,1536]{1,0:T(8,128)(2,1)}, u32[]{:S(2)}, u32[]{:S(2)}) collective-permute-start(bf16[128,1536]{1,0:T(8,128)(2,1)} %get-tuple-element.206), channel_id=1, source_target_pairs={{0,4},{2,6},{4,0},{6,2},{1,5},{3,7},{5,1},{7,3},{8,12},{10,14},{12... | collective-permute-start | bytes 1179656 | tf_op jit(solution)/shard_map/ppermute | solution.py:393
  378.2 34.7 %collective-permute-start.59 = (bf16[128,1536]{1,0:T(8,128)(2,1)}, bf16[128,1536]{1,0:T(8,128)(2,1)S(1)}, u32[]{:S(2)}, u32[]{:S(2)}) collective-permute-start(bf16[128,1536]{1,0:T(8,128)(2,1)} %get-tuple-element.207), channel_id=1, source_target_pairs={{0,2},{2,4},{4,6},{6,0},{1,3},{3,5},{5,7},{7,1},{8,10},{10,12},{12... | collective-permute-start | bytes 1179656 | tf_op jit(solution)/shard_map/ppermute | solution.py:393
  388.6 29.2 %collective-permute-start.65 = (bf16[2,192,1792]{2,1,0:T(8,128)(2,1)S(1)}, bf16[2,192,1792]{2,1,0:T(8,128)(2,1)S(1)}, u32[]{:S(2)}, u32[]{:S(2)}) collective-permute-start(bf16[2,192,1792]{2,1,0:T(8,128)(2,1)S(1)} %get-tuple-element.266), channel_id=1, source_target_pairs={{0,8},{8,0},{16,24},{24,16},{1,9},{9,1},{17,25},{25,17},{2,10},{10... | collective-permute-start | bytes 4128776 | tf_op jit(solution)/shard_map/ppermute | solution.py:397
  389.8 29.0 %collective-permute-start.66 = (bf16[2,192,1792]{2,1,0:T(8,128)(2,1)S(1)}, bf16[2,192,1792]{2,1,0:T(8,128)(2,1)S(1)}, u32[]{:S(2)}, u32[]{:S(2)}) collective-permute-start(bf16[2,192,1792]{2,1,0:T(8,128)(2,1)S(1)} %get-tuple-element.264), channel_id=1, source_target_pairs={{0,16},{8,24},{16,0},{24,8},{1,17},{9,25},{17,1},{25,9},{2,18},{10... | collective-permute-start | bytes 4128776 | tf_op jit(solution)/shard_map/ppermute | solution.py:401
  421.2 29.1 %collective-permute-start.73 = (bf16[96,2304]{1,0:T(8,128)(2,1)S(1)}, bf16[96,2304]{1,0:T(8,128)(2,1)S(1)}, u32[]{:S(2)}, u32[]{:S(2)}) collective-permute-start(bf16[96,2304]{1,0:T(8,128)(2,1)S(1)} %get-tuple-element.269), channel_id=1, source_target_pairs={{0,4},{2,6},{4,0},{6,2},{1,5},{3,7},{5,1},{7,3},{8,12},{10,14},{12... | collective-permute-start | bytes 1327112 | tf_op jit(solution)/shard_map/ppermute | solution.py:393
  424.3 26.0 %collective-permute-start.74 = (bf16[96,2304]{1,0:T(8,128)(2,1)S(1)}, bf16[96,2304]{1,0:T(8,128)(2,1)S(1)}, u32[]{:S(2)}, u32[]{:S(2)}) collective-permute-start(bf16[96,2304]{1,0:T(8,128)(2,1)S(1)} %get-tuple-element.268), channel_id=1, source_target_pairs={{0,6},{2,0},{4,2},{6,4},{1,7},{3,1},{5,3},{7,5},{8,14},{10,8},{12,... | collective-permute-start | bytes 1327112 | tf_op jit(solution)/shard_map/ppermute | solution.py:393
  424.4 50.4 %collective-permute-start.68 = (bf16[192,1792]{1,0:T(8,128)(2,1)S(1)}, bf16[192,1792]{1,0:T(8,128)(2,1)S(1)}, u32[]{:S(2)}, u32[]{:S(2)}) collective-permute-start(bf16[192,1792]{1,0:T(8,128)(2,1)S(1)} %get-tuple-element.308), channel_id=1, source_target_pairs={{0,8},{8,0},{16,24},{24,16},{1,9},{9,1},{17,25},{25,17},{2,10},{10... | collective-permute-start | bytes 2064392 | tf_op jit(solution)/shard_map/ppermute | solution.py:397
  425.6 49.2 %collective-permute-start.67 = (bf16[192,1792]{1,0:T(8,128)(2,1)S(1)}, bf16[192,1792]{1,0:T(8,128)(2,1)S(1)}, u32[]{:S(2)}, u32[]{:S(2)}) collective-permute-start(bf16[192,1792]{1,0:T(8,128)(2,1)S(1)} %get-tuple-element.310), channel_id=1, source_target_pairs={{0,16},{8,24},{16,0},{24,8},{1,17},{9,25},{17,1},{25,9},{2,18},{10... | collective-permute-start | bytes 2064392 | tf_op jit(solution)/shard_map/ppermute | solution.py:401
  476.9 27.6 %collective-permute-start.71 = (bf16[96,1792]{1,0:T(8,128)(2,1)S(1)}, bf16[96,1792]{1,0:T(8,128)(2,1)S(1)}, u32[]{:S(2)}, u32[]{:S(2)}) collective-permute-start(bf16[96,1792]{1,0:T(8,128)(2,1)S(1)} %get-tuple-element.307), channel_id=1, source_target_pairs={{0,4},{2,6},{4,0},{6,2},{1,5},{3,7},{5,1},{7,3},{8,12},{10,14},{12... | collective-permute-start | bytes 1032200 | tf_op jit(solution)/shard_map/ppermute | solution.py:393
  479.0 25.4 %collective-permute-start.72 = (bf16[96,1792]{1,0:T(8,128)(2,1)S(1)}, bf16[96,1792]{1,0:T(8,128)(2,1)S(1)}, u32[]{:S(2)}, u32[]{:S(2)}) collective-permute-start(bf16[96,1792]{1,0:T(8,128)(2,1)S(1)} %get-tuple-element.306), channel_id=1, source_target_pairs={{0,2},{2,4},{4,6},{6,0},{1,3},{3,5},{5,7},{7,1},{8,10},{10,12},{12... | collective-permute-start | bytes 1032200 | tf_op jit(solution)/shard_map/ppermute | solution.py:393
  (140 other events, 1307.8 us)

commit v5 on v4

--- a/solution.py
+++ b/solution.py
@@ -26,7 +26,7 @@
     return (jnp.cos(angles)[:, None, :], jnp.sin(angles)[:, None, :])
 
 
-VMEM_LIMIT = 32 * 1024 * 1024
+VMEM_LIMIT = 28 * 1024 * 1024
 
 
 def params():

time: 514 us -> 512 us (level)
  starting transfers between devices: 144 us -> 150 us
    ppermute x39, starting transfers between devices: 98.7 us -> 105 us  [shift_ctx(): lax.ppermute(value, 'ctx', [(i, (i + distance) % size) for i in range(siz...]
    ppermute x39, waiting for transfers between devices: 134 us -> 129 us  [shift_ctx(): lax.ppermute(value, 'ctx', [(i, (i + distance) % size) for i in range(siz...]
    unnamed x199 -> x201, local copies, waits for them, and re-layouts: 14.3 us -> 13.8 us
  transfers between devices with their start and end apart: 80 -> 80, of which waited for: 37 -> 37; matrix products, arithmetic and copies ran while one was open for 15% -> 15% of each run, Pallas kernels for 10% -> 9%
where the time goes in v5:
time: 512 us; the launch traced here: 505 us
  waiting for transfers between devices  189 us (37%)
  starting transfers between devices  150 us (29%)
  Pallas kernels  64.3 us (13%)
  other arithmetic  61 us (12%)
  local copies, waits for them, and re-layouts  34.8 us (7%)
    ppermute x39, waiting for transfers between devices, shift_ctx(): lax.ppermute(value, 'ctx', [(i, (i + distance) % size) for i in range(siz...  129 us
    ppermute x39, starting transfers between devices, shift_ctx(): lax.ppermute(value, 'ctx', [(i, (i + distance) % size) for i in range(siz...  105 us
    ppermute x14, waiting for transfers between devices, swap_x(): return lax.ppermute(value, 'dp', [(i, i ^ 1) for i in range(4)])  36.9 us
    ppermute x14, starting transfers between devices, swap_y(): return lax.ppermute(value, 'dp', [(i, i ^ 2) for i in range(4)])  18.1 us
    pallas_call x1, Pallas kernels, hidden_back(): pl.pallas_call(hidden_back_kernel, out_shape=(out, out, out_x), grid=(row...  16.8 us
    ppermute x14, waiting for transfers between devices, swap_y(): return lax.ppermute(value, 'dp', [(i, i ^ 2) for i in range(4)])  14.5 us
    ppermute x14, starting transfers between devices, swap_x(): return lax.ppermute(value, 'dp', [(i, i ^ 1) for i in range(4)])  13.9 us
    unnamed x201, local copies, waits for them, and re-layouts  13.8 us
  transfers between devices with their start and end apart: 80, of which 37 were waited for; matrix products, arithmetic and copies ran while one was open for 15% of the time, Pallas kernels for 9%

profile of v5, /device:TPU:0, one launch (start us, length us, event | category | flops | bytes accessed | tf_op | source)
XLA Modules:
  0.0 505.0 jit_solution(11729510709393830072)
XLA Ops:
  25.7 5.8 %collective-permute-start.10 = (bf16[96,768]{1,0:T(8,128)(2,1)S(1)}, bf16[96,768]{1,0:T(8,128)(2,1)S(1)}, u32[]{:S(2)}, u32[]{:S(2)}) collective-permute-start(bf16[96,768]{1,0:T(8,128)(2,1)S(1)} %convert_element_type.285), channel_id=1, source_target_pairs={{0,6},{2,0},{4,2},{6,4},{1,7},{3,1},{5,3},{7,5},{8,14},{10,8},{12,... | collective-permute-start | bytes 442376 | tf_op jit(solution)/shard_map/ppermute | solution.py:393
  39.5 5.4 %collective-permute-done.9 = bf16[96,768]{1,0:T(8,128)(2,1)S(1)} collective-permute-done((bf16[96,768]{1,0:T(8,128)(2,1)S(1)}, bf16[96,768]{1,0:T(8,128)(2,1)S(1)}, u32[]{:S(2)}, u32[]{:S(2)}) %collective-permute-start.9) | collective-permute-done | bytes 147488 | tf_op jit(solution)/shard_map/ppermute | solution.py:393
  49.2 5.6 %collective-permute-start.11 = (bf16[96,2304]{1,0:T(8,128)(2,1)S(1)}, bf16[96,2304]{1,0:T(8,128)(2,1)S(1)}, u32[]{:S(2)}, u32[]{:S(2)}) collective-permute-start(bf16[96,2304]{1,0:T(8,128)(2,1)S(1)} %get-tuple-element.291), channel_id=1, source_target_pairs={{0,2},{2,4},{4,6},{6,0},{1,3},{3,5},{5,7},{7,1},{8,10},{10,12},{12... | collective-permute-start | bytes 1327112 | tf_op jit(solution)/shard_map/ppermute | solution.py:393
  58.7 6.3 %collective-permute-done.5 = bf16[2,192,1024]{2,1,0:T(8,128)(2,1)S(1)} collective-permute-done((bf16[2,192,1024]{2,1,0:T(8,128)(2,1)S(1)}, bf16[2,192,1024]{2,1,0:T(8,128)(2,1)S(1)}, u32[]{:S(2)}, u32[]{:S(2)}) %collective-permute-start.5) | collective-permute-done | bytes 786464 | tf_op jit(solution)/shard_map/ppermute | solution.py:401
  70.9 9.5 %collective-permute-done.12 = bf16[96,2304]{1,0:T(8,128)(2,1)S(1)} collective-permute-done((bf16[96,2304]{1,0:T(8,128)(2,1)S(1)}, bf16[96,2304]{1,0:T(8,128)(2,1)S(1)}, u32[]{:S(2)}, u32[]{:S(2)}) %collective-permute-start.12) | collective-permute-done | bytes 442400 | tf_op jit(solution)/shard_map/ppermute | solution.py:393
  80.8 11.4 %collective-permute-start.16 = (bf16[2,128,256]{2,1,0:T(8,128)(2,1)S(1)}, bf16[2,128,256]{2,1,0:T(8,128)(2,1)S(1)}, u32[]{:S(2)}, u32[]{:S(2)}) collective-permute-start(bf16[2,128,256]{2,1,0:T(8,128)(2,1)S(1)} %bitcast.419), channel_id=1, source_target_pairs={{0,2},{2,4},{4,6},{6,0},{1,3},{3,5},{5,7},{7,1},{8,10},{10,12},{12... | collective-permute-start | bytes 393224 | tf_op jit(solution)/shard_map/ppermute | solution.py:393
  97.3 3.6 collective-permute-done.17
  101.0 5.1 %attend.1.right2_ref = bf16[256,768]{1,0:T(8,128)(2,1)S(1)} custom-call(s32[2]{0:T(128)S(1)} %copy-done.27, s32[128,1]{1,0:T(8,128)S(1)} %copy-done.20, s32[1,512]{1,0:T(1,128)S(1)} %bitcast.393, bf16[256,768]{1,0:T(8,128)(2,1)S(1)} %slice.286.q_ref, bf16[2,512,256]{2,1,0:T(8,128)(2,1)S(1)} %constant_dynamic-update-slice_fusion.kv_ref), custom_call_target="tpu_custom_call" | custom-call | flops 402653184 | bytes 1310720 | tf_op jit(solution)/shard_map/attend/pallas_call | solution.py:146
  119.9 15.4 %collective-permute-done.25 = bf16[192,2304]{1,0:T(8,128)(2,1)S(1)} collective-permute-done((bf16[192,2304]{1,0:T(8,128)(2,1)S(1)}, bf16[192,2304]{1,0:T(8,128)(2,1)S(1)}, u32[]{:S(2)}, u32[]{:S(2)}) %collective-permute-start.25) | collective-permute-done | bytes 884768 | tf_op jit(solution)/shard_map/ppermute | solution.py:397
  136.3 9.6 %collective-permute-done.23 = bf16[2,64,1536]{2,1,0:T(8,128)(2,1)S(1)} collective-permute-done((bf16[2,64,1536]{2,1,0:T(8,128)(2,1)S(1)}, bf16[2,64,1536]{2,1,0:T(8,128)(2,1)S(1)}, u32[]{:S(2)}, u32[]{:S(2)}) %collective-permute-start.23) | collective-permute-done | bytes 393248 | tf_op jit(solution)/shard_map/ppermute | solution.py:393
  149.7 18.5 %collective-permute-start.28 = (bf16[96,1152]{1,0:T(8,128)(2,1)S(1)}, bf16[96,1152]{1,0:T(8,128)(2,1)S(1)}, u32[]{:S(2)}, u32[]{:S(2)}) collective-permute-start(bf16[96,1152]{1,0:T(8,128)(2,1)S(1)} %get-tuple-element.337), channel_id=1, source_target_pairs={{0,2},{2,4},{4,6},{6,0},{1,3},{3,5},{5,7},{7,1},{8,10},{10,12},{12... | collective-permute-start | bytes 663560 | tf_op jit(solution)/shard_map/ppermute | solution.py:393
  170.6 3.7 collective-permute-done.28
  174.3 9.0 %collective-permute-done.29 = bf16[96,1152]{1,0:T(8,128)(2,1)S(1)} collective-permute-done((bf16[96,1152]{1,0:T(8,128)(2,1)S(1)}, bf16[96,1152]{1,0:T(8,128)(2,1)S(1)}, u32[]{:S(2)}, u32[]{:S(2)}) %collective-permute-start.29) | collective-permute-done | bytes 221216 | tf_op jit(solution)/shard_map/ppermute | solution.py:393
  183.4 5.3 %collective-permute-start.35 = (bf16[2,64,1536]{2,1,0:T(8,128)(2,1)S(1)}, bf16[2,64,1536]{2,1,0:T(8,128)(2,1)}, u32[]{:S(2)}, u32[]{:S(2)}) collective-permute-start(bf16[2,64,1536]{2,1,0:T(8,128)(2,1)S(1)} %copy-done.49), channel_id=1, source_target_pairs={{0,2},{2,4},{4,6},{6,0},{1,3},{3,5},{5,7},{7,1},{8,10},{10,12},{12... | collective-permute-start | bytes 1179656 | tf_op jit(solution)/shard_map/ppermute | solution.py:393
  199.4 3.9 pad_maximum_fusion
  203.3 12.2 %hidden_units.1 = (bf16[1024,1152]{1,0:T(8,128)(2,1)S(1)}, bf16[1024,1152]{1,0:T(8,128)(2,1)S(1)}, bf16[1024,1152]{1,0:T(8,128)(2,1)S(1)}) custom-call(bf16[1024,1536]{1,0:T(8,128)(2,1)S(1)} %copy-done.23, bf16[1536,2304]{1,0:T(8,128)(2,1)S(1)} %bitcast.376, bf16[1536,2304]{1,0:T(8,128)(2,1)S(1)} %bitcast.377), custom_call_target="tpu_custom_call" | custom-call | flops 7247757312 | bytes 17301504 | tf_op jit(solution)/shard_map/hidden_units/pallas_call | solution.py:218
  226.3 4.9 weight_terms.1
  231.2 8.3 %collective-permute-done.40 = bf16[2,192,1152]{2,1,0:T(8,128)(2,1)S(1)} collective-permute-done((bf16[2,192,1152]{2,1,0:T(8,128)(2,1)S(1)}, bf16[2,192,1152]{2,1,0:T(8,128)(2,1)S(1)}, u32[]{:S(2)}, u32[]{:S(2)}) %collective-permute-start.40) | collective-permute-done | bytes 884768 | tf_op jit(solution)/shard_map/ppermute | solution.py:397
  239.5 4.1 collective-permute-done.39
  244.7 16.8 %hidden_back.1 = (bf16[1024,1152]{1,0:T(8,128)(2,1)S(1)}, bf16[1024,1152]{1,0:T(8,128)(2,1)S(1)}, bf16[1024,1536]{1,0:T(8,128)(2,1)S(1)}) custom-call(bf16[1024,1536]{1,0:T(8,128)(2,1)S(1)} %constant_dynamic-update-slice_fusion.9.left_ref.dy_ref, bf16[1024,1152]{1,0:T(8,128)(2,1)S(1)} %get-tuple-element.168.silu_ref, ...), custom_call_target="tpu_custom_call" | custom-call | flops 10871635968 | bytes 26345472 | tf_op jit(solution)/shard_map/hidden_back/pallas_call | solution.py:265
  274.8 9.1 %collective-permute-start.43 = (bf16[128,1536]{1,0:T(8,128)(2,1)}, bf16[128,1536]{1,0:T(8,128)(2,1)}, u32[]{:S(2)}, u32[]{:S(2)}) collective-permute-start(bf16[128,1536]{1,0:T(8,128)(2,1)} %get-tuple-element.299), channel_id=1, source_target_pairs={{0,6},{2,0},{4,2},{6,4},{1,7},{3,1},{5,3},{7,5},{8,14},{10,8},{12,... | collective-permute-start | bytes 1179656 | tf_op jit(solution)/shard_map/ppermute | solution.py:393
  285.2 13.2 %pair_terms.1 = (bf16[1536,2304]{1,0:T(8,128)(2,1)S(1)}, bf16[1024,1536]{1,0:T(8,128)(2,1)S(1)}) custom-call(bf16[1024,1536]{1,0:T(8,128)(2,1)S(1)} %copy-done.24, bf16[1024,1152]{1,0:T(8,128)(2,1)S(1)} %copy-done.31, bf16[1024,1152]{1,0:T(8,128)(2,1)S(1)} %copy-done.33, bf16[1024,1152]{1,0:T(8,128)(2,1)S(1)} %copy-done.29, bf16[1536,1152]{1,0:T(8,128)(2,1)S(1)} %bitcast.385), custom_call_target="tpu_custom_call" | custom-call | flops 10871635968 | bytes 23986176 | tf_op jit(solution)/shard_map/pair_terms/pallas_call | solution.py:298
  306.2 13.8 %collective-permute-done.44 = bf16[128,1536]{1,0:T(8,128)(2,1)} collective-permute-done((bf16[128,1536]{1,0:T(8,128)(2,1)}, bf16[128,1536]{1,0:T(8,128)(2,1)}, u32[]{:S(2)}, u32[]{:S(2)}) %collective-permute-start.44) | collective-permute-done | bytes 393248 | tf_op jit(solution)/shard_map/ppermute | solution.py:393
  336.2 7.5 %attend_back.1 = (bf16[256,768]{1,0:T(8,128)(2,1)S(1)}, bf16[2,512,256]{2,1,0:T(8,128)(2,1)S(1)}) custom-call(s32[2]{0:T(128)S(1)} %copy-done.27, s32[128,1]{1,0:T(8,128)S(1)} %copy-done.21, s32[1,512]{1,0:T(1,128)S(1)} %bitcast.394, bf16[256,768]{1,0:T(8,128)(2,1)S(1)} %copy-done.19, bf16[2,512,256]{2,1,0:T(8,128)(2,1)S(1)} %copy-done.26, ...), custom_call_target="tpu_custom_call" | custom-call | flops 1006632960 | bytes 2228224 | tf_op jit(solution)/shard_map/attend_back/pallas_call | solution.py:161
  343.7 5.6 %collective-permute-done.52 = bf16[96,1152]{1,0:T(8,128)(2,1)S(1)} collective-permute-done((bf16[96,1152]{1,0:T(8,128)(2,1)S(1)}, bf16[96,1152]{1,0:T(8,128)(2,1)S(1)}, u32[]{:S(2)}, u32[]{:S(2)}) %collective-permute-start.52) | collective-permute-done | bytes 221216 | tf_op jit(solution)/shard_map/ppermute | solution.py:393
  350.1 3.9 collective-permute-start.54
  391.7 20.7 %collective-permute-done.58 = bf16[128,1536]{1,0:T(8,128)(2,1)} collective-permute-done((bf16[128,1536]{1,0:T(8,128)(2,1)}, bf16[128,1536]{1,0:T(8,128)(2,1)}, u32[]{:S(2)}, u32[]{:S(2)}) %collective-permute-start.58) | collective-permute-done | bytes 393248 | tf_op jit(solution)/shard_map/ppermute | solution.py:393
  426.9 8.2 %collective-permute-done.69 = bf16[96,2304]{1,0:T(8,128)(2,1)S(1)} collective-permute-done((bf16[96,2304]{1,0:T(8,128)(2,1)S(1)}, bf16[96,2304]{1,0:T(8,128)(2,1)S(1)}, u32[]{:S(2)}, u32[]{:S(2)}) %collective-permute-start.69) | collective-permute-done | bytes 442400 | tf_op jit(solution)/shard_map/ppermute | solution.py:393
  435.1 14.6 %collective-permute-done.73 = bf16[96,2304]{1,0:T(8,128)(2,1)S(1)} collective-permute-done((bf16[96,2304]{1,0:T(8,128)(2,1)S(1)}, bf16[96,2304]{1,0:T(8,128)(2,1)S(1)}, u32[]{:S(2)}, u32[]{:S(2)}) %collective-permute-start.73) | collective-permute-done | bytes 442400 | tf_op jit(solution)/shard_map/ppermute | solution.py:393
  457.6 9.4 %collective-permute-start.78 = (f32[40,128]{1,0:T(8,128)S(1)}, f32[40,128]{1,0:T(8,128)S(1)}, u32[]{:S(2)}, u32[]{:S(2)}) collective-permute-start(f32[40,128]{1,0:T(8,128)S(1)} %add.478), channel_id=1, source_target_pairs={{0,2},{2,0},{4,6},{6,4},{1,3},{3,1},{5,7},{7,5},{8,10},{10,8},{12,... | collective-permute-start | bytes 61448 | tf_op jit(solution)/shard_map/ppermute | solution.py:526
  474.2 9.7 %collective-permute-start.70 = (bf16[96,1792]{1,0:T(8,128)(2,1)S(1)}, bf16[96,1792]{1,0:T(8,128)(2,1)S(1)}, u32[]{:S(2)}, u32[]{:S(2)}) collective-permute-start(bf16[96,1792]{1,0:T(8,128)(2,1)S(1)} %get-tuple-element.305), channel_id=1, source_target_pairs={{0,6},{2,0},{4,2},{6,4},{1,7},{3,1},{5,3},{7,5},{8,14},{10,8},{12,... | collective-permute-start | bytes 1032200 | tf_op jit(solution)/shard_map/ppermute | solution.py:393
  489.2 14.0 %collective-permute-done.71 = bf16[96,1792]{1,0:T(8,128)(2,1)S(1)} collective-permute-done((bf16[96,1792]{1,0:T(8,128)(2,1)S(1)}, bf16[96,1792]{1,0:T(8,128)(2,1)S(1)}, u32[]{:S(2)}, u32[]{:S(2)}) %collective-permute-start.71) | collective-permute-done | bytes 344096 | tf_op jit(solution)/shard_map/ppermute | solution.py:393
  (519 shorter events, 208.1 us)
Async XLA Ops:
  13.9 41.1 %collective-permute-start = (bf16[2,64,1536]{2,1,0:T(8,128)(2,1)}, bf16[2,64,1536]{2,1,0:T(8,128)(2,1)}, u32[]{:S(2)}, u32[]{:S(2)}) collective-permute-start(bf16[2,64,1536]{2,1,0:T(8,128)(2,1)} %fusion.5), channel_id=1, source_target_pairs={{0,1},{1,0},{2,3},{3,2},{4,5},{5,4},{6,7},{7,6},{8,9},{9,8},{10,11... | collective-permute-start | bytes 1179656 | tf_op jit(solution)/shard_map/ppermute | solution.py:388
  54.8 25.7 %collective-permute-start.12 = (bf16[96,2304]{1,0:T(8,128)(2,1)S(1)}, bf16[96,2304]{1,0:T(8,128)(2,1)S(1)}, u32[]{:S(2)}, u32[]{:S(2)}) collective-permute-start(bf16[96,2304]{1,0:T(8,128)(2,1)S(1)} %get-tuple-element.290), channel_id=1, source_target_pairs={{0,4},{2,6},{4,0},{6,2},{1,5},{3,7},{5,1},{7,3},{8,12},{10,14},{12... | collective-permute-start | bytes 1327112 | tf_op jit(solution)/shard_map/ppermute | solution.py:393
  55.0 25.5 %collective-permute-start.13 = (bf16[96,2304]{1,0:T(8,128)(2,1)S(1)}, bf16[96,2304]{1,0:T(8,128)(2,1)S(1)}, u32[]{:S(2)}, u32[]{:S(2)}) collective-permute-start(bf16[96,2304]{1,0:T(8,128)(2,1)S(1)} %get-tuple-element.289), channel_id=1, source_target_pairs={{0,6},{2,0},{4,2},{6,4},{1,7},{3,1},{5,3},{7,5},{8,14},{10,8},{12,... | collective-permute-start | bytes 1327112 | tf_op jit(solution)/shard_map/ppermute | solution.py:393
  113.2 22.1 %collective-permute-start.25 = (bf16[192,2304]{1,0:T(8,128)(2,1)S(1)}, bf16[192,2304]{1,0:T(8,128)(2,1)S(1)}, u32[]{:S(2)}, u32[]{:S(2)}) collective-permute-start(bf16[192,2304]{1,0:T(8,128)(2,1)S(1)} %get-tuple-element.142), channel_id=1, source_target_pairs={{0,8},{8,0},{16,24},{24,16},{1,9},{9,1},{17,25},{25,17},{2,10},{10... | collective-permute-start | bytes 2654216 | tf_op jit(solution)/shard_map/ppermute | solution.py:397
  116.1 29.8 %collective-permute-start.23 = (bf16[2,64,1536]{2,1,0:T(8,128)(2,1)S(1)}, bf16[2,64,1536]{2,1,0:T(8,128)(2,1)S(1)}, u32[]{:S(2)}, u32[]{:S(2)}) collective-permute-start(bf16[2,64,1536]{2,1,0:T(8,128)(2,1)S(1)} %multiply_convert_fusion), channel_id=1, source_target_pairs={{0,4},{2,6},{4,0},{6,2},{1,5},{3,7},{5,1},{7,3},{8,12},{10,14},{12... | collective-permute-start | bytes 1179656 | tf_op jit(solution)/shard_map/ppermute | solution.py:393
  118.3 27.6 %collective-permute-start.24 = (bf16[2,64,1536]{2,1,0:T(8,128)(2,1)S(1)}, bf16[2,64,1536]{2,1,0:T(8,128)(2,1)S(1)}, u32[]{:S(2)}, u32[]{:S(2)}) collective-permute-start(bf16[2,64,1536]{2,1,0:T(8,128)(2,1)S(1)} %multiply_convert_fusion), channel_id=1, source_target_pairs={{0,6},{2,0},{4,2},{6,4},{1,7},{3,1},{5,3},{7,5},{8,14},{10,8},{12,... | collective-permute-start | bytes 1179656 | tf_op jit(solution)/shard_map/ppermute | solution.py:393
  146.3 45.1 %collective-permute-start.32 = (bf16[2,192,2304]{2,1,0:T(8,128)(2,1)S(1)}, bf16[2,192,2304]{2,1,0:T(8,128)(2,1)S(1)}, u32[]{:S(2)}, u32[]{:S(2)}) collective-permute-start(bf16[2,192,2304]{2,1,0:T(8,128)(2,1)S(1)} %pad_maximum_fusion.6), channel_id=1, source_target_pairs={{0,8},{8,0},{16,24},{24,16},{1,9},{9,1},{17,25},{25,17},{2,10},{10... | collective-permute-start | bytes 5308424 | tf_op jit(solution)/shard_map/ppermute | solution.py:397
  147.3 44.1 %collective-permute-start.31 = (bf16[2,192,2304]{2,1,0:T(8,128)(2,1)S(1)}, bf16[2,192,2304]{2,1,0:T(8,128)(2,1)S(1)}, u32[]{:S(2)}, u32[]{:S(2)}) collective-permute-start(bf16[2,192,2304]{2,1,0:T(8,128)(2,1)S(1)} %pad_maximum_fusion.5), channel_id=1, source_target_pairs={{0,16},{8,24},{16,0},{24,8},{1,17},{9,25},{17,1},{25,9},{2,18},{10... | collective-permute-start | bytes 5308424 | tf_op jit(solution)/shard_map/ppermute | solution.py:401
  149.7 24.6 %collective-permute-start.28 = (bf16[96,1152]{1,0:T(8,128)(2,1)S(1)}, bf16[96,1152]{1,0:T(8,128)(2,1)S(1)}, u32[]{:S(2)}, u32[]{:S(2)}) collective-permute-start(bf16[96,1152]{1,0:T(8,128)(2,1)S(1)} %get-tuple-element.337), channel_id=1, source_target_pairs={{0,2},{2,4},{4,6},{6,0},{1,3},{3,5},{5,7},{7,1},{8,10},{10,12},{12... | collective-permute-start | bytes 663560 | tf_op jit(solution)/shard_map/ppermute | solution.py:393
  183.4 32.2 %collective-permute-start.35 = (bf16[2,64,1536]{2,1,0:T(8,128)(2,1)S(1)}, bf16[2,64,1536]{2,1,0:T(8,128)(2,1)}, u32[]{:S(2)}, u32[]{:S(2)}) collective-permute-start(bf16[2,64,1536]{2,1,0:T(8,128)(2,1)S(1)} %copy-done.49), channel_id=1, source_target_pairs={{0,2},{2,4},{4,6},{6,0},{1,3},{3,5},{5,7},{7,1},{8,10},{10,12},{12... | collective-permute-start | bytes 1179656 | tf_op jit(solution)/shard_map/ppermute | solution.py:393
  188.7 28.0 %collective-permute-start.36 = (bf16[2,64,1536]{2,1,0:T(8,128)(2,1)S(1)}, bf16[2,64,1536]{2,1,0:T(8,128)(2,1)}, u32[]{:S(2)}, u32[]{:S(2)}) collective-permute-start(bf16[2,64,1536]{2,1,0:T(8,128)(2,1)S(1)} %copy-done.49), channel_id=1, source_target_pairs={{0,4},{2,6},{4,0},{6,2},{1,5},{3,7},{5,1},{7,3},{8,12},{10,14},{12... | collective-permute-start | bytes 1179656 | tf_op jit(solution)/shard_map/ppermute | solution.py:393
  191.2 25.4 %collective-permute-start.37 = (bf16[2,64,1536]{2,1,0:T(8,128)(2,1)S(1)}, bf16[2,64,1536]{2,1,0:T(8,128)(2,1)}, u32[]{:S(2)}, u32[]{:S(2)}) collective-permute-start(bf16[2,64,1536]{2,1,0:T(8,128)(2,1)S(1)} %copy-done.49), channel_id=1, source_target_pairs={{0,6},{2,0},{4,2},{6,4},{1,7},{3,1},{5,3},{7,5},{8,14},{10,8},{12,... | collective-permute-start | bytes 1179656 | tf_op jit(solution)/shard_map/ppermute | solution.py:393
  192.8 23.8 %collective-permute-start.33 = (bf16[192,1152]{1,0:T(8,128)(2,1)S(1)}, bf16[192,1152]{1,0:T(8,128)(2,1)}, u32[]{:S(2)}, u32[]{:S(2)}) collective-permute-start(bf16[192,1152]{1,0:T(8,128)(2,1)S(1)} %get-tuple-element.162), channel_id=1, source_target_pairs={{0,8},{8,0},{16,24},{24,16},{1,9},{9,1},{17,25},{25,17},{2,10},{10... | collective-permute-start | bytes 1327112 | tf_op jit(solution)/shard_map/ppermute | solution.py:397
  193.6 23.0 %collective-permute-start.34 = (bf16[192,1152]{1,0:T(8,128)(2,1)}, bf16[192,1152]{1,0:T(8,128)(2,1)}, u32[]{:S(2)}, u32[]{:S(2)}) collective-permute-start(bf16[192,1152]{1,0:T(8,128)(2,1)} %get-tuple-element.163), channel_id=1, source_target_pairs={{0,16},{8,24},{16,0},{24,8},{1,17},{9,25},{17,1},{25,9},{2,18},{10... | collective-permute-start | bytes 1327112 | tf_op jit(solution)/shard_map/ppermute | solution.py:401
  221.5 22.1 %collective-permute-start.39 = (bf16[2,192,1152]{2,1,0:T(8,128)(2,1)S(1)}, bf16[2,192,1152]{2,1,0:T(8,128)(2,1)S(1)}, u32[]{:S(2)}, u32[]{:S(2)}) collective-permute-start(bf16[2,192,1152]{2,1,0:T(8,128)(2,1)S(1)} %pad_maximum_fusion.13), channel_id=1, source_target_pairs={{0,16},{8,24},{16,0},{24,8},{1,17},{9,25},{17,1},{25,9},{2,18},{10... | collective-permute-start | bytes 2654216 | tf_op jit(solution)/shard_map/ppermute | solution.py:401
  268.6 31.1 %collective-permute-start.46 = (bf16[2,192,1152]{2,1,0:T(8,128)(2,1)S(1)}, bf16[2,192,1152]{2,1,0:T(8,128)(2,1)S(1)}, u32[]{:S(2)}, u32[]{:S(2)}) collective-permute-start(bf16[2,192,1152]{2,1,0:T(8,128)(2,1)S(1)} %get-tuple-element.273), channel_id=1, source_target_pairs={{0,8},{8,0},{16,24},{24,16},{1,9},{9,1},{17,25},{25,17},{2,10},{10... | collective-permute-start | bytes 2654216 | tf_op jit(solution)/shard_map/ppermute | solution.py:397
  270.0 29.7 %collective-permute-start.47 = (bf16[2,192,1152]{2,1,0:T(8,128)(2,1)S(1)}, bf16[2,192,1152]{2,1,0:T(8,128)(2,1)S(1)}, u32[]{:S(2)}, u32[]{:S(2)}) collective-permute-start(bf16[2,192,1152]{2,1,0:T(8,128)(2,1)S(1)} %get-tuple-element.271), channel_id=1, source_target_pairs={{0,16},{8,24},{16,0},{24,8},{1,17},{9,25},{17,1},{25,9},{2,18},{10... | collective-permute-start | bytes 2654216 | tf_op jit(solution)/shard_map/ppermute | solution.py:401
  274.8 29.1 %collective-permute-start.43 = (bf16[128,1536]{1,0:T(8,128)(2,1)}, bf16[128,1536]{1,0:T(8,128)(2,1)}, u32[]{:S(2)}, u32[]{:S(2)}) collective-permute-start(bf16[128,1536]{1,0:T(8,128)(2,1)} %get-tuple-element.299), channel_id=1, source_target_pairs={{0,6},{2,0},{4,2},{6,4},{1,7},{3,1},{5,3},{7,5},{8,14},{10,8},{12,... | collective-permute-start | bytes 1179656 | tf_op jit(solution)/shard_map/ppermute | solution.py:393
  283.9 36.1 %collective-permute-start.44 = (bf16[128,1536]{1,0:T(8,128)(2,1)}, bf16[128,1536]{1,0:T(8,128)(2,1)}, u32[]{:S(2)}, u32[]{:S(2)}) collective-permute-start(bf16[128,1536]{1,0:T(8,128)(2,1)} %get-tuple-element.298), channel_id=1, source_target_pairs={{0,4},{2,6},{4,0},{6,2},{1,5},{3,7},{5,1},{7,3},{8,12},{10,14},{12... | collective-permute-start | bytes 1179656 | tf_op jit(solution)/shard_map/ppermute | solution.py:393
  285.2 35.6 %collective-permute-start.45 = (bf16[128,1536]{1,0:T(8,128)(2,1)}, bf16[128,1536]{1,0:T(8,128)(2,1)}, u32[]{:S(2)}, u32[]{:S(2)}) collective-permute-start(bf16[128,1536]{1,0:T(8,128)(2,1)} %get-tuple-element.297), channel_id=1, source_target_pairs={{0,2},{2,4},{4,6},{6,0},{1,3},{3,5},{5,7},{7,1},{8,10},{10,12},{12... | collective-permute-start | bytes 1179656 | tf_op jit(solution)/shard_map/ppermute | solution.py:393
  299.7 22.6 %collective-permute-start.42 = (bf16[512,1536]{1,0:T(8,128)(2,1)}, bf16[512,1536]{1,0:T(8,128)(2,1)}, u32[]{:S(2)}, u32[]{:S(2)}) collective-permute-start(bf16[512,1536]{1,0:T(8,128)(2,1)} %slice.254), channel_id=1, source_target_pairs={{0,1},{1,0},{2,3},{3,2},{4,5},{5,4},{6,7},{7,6},{8,9},{9,8},{10,11... | collective-permute-start | bytes 4718600 | tf_op jit(solution)/shard_map/ppermute | solution.py:388
  300.9 24.4 %collective-permute-start.49 = (bf16[192,1152]{1,0:T(8,128)(2,1)}, bf16[192,1152]{1,0:T(8,128)(2,1)}, u32[]{:S(2)}, u32[]{:S(2)}) collective-permute-start(bf16[192,1152]{1,0:T(8,128)(2,1)} %get-tuple-element.324), channel_id=1, source_target_pairs={{0,8},{8,0},{16,24},{24,16},{1,9},{9,1},{17,25},{25,17},{2,10},{10... | collective-permute-start | bytes 1327112 | tf_op jit(solution)/shard_map/ppermute | solution.py:397
  320.0 39.9 %collective-permute-start.60 = (bf16[2,192,2304]{2,1,0:T(8,128)(2,1)S(1)}, bf16[2,192,2304]{2,1,0:T(8,128)(2,1)S(1)}, u32[]{:S(2)}, u32[]{:S(2)}) collective-permute-start(bf16[2,192,2304]{2,1,0:T(8,128)(2,1)S(1)} %get-tuple-element.252), channel_id=1, source_target_pairs={{0,8},{8,0},{16,24},{24,16},{1,9},{9,1},{17,25},{25,17},{2,10},{10... | collective-permute-start | bytes 5308424 | tf_op jit(solution)/shard_map/ppermute | solution.py:397
  320.8 39.6 %collective-permute-start.61 = (bf16[2,192,2304]{2,1,0:T(8,128)(2,1)S(1)}, bf16[2,192,2304]{2,1,0:T(8,128)(2,1)S(1)}, u32[]{:S(2)}, u32[]{:S(2)}) collective-permute-start(bf16[2,192,2304]{2,1,0:T(8,128)(2,1)S(1)} %get-tuple-element.250), channel_id=1, source_target_pairs={{0,16},{8,24},{16,0},{24,8},{1,17},{9,25},{17,1},{25,9},{2,18},{10... | collective-permute-start | bytes 5308424 | tf_op jit(solution)/shard_map/ppermute | solution.py:401
  375.5 37.0 %collective-permute-start.58 = (bf16[128,1536]{1,0:T(8,128)(2,1)}, bf16[128,1536]{1,0:T(8,128)(2,1)}, u32[]{:S(2)}, u32[]{:S(2)}) collective-permute-start(bf16[128,1536]{1,0:T(8,128)(2,1)} %get-tuple-element.206), channel_id=1, source_target_pairs={{0,4},{2,6},{4,0},{6,2},{1,5},{3,7},{5,1},{7,3},{8,12},{10,14},{12... | collective-permute-start | bytes 1179656 | tf_op jit(solution)/shard_map/ppermute | solution.py:393
  377.8 34.7 %collective-permute-start.59 = (bf16[128,1536]{1,0:T(8,128)(2,1)}, bf16[128,1536]{1,0:T(8,128)(2,1)S(1)}, u32[]{:S(2)}, u32[]{:S(2)}) collective-permute-start(bf16[128,1536]{1,0:T(8,128)(2,1)} %get-tuple-element.207), channel_id=1, source_target_pairs={{0,2},{2,4},{4,6},{6,0},{1,3},{3,5},{5,7},{7,1},{8,10},{10,12},{12... | collective-permute-start | bytes 1179656 | tf_op jit(solution)/shard_map/ppermute | solution.py:393
  388.9 29.2 %collective-permute-start.65 = (bf16[2,192,1792]{2,1,0:T(8,128)(2,1)S(1)}, bf16[2,192,1792]{2,1,0:T(8,128)(2,1)S(1)}, u32[]{:S(2)}, u32[]{:S(2)}) collective-permute-start(bf16[2,192,1792]{2,1,0:T(8,128)(2,1)S(1)} %get-tuple-element.266), channel_id=1, source_target_pairs={{0,8},{8,0},{16,24},{24,16},{1,9},{9,1},{17,25},{25,17},{2,10},{10... | collective-permute-start | bytes 4128776 | tf_op jit(solution)/shard_map/ppermute | solution.py:397
  390.1 29.0 %collective-permute-start.66 = (bf16[2,192,1792]{2,1,0:T(8,128)(2,1)S(1)}, bf16[2,192,1792]{2,1,0:T(8,128)(2,1)S(1)}, u32[]{:S(2)}, u32[]{:S(2)}) collective-permute-start(bf16[2,192,1792]{2,1,0:T(8,128)(2,1)S(1)} %get-tuple-element.264), channel_id=1, source_target_pairs={{0,16},{8,24},{16,0},{24,8},{1,17},{9,25},{17,1},{25,9},{2,18},{10... | collective-permute-start | bytes 4128776 | tf_op jit(solution)/shard_map/ppermute | solution.py:401
  420.9 28.7 %collective-permute-start.73 = (bf16[96,2304]{1,0:T(8,128)(2,1)S(1)}, bf16[96,2304]{1,0:T(8,128)(2,1)S(1)}, u32[]{:S(2)}, u32[]{:S(2)}) collective-permute-start(bf16[96,2304]{1,0:T(8,128)(2,1)S(1)} %get-tuple-element.269), channel_id=1, source_target_pairs={{0,4},{2,6},{4,0},{6,2},{1,5},{3,7},{5,1},{7,3},{8,12},{10,14},{12... | collective-permute-start | bytes 1327112 | tf_op jit(solution)/shard_map/ppermute | solution.py:393
  422.7 26.9 %collective-permute-start.74 = (bf16[96,2304]{1,0:T(8,128)(2,1)S(1)}, bf16[96,2304]{1,0:T(8,128)(2,1)S(1)}, u32[]{:S(2)}, u32[]{:S(2)}) collective-permute-start(bf16[96,2304]{1,0:T(8,128)(2,1)S(1)} %get-tuple-element.268), channel_id=1, source_target_pairs={{0,6},{2,0},{4,2},{6,4},{1,7},{3,1},{5,3},{7,5},{8,14},{10,8},{12,... | collective-permute-start | bytes 1327112 | tf_op jit(solution)/shard_map/ppermute | solution.py:393
  424.0 49.7 %collective-permute-start.68 = (bf16[192,1792]{1,0:T(8,128)(2,1)S(1)}, bf16[192,1792]{1,0:T(8,128)(2,1)S(1)}, u32[]{:S(2)}, u32[]{:S(2)}) collective-permute-start(bf16[192,1792]{1,0:T(8,128)(2,1)S(1)} %get-tuple-element.308), channel_id=1, source_target_pairs={{0,8},{8,0},{16,24},{24,16},{1,9},{9,1},{17,25},{25,17},{2,10},{10... | collective-permute-start | bytes 2064392 | tf_op jit(solution)/shard_map/ppermute | solution.py:397
  425.1 48.5 %collective-permute-start.67 = (bf16[192,1792]{1,0:T(8,128)(2,1)S(1)}, bf16[192,1792]{1,0:T(8,128)(2,1)S(1)}, u32[]{:S(2)}, u32[]{:S(2)}) collective-permute-start(bf16[192,1792]{1,0:T(8,128)(2,1)S(1)} %get-tuple-element.310), channel_id=1, source_target_pairs={{0,16},{8,24},{16,0},{24,8},{1,17},{9,25},{17,1},{25,9},{2,18},{10... | collective-permute-start | bytes 2064392 | tf_op jit(solution)/shard_map/ppermute | solution.py:401
  (141 other events, 1287.4 us)
